TPU v7x, 32 devices: a whole 2x2x4 slice. The times are simulated.
32 devices in a mesh: sec: 4 (over x, core), tile: 8 (over z, y).
Axes of the slice: x: 2, y: 2, z: 4, core: 2. Of those that a mesh axis runs over, the one named last changes fastest.
Arguments:
- atmos: float32 [64, 256, 256], P('sec', 'tile'), may hold values from -6 to 6
- cloudy: int32 [64, 256], P('sec', 'tile'), may hold values from 0 to 1, as said below
- weight_in: bfloat16 [256, 1024], replicated, may hold values from -0.375 to 0.375
- weight_out: bfloat16 [1024, 256], replicated, may hold values from -0.1875 to 0.1875
- cloud_in: bfloat16 [256, 1024], replicated, may hold values from -0.375 to 0.375
- cloud_out: bfloat16 [1024, 256], replicated, may hold values from -0.1875 to 0.1875
- ocean: float32 [32, 128, 128], P('sec', 'tile'), may hold values from -6 to 6
- tile_map: int32 [8], replicated, may hold values from 0 to 7, each once
Outputs:
- atmos_out: float32 [64, 256, 256], P('sec', 'tile')
- ocean_out: float32 [32, 128, 128], P('sec', 'tile')
- sst_back: float32 [64, 256], P('sec', 'tile')
Inputs may be any that keep to these rules, and one draw needn't show every extreme that they name: Read each device's 16 x 32 block of columns row by row and cut it into 8 runs of 64 columns. In every row of devices along tile, 1 device, drawn, have all 64 columns of every run cloudy; every other device has exactly 8 cloudy columns in every run, at drawn places.
All inputs are finite; a program needn't handle non-finite values.
Results may differ from a plain program's by a relative error of at most 0.0026.
Values may be sent and summed in bfloat16 or wider, within the bound.
No kernel may reach another device: no remote copies, remote signals or barrier semaphores. Data moves between devices by JAX's collectives and lax.ppermute only.
A program may use at most 64 MiB of HBM per device.

v0:
```python
import jax
import jax.numpy as jnp
from jax import lax
from jax.sharding import PartitionSpec as P

ASTEPS = 2
OSTEPS = 4


kappa_air = 0.2
kappa_sea = 0.2


def padded_2(block, sides, width):
    for axis, dim in sides:
        count = lax.axis_size(axis)
        forward = [(i, i + 1) for i in range(count - 1)]
        backward = [(target, source) for source, target in forward]
        low = lax.ppermute(
            lax.slice_in_dim(block, block.shape[dim] - width, None, axis=dim), axis, forward
        )
        high = lax.ppermute(lax.slice_in_dim(block, 0, width, axis=dim), axis, backward)
        block = jnp.concatenate([low, block, high], axis=dim)
    return block


def relax(padded, rate):
    inner = padded[1:-1, 1:-1]
    beside = padded[2:, 1:-1] + padded[:-2, 1:-1] + padded[1:-1, 2:] + padded[1:-1, :-2]
    return inner + rate * (beside - 4.0 * inner)


def spread(values):
    return jnp.repeat(jnp.repeat(values, 2, axis=0), 2, axis=1)


def coarsen(values):
    height, width = values.shape
    return values.reshape(height // 2, 2, width // 2, 2).mean(axis=(1, 3))


def local(atmos, cloudy, weight_in, weight_out, cloud_in, cloud_out, ocean, tile_map):
    rows, cols, feat = atmos.shape
    levels = feat // 2
    sea_levels = ocean.shape[2] // 2
    half_rows = rows // 2
    half_cols = cols // 2
    columns = rows * cols
    tiles = lax.axis_size("tile")
    me_tile = lax.axis_index("tile")
    table = jnp.arange(tiles, dtype=jnp.int32)

    def lookup(owners):
        return jnp.sum(jnp.where(owners[:, None] == table[None, :], tile_map[None, :], 0), axis=1)

    source_tile = jnp.sum(jnp.where(table == me_tile, tile_map, 0))

    def take_mine(piece):
        count = piece.shape[1] // half_cols
        owners = jnp.arange(count, dtype=jnp.int32)
        wanted = (lookup(owners) == me_tile)[None, :, None]
        blocks = piece.reshape(piece.shape[0], count, half_cols)
        return jnp.sum(jnp.where(wanted, blocks, 0.0), axis=1)

    landing = spread(take_mine(lax.all_gather(ocean[:, :, 0], "tile", axis=1, tiled=True)))
    field = atmos
    for step in range(ASTEPS):
        padded = padded_2(field, (("sec", 0), ("tile", 1)), 1)
        field = relax(padded, kappa_air)
    inputs = field.reshape(columns, feat).astype(jnp.bfloat16)
    flags = cloudy.reshape(columns)
    hidden = jax.nn.silu(jnp.dot(inputs, weight_in, preferred_element_type=jnp.float32)).astype(
        jnp.bfloat16
    )
    condensed = jax.nn.silu(jnp.dot(inputs, cloud_in, preferred_element_type=jnp.float32)).astype(
        jnp.bfloat16
    )
    total = jnp.dot(hidden, weight_out, preferred_element_type=jnp.float32) + flags.astype(
        jnp.float32
    )[:, None] * jnp.dot(condensed, cloud_out, preferred_element_type=jnp.float32)
    tendency = total.astype(jnp.bfloat16)
    field = field + tendency.astype(jnp.float32).reshape(rows, cols, feat)
    heat = 0.8 * (landing - field[:, :, 0])
    moisture = 0.8 * (0.5 * landing - field[:, :, levels])
    field = field.at[:, :, 0].add(0.5 * heat).at[:, :, levels].add(0.5 * moisture)
    pieces = (
        lax.all_gather(coarsen(heat), "tile", axis=1, tiled=True),
        lax.all_gather(coarsen(moisture), "tile", axis=1, tiled=True),
    )
    count = pieces[0].shape[1] // half_cols
    owners = jnp.arange(count, dtype=jnp.int32)
    wanted = (owners == source_tile)[None, :, None]
    heat_sea, moist_sea = tuple(
        (
            jnp.sum(jnp.where(wanted, member.reshape(half_rows, count, half_cols), 0.0), axis=1)
            for member in pieces
        )
    )
    sea = ocean.at[:, :, 0].add(0.5 * heat_sea).at[:, :, sea_levels].add(0.5 * moist_sea)
    for step in range(OSTEPS):
        padded_sea = padded_2(sea, (("sec", 0), ("tile", 1)), 1)
        sea = relax(padded_sea, kappa_sea)
    returned = spread(take_mine(lax.all_gather(sea[:, :, 0], "tile", axis=1, tiled=True)))
    return (field, sea, returned)


def solution(mesh):
    placed = (
        P("sec", "tile", None),
        P("sec", "tile"),
        P(),
        P(),
        P(),
        P(),
        P("sec", "tile", None),
        P(),
    )
    return jax.shard_map(
        local,
        mesh=mesh,
        in_specs=placed,
        out_specs=(P("sec", "tile", None), P("sec", "tile", None), P("sec", "tile")),
        check_vma=False,
    )
```

profile of v0, /device:TPU:0, one launch (start us, length us, event | category | flops | bytes accessed | tf_op | source)
XLA Modules:
  0.0 262.4 jit_solution(8618443986985856060)
XLA Ops:
  2.4 2.3 collective-permute-start.1
  6.2 31.7 %all-gather = f32[8,128,1]{0,2,1:T(1,128)S(1)} all-gather(f32[8,16,1]{0,2,1:T(1,128)S(1)} %copy.320), channel_id=2, replica_groups=mesh['sec'=4,'tile'=8] {'tile'}, dimensions={1}, use_global_device_ids=true | all-gather | bytes 4608 | tf_op jit(solution)/shard_map/all_gather | solution.py:65
  38.9 1.6 pad_maximum_fusion.10
  41.8 4.5 %collective-permute-start.3 = (f32[18,1,256]{2,1,0:T(1,128)S(1)}, f32[18,1,256]{2,1,0:T(1,128)S(1)}, u32[]{:S(2)}, u32[]{:S(2)}) collective-permute-start(f32[18,1,256]{2,1,0:T(1,128)S(1)} %get-tuple-element.97), channel_id=1, source_target_pairs={{0,1},{1,2},{2,3},{3,4},{4,5},{5,6},{6,7},{8,9},{9,10},{10,11},{11... | collective-permute-start | bytes 55304 | tf_op jit(solution)/shard_map/ppermute | solution.py:19
  47.0 2.5 copy.312
  49.4 2.5 copy.336
  52.0 2.5 copy.337
  54.6 2.5 copy.338
  57.1 2.4 copy.339
  59.6 4.7 %multiply_add_fusion = f32[16,32,256]{1,0,2:T(8,128)S(1)} fusion(f32[16,32,256]{1,0,2:T(8,128)} %copy.312, f32[16,32,256]{1,0,2:T(8,128)} %copy.339, f32[16,32,256]{1,0,2:T(8,128)} %copy.338, f32[16,32,256]{1,0,2:T(8,128)} %copy.336, f32[16,32,256]{1,0,2:T(8,128)} %copy.337), kind=kLoop, calls=%fused_computation.10 | loop fusion | flops 917504 | bytes 3145728 | tf_op jit(solution)/shard_map/add | solution.py:30
  69.5 4.7 %collective-permute-done.4 = f32[1,32,256]{1,0,2:T(1,128)S(1)} collective-permute-done((f32[1,32,256]{1,0,2:T(1,128)}, f32[1,32,256]{1,0,2:T(1,128)S(1)}, u32[]{:S(2)}, u32[]{:S(2)}) %collective-permute-start.4) | collective-permute-done | bytes 32800 | tf_op jit(solution)/shard_map/ppermute | solution.py:22
  76.2 5.6 %collective-permute-start.7 = (f32[18,1,256]{2,1,0:T(1,128)}, f32[18,1,256]{2,1,0:T(1,128)}, u32[]{:S(2)}, u32[]{:S(2)}) collective-permute-start(f32[18,1,256]{2,1,0:T(1,128)} %get-tuple-element.93), channel_id=1, source_target_pairs={{0,1},{1,2},{2,3},{3,4},{4,5},{5,6},{6,7},{8,9},{9,10},{10,11},{11... | collective-permute-start | bytes 55304 | tf_op jit(solution)/shard_map/ppermute | solution.py:19
  87.1 1.9 pad_maximum_fusion.5
  89.0 3.6 %copy.340 = f32[16,32,256]{1,0,2:T(8,128)} copy(f32[16,32,256]{2,1,0:T(8,128)} %get-tuple-element.90) | data formatting | bytes 1048576
  92.6 2.4 copy.341
  95.0 5.2 %fusion.37 = (bf16[16,32,256]{1,0,2:T(8,128)(2,1)}, f32[16,32,256]{1,0,2:T(8,128)}) fusion(f32[16,32,256]{1,0,2:T(8,128)S(1)} %multiply_add_fusion, f32[16,32,256]{1,0,2:T(8,128)} %copy.341, f32[16,32,256]{1,0,2:T(8,128)} %copy.340, f32[1,32,256]{1,0,2:T(1,128)S(1)} %collective-permute-done.5, f32[1,32,256]{1,0,2:T(1,128)S(1)} %collective-permute-done.4), kind=kLoop, calls=%fused_computation.124 | loop fusion | flops 1310720 | bytes 2424832 | tf_op jit(solution)/shard_map/convert_element_type | solution.py:70
  100.2 2.0 copy.318
  104.2 2.1 copy.319
  106.4 1.9 add.124
  109.1 30.4 %all-gather.3 = f32[8,16,8]{1,2,0:T(8,128)S(1)} all-gather(f32[1,16,8]{1,2,0:T(8,128)S(1)} %multiply_bitcast_fusion.1), channel_id=1, replica_groups=mesh['sec'=4,'tile'=8] {'tile'}, dimensions={0}, use_global_device_ids=true | all-gather | bytes 4608 | tf_op jit(solution)/shard_map/all_gather | solution.py:88
  139.9 30.4 %all-gather.2 = f32[8,16,8]{1,2,0:T(8,128)S(1)} all-gather(f32[1,16,8]{1,2,0:T(8,128)S(1)} %multiply_bitcast_fusion.3), channel_id=1, replica_groups=mesh['sec'=4,'tile'=8] {'tile'}, dimensions={0}, use_global_device_ids=true | all-gather | bytes 4608 | tf_op jit(solution)/shard_map/all_gather | solution.py:87
  173.0 3.0 %collective-permute-start.9 = (f32[1,16,128]{2,1,0:T(8,128)S(1)}, f32[1,16,128]{2,1,0:T(8,128)S(1)}, u32[]{:S(2)}, u32[]{:S(2)}) collective-permute-start(f32[1,16,128]{2,1,0:T(8,128)S(1)} %get-tuple-element.117), channel_id=1, source_target_pairs={{0,8},{8,16},{16,24},{1,9},{9,17},{17,25},{2,10},{10,18},{18,26},{... | collective-permute-start | bytes 24584 | tf_op jit(solution)/shard_map/ppermute | solution.py:19
  178.2 4.5 %collective-permute-start.11 = (f32[10,1,128]{2,1,0:T(1,128)S(1)}, f32[10,1,128]{2,1,0:T(1,128)S(1)}, u32[]{:S(2)}, u32[]{:S(2)}) collective-permute-start(f32[10,1,128]{2,1,0:T(1,128)S(1)} %get-tuple-element.110), channel_id=1, source_target_pairs={{0,1},{1,2},{2,3},{3,4},{4,5},{5,6},{6,7},{8,9},{9,10},{10,11},{11... | collective-permute-start | bytes 15368 | tf_op jit(solution)/shard_map/ppermute | solution.py:19
  182.8 1.3 collective-permute-done.11
  185.4 4.4 %collective-permute-start.13 = (f32[1,16,128]{2,1,0:T(8,128)S(1)}, f32[1,16,128]{2,1,0:T(8,128)S(1)}, u32[]{:S(2)}, u32[]{:S(2)}) collective-permute-start(f32[1,16,128]{2,1,0:T(8,128)S(1)} %get-tuple-element.115), channel_id=1, source_target_pairs={{0,8},{8,16},{16,24},{1,9},{9,17},{17,25},{2,10},{10,18},{18,26},{... | collective-permute-start | bytes 24584 | tf_op jit(solution)/shard_map/ppermute | solution.py:19
  191.9 4.5 %collective-permute-start.15 = (f32[10,1,128]{2,1,0:T(1,128)S(1)}, f32[10,1,128]{2,1,0:T(1,128)S(1)}, u32[]{:S(2)}, u32[]{:S(2)}) collective-permute-start(f32[10,1,128]{2,1,0:T(1,128)S(1)} %get-tuple-element.108), channel_id=1, source_target_pairs={{0,1},{1,2},{2,3},{3,4},{4,5},{5,6},{6,7},{8,9},{9,10},{10,11},{11... | collective-permute-start | bytes 15368 | tf_op jit(solution)/shard_map/ppermute | solution.py:19
  199.2 5.3 %collective-permute-start.17 = (f32[1,16,128]{2,1,0:T(8,128)S(1)}, f32[1,16,128]{2,1,0:T(8,128)S(1)}, u32[]{:S(2)}, u32[]{:S(2)}) collective-permute-start(f32[1,16,128]{2,1,0:T(8,128)S(1)} %get-tuple-element.113), channel_id=1, source_target_pairs={{0,8},{8,16},{16,24},{1,9},{9,17},{17,25},{2,10},{10,18},{18,26},{... | collective-permute-start | bytes 24584 | tf_op jit(solution)/shard_map/ppermute | solution.py:19
  206.6 5.2 %collective-permute-start.19 = (f32[10,1,128]{2,1,0:T(1,128)S(1)}, f32[10,1,128]{2,1,0:T(1,128)S(1)}, u32[]{:S(2)}, u32[]{:S(2)}) collective-permute-start(f32[10,1,128]{2,1,0:T(1,128)S(1)} %get-tuple-element.106), channel_id=1, source_target_pairs={{0,1},{1,2},{2,3},{3,4},{4,5},{5,6},{6,7},{8,9},{9,10},{10,11},{11... | collective-permute-start | bytes 15368 | tf_op jit(solution)/shard_map/ppermute | solution.py:19
  214.5 5.1 %collective-permute-start.21 = (f32[1,16,128]{2,1,0:T(8,128)S(1)}, f32[1,16,128]{2,1,0:T(8,128)S(1)}, u32[]{:S(2)}, u32[]{:S(2)}) collective-permute-start(f32[1,16,128]{2,1,0:T(8,128)S(1)} %get-tuple-element.111), channel_id=1, source_target_pairs={{0,8},{8,16},{16,24},{1,9},{9,17},{17,25},{2,10},{10,18},{18,26},{... | collective-permute-start | bytes 24584 | tf_op jit(solution)/shard_map/ppermute | solution.py:19
  221.7 5.7 %collective-permute-start.23 = (f32[10,1,128]{2,1,0:T(1,128)S(1)}, f32[10,1,128]{2,1,0:T(1,128)S(1)}, u32[]{:S(2)}, u32[]{:S(2)}) collective-permute-start(f32[10,1,128]{2,1,0:T(1,128)S(1)} %get-tuple-element.104), channel_id=1, source_target_pairs={{0,1},{1,2},{2,3},{3,4},{4,5},{5,6},{6,7},{8,9},{9,10},{10,11},{11... | collective-permute-start | bytes 15368 | tf_op jit(solution)/shard_map/ppermute | solution.py:19
  227.4 1.8 copy.334
  229.4 32.0 %all-gather.1 = f32[8,128,1]{0,2,1:T(1,128)S(1)} all-gather(f32[8,16,1]{0,2,1:T(1,128)S(1)} %copy.331), channel_id=3, replica_groups=mesh['sec'=4,'tile'=8] {'tile'}, dimensions={1}, use_global_device_ids=true | all-gather | bytes 4608 | tf_op jit(solution)/shard_map/all_gather | solution.py:103
  (134 shorter events, 40.8 us)
Async XLA Ops:
  0.6 101.5 %copy-start = (bf16[1024,256]{1,0:T(8,128)(2,1)S(1)}, bf16[1024,256]{1,0:T(8,128)(2,1)}, u32[]{:S(2)}) copy-start(bf16[1024,256]{1,0:T(8,128)(2,1)} %param.21) | copy-start | bytes 1572868
  0.6 46.3 %copy-start.2 = (f32[16,32,256]{2,1,0:T(8,128)S(1)}, f32[16,32,256]{2,1,0:T(8,128)}, u32[]{:S(2)}) copy-start(f32[16,32,256]{2,1,0:T(8,128)} %param.16) | copy-start | bytes 1572868
  2.4 36.5 %collective-permute-start.1 = (f32[1,32,256]{2,1,0:T(8,128)S(1)}, f32[1,32,256]{2,1,0:T(8,128)S(1)}, u32[]{:S(2)}, u32[]{:S(2)}) collective-permute-start(f32[1,32,256]{2,1,0:T(8,128)S(1)} %get-tuple-element.102), channel_id=1, source_target_pairs={{0,8},{8,16},{16,24},{1,9},{9,17},{17,25},{2,10},{10,18},{18,26},{... | collective-permute-start | bytes 98312 | tf_op jit(solution)/shard_map/ppermute | solution.py:19
  4.7 34.1 %collective-permute-start = (f32[1,32,256]{2,1,0:T(8,128)S(1)}, f32[1,32,256]{2,1,0:T(8,128)S(1)}, u32[]{:S(2)}, u32[]{:S(2)}) collective-permute-start(f32[1,32,256]{2,1,0:T(8,128)S(1)} %get-tuple-element.101), channel_id=1, source_target_pairs={{8,0},{16,8},{24,16},{9,1},{17,9},{25,17},{10,2},{18,10},{26,18},{... | collective-permute-start | bytes 98312 | tf_op jit(solution)/shard_map/ppermute | solution.py:22
  40.5 14.0 %collective-permute-start.2 = (f32[18,1,256]{2,1,0:T(1,128)S(1)}, f32[18,1,256]{2,1,0:T(1,128)S(1)}, u32[]{:S(2)}, u32[]{:S(2)}) collective-permute-start(f32[18,1,256]{2,1,0:T(1,128)S(1)} %get-tuple-element.96), channel_id=1, source_target_pairs={{1,0},{2,1},{3,2},{4,3},{5,4},{6,5},{7,6},{9,8},{10,9},{11,10},{12... | collective-permute-start | bytes 55304 | tf_op jit(solution)/shard_map/ppermute | solution.py:22
  41.8 12.7 %collective-permute-start.3 = (f32[18,1,256]{2,1,0:T(1,128)S(1)}, f32[18,1,256]{2,1,0:T(1,128)S(1)}, u32[]{:S(2)}, u32[]{:S(2)}) collective-permute-start(f32[18,1,256]{2,1,0:T(1,128)S(1)} %get-tuple-element.97), channel_id=1, source_target_pairs={{0,1},{1,2},{2,3},{3,4},{4,5},{5,6},{6,7},{8,9},{9,10},{10,11},{11... | collective-permute-start | bytes 55304 | tf_op jit(solution)/shard_map/ppermute | solution.py:19
  59.6 8.2 %copy-start.13 = (s32[8]{0:T(128)S(1)}, s32[8]{0:T(128)}, u32[]{:S(2)}) copy-start(s32[8]{0:T(128)} %param.23) | copy-start | bytes 100
  65.2 4.3 %collective-permute-start.5 = (f32[1,32,256]{1,0,2:T(1,128)}, f32[1,32,256]{1,0,2:T(1,128)S(1)}, u32[]{:S(2)}, u32[]{:S(2)}) collective-permute-start(f32[1,32,256]{1,0,2:T(1,128)} %get-tuple-element.88), channel_id=1, source_target_pairs={{0,8},{8,16},{16,24},{1,9},{9,17},{17,25},{2,10},{10,18},{18,26},{... | collective-permute-start | bytes 98312 | tf_op jit(solution)/shard_map/ppermute | solution.py:19
  66.5 7.7 %collective-permute-start.4 = (f32[1,32,256]{1,0,2:T(1,128)}, f32[1,32,256]{1,0,2:T(1,128)S(1)}, u32[]{:S(2)}, u32[]{:S(2)}) collective-permute-start(f32[1,32,256]{1,0,2:T(1,128)} %get-tuple-element.89), channel_id=1, source_target_pairs={{8,0},{16,8},{24,16},{9,1},{17,9},{25,17},{10,2},{18,10},{26,18},{... | collective-permute-start | bytes 98312 | tf_op jit(solution)/shard_map/ppermute | solution.py:22
  74.9 12.2 %collective-permute-start.6 = (f32[18,1,256]{2,1,0:T(1,128)}, f32[18,1,256]{2,1,0:T(1,128)}, u32[]{:S(2)}, u32[]{:S(2)}) collective-permute-start(f32[18,1,256]{2,1,0:T(1,128)} %get-tuple-element.92), channel_id=1, source_target_pairs={{1,0},{2,1},{3,2},{4,3},{5,4},{6,5},{7,6},{9,8},{10,9},{11,10},{12... | collective-permute-start | bytes 55304 | tf_op jit(solution)/shard_map/ppermute | solution.py:22
  76.2 10.9 %collective-permute-start.7 = (f32[18,1,256]{2,1,0:T(1,128)}, f32[18,1,256]{2,1,0:T(1,128)}, u32[]{:S(2)}, u32[]{:S(2)}) collective-permute-start(f32[18,1,256]{2,1,0:T(1,128)} %get-tuple-element.93), channel_id=1, source_target_pairs={{0,1},{1,2},{2,3},{3,4},{4,5},{5,6},{6,7},{8,9},{9,10},{10,11},{11... | collective-permute-start | bytes 55304 | tf_op jit(solution)/shard_map/ppermute | solution.py:19
  95.0 7.2 %copy-start.8 = (f32[512]{0:T(512)S(1)}, f32[512]{0:T(512)}, u32[]{:S(2)}) copy-start(f32[512]{0:T(512)} %convert_element_type.30) | copy-start | bytes 6148
  95.0 7.2 %copy-start.10 = (bf16[256,1024]{1,0:T(8,128)(2,1)S(1)}, bf16[256,1024]{1,0:T(8,128)(2,1)}, u32[]{:S(2)}) copy-start(bf16[256,1024]{1,0:T(8,128)(2,1)} %param.20) | copy-start | bytes 1572868
  108.2 62.2 %copy-start.9 = (pred[8]{0:T(512)(128)(4,1)S(1)}, pred[8]{0:T(512)(128)(4,1)}, u32[]{:S(2)}) copy-start(pred[8]{0:T(512)(128)(4,1)} %iota_compare_fusion.1) | copy-start | bytes 28
  171.0 90.5 %copy-start.7 = (pred[8]{0:T(512)(128)(4,1)S(1)}, pred[8]{0:T(512)(128)(4,1)}, u32[]{:S(2)}) copy-start(pred[8]{0:T(512)(128)(4,1)} %copy-done.6) | copy-start | bytes 28
  171.7 4.3 %collective-permute-start.8 = (f32[1,16,128]{2,1,0:T(8,128)S(1)}, f32[1,16,128]{2,1,0:T(8,128)S(1)}, u32[]{:S(2)}, u32[]{:S(2)}) collective-permute-start(f32[1,16,128]{2,1,0:T(8,128)S(1)} %get-tuple-element.118), channel_id=1, source_target_pairs={{8,0},{16,8},{24,16},{9,1},{17,9},{25,17},{10,2},{18,10},{26,18},{... | collective-permute-start | bytes 24584 | tf_op jit(solution)/shard_map/ppermute | solution.py:22
  173.0 3.8 %collective-permute-start.9 = (f32[1,16,128]{2,1,0:T(8,128)S(1)}, f32[1,16,128]{2,1,0:T(8,128)S(1)}, u32[]{:S(2)}, u32[]{:S(2)}) collective-permute-start(f32[1,16,128]{2,1,0:T(8,128)S(1)} %get-tuple-element.117), channel_id=1, source_target_pairs={{0,8},{8,16},{16,24},{1,9},{9,17},{17,25},{2,10},{10,18},{18,26},{... | collective-permute-start | bytes 24584 | tf_op jit(solution)/shard_map/ppermute | solution.py:19
  176.9 5.9 %collective-permute-start.10 = (f32[10,1,128]{2,1,0:T(1,128)S(1)}, f32[10,1,128]{2,1,0:T(1,128)S(1)}, u32[]{:S(2)}, u32[]{:S(2)}) collective-permute-start(f32[10,1,128]{2,1,0:T(1,128)S(1)} %get-tuple-element.109), channel_id=1, source_target_pairs={{1,0},{2,1},{3,2},{4,3},{5,4},{6,5},{7,6},{9,8},{10,9},{11,10},{12... | collective-permute-start | bytes 15368 | tf_op jit(solution)/shard_map/ppermute | solution.py:22
  178.2 5.9 %collective-permute-start.11 = (f32[10,1,128]{2,1,0:T(1,128)S(1)}, f32[10,1,128]{2,1,0:T(1,128)S(1)}, u32[]{:S(2)}, u32[]{:S(2)}) collective-permute-start(f32[10,1,128]{2,1,0:T(1,128)S(1)} %get-tuple-element.110), channel_id=1, source_target_pairs={{0,1},{1,2},{2,3},{3,4},{4,5},{5,6},{6,7},{8,9},{9,10},{10,11},{11... | collective-permute-start | bytes 15368 | tf_op jit(solution)/shard_map/ppermute | solution.py:19
  184.1 5.7 %collective-permute-start.12 = (f32[1,16,128]{2,1,0:T(8,128)S(1)}, f32[1,16,128]{2,1,0:T(8,128)S(1)}, u32[]{:S(2)}, u32[]{:S(2)}) collective-permute-start(f32[1,16,128]{2,1,0:T(8,128)S(1)} %get-tuple-element.116), channel_id=1, source_target_pairs={{8,0},{16,8},{24,16},{9,1},{17,9},{25,17},{10,2},{18,10},{26,18},{... | collective-permute-start | bytes 24584 | tf_op jit(solution)/shard_map/ppermute | solution.py:22
  185.4 5.2 %collective-permute-start.13 = (f32[1,16,128]{2,1,0:T(8,128)S(1)}, f32[1,16,128]{2,1,0:T(8,128)S(1)}, u32[]{:S(2)}, u32[]{:S(2)}) collective-permute-start(f32[1,16,128]{2,1,0:T(8,128)S(1)} %get-tuple-element.115), channel_id=1, source_target_pairs={{0,8},{8,16},{16,24},{1,9},{9,17},{17,25},{2,10},{10,18},{18,26},{... | collective-permute-start | bytes 24584 | tf_op jit(solution)/shard_map/ppermute | solution.py:19
  190.6 5.9 %collective-permute-start.14 = (f32[10,1,128]{2,1,0:T(1,128)S(1)}, f32[10,1,128]{2,1,0:T(1,128)S(1)}, u32[]{:S(2)}, u32[]{:S(2)}) collective-permute-start(f32[10,1,128]{2,1,0:T(1,128)S(1)} %get-tuple-element.107), channel_id=1, source_target_pairs={{1,0},{2,1},{3,2},{4,3},{5,4},{6,5},{7,6},{9,8},{10,9},{11,10},{12... | collective-permute-start | bytes 15368 | tf_op jit(solution)/shard_map/ppermute | solution.py:22
  191.9 5.9 %collective-permute-start.15 = (f32[10,1,128]{2,1,0:T(1,128)S(1)}, f32[10,1,128]{2,1,0:T(1,128)S(1)}, u32[]{:S(2)}, u32[]{:S(2)}) collective-permute-start(f32[10,1,128]{2,1,0:T(1,128)S(1)} %get-tuple-element.108), channel_id=1, source_target_pairs={{0,1},{1,2},{2,3},{3,4},{4,5},{5,6},{6,7},{8,9},{9,10},{10,11},{11... | collective-permute-start | bytes 15368 | tf_op jit(solution)/shard_map/ppermute | solution.py:19
  197.9 6.6 %collective-permute-start.16 = (f32[1,16,128]{2,1,0:T(8,128)S(1)}, f32[1,16,128]{2,1,0:T(8,128)S(1)}, u32[]{:S(2)}, u32[]{:S(2)}) collective-permute-start(f32[1,16,128]{2,1,0:T(8,128)S(1)} %get-tuple-element.114), channel_id=1, source_target_pairs={{8,0},{16,8},{24,16},{9,1},{17,9},{25,17},{10,2},{18,10},{26,18},{... | collective-permute-start | bytes 24584 | tf_op jit(solution)/shard_map/ppermute | solution.py:22
  199.2 6.1 %collective-permute-start.17 = (f32[1,16,128]{2,1,0:T(8,128)S(1)}, f32[1,16,128]{2,1,0:T(8,128)S(1)}, u32[]{:S(2)}, u32[]{:S(2)}) collective-permute-start(f32[1,16,128]{2,1,0:T(8,128)S(1)} %get-tuple-element.113), channel_id=1, source_target_pairs={{0,8},{8,16},{16,24},{1,9},{9,17},{17,25},{2,10},{10,18},{18,26},{... | collective-permute-start | bytes 24584 | tf_op jit(solution)/shard_map/ppermute | solution.py:19
  205.3 6.5 %collective-permute-start.18 = (f32[10,1,128]{2,1,0:T(1,128)S(1)}, f32[10,1,128]{2,1,0:T(1,128)S(1)}, u32[]{:S(2)}, u32[]{:S(2)}) collective-permute-start(f32[10,1,128]{2,1,0:T(1,128)S(1)} %get-tuple-element.105), channel_id=1, source_target_pairs={{1,0},{2,1},{3,2},{4,3},{5,4},{6,5},{7,6},{9,8},{10,9},{11,10},{12... | collective-permute-start | bytes 15368 | tf_op jit(solution)/shard_map/ppermute | solution.py:22
  206.6 6.5 %collective-permute-start.19 = (f32[10,1,128]{2,1,0:T(1,128)S(1)}, f32[10,1,128]{2,1,0:T(1,128)S(1)}, u32[]{:S(2)}, u32[]{:S(2)}) collective-permute-start(f32[10,1,128]{2,1,0:T(1,128)S(1)} %get-tuple-element.106), channel_id=1, source_target_pairs={{0,1},{1,2},{2,3},{3,4},{4,5},{5,6},{6,7},{8,9},{9,10},{10,11},{11... | collective-permute-start | bytes 15368 | tf_op jit(solution)/shard_map/ppermute | solution.py:19
  213.2 6.4 %collective-permute-start.20 = (f32[1,16,128]{2,1,0:T(8,128)S(1)}, f32[1,16,128]{2,1,0:T(8,128)S(1)}, u32[]{:S(2)}, u32[]{:S(2)}) collective-permute-start(f32[1,16,128]{2,1,0:T(8,128)S(1)} %get-tuple-element.112), channel_id=1, source_target_pairs={{8,0},{16,8},{24,16},{9,1},{17,9},{25,17},{10,2},{18,10},{26,18},{... | collective-permute-start | bytes 24584 | tf_op jit(solution)/shard_map/ppermute | solution.py:22
  214.5 5.9 %collective-permute-start.21 = (f32[1,16,128]{2,1,0:T(8,128)S(1)}, f32[1,16,128]{2,1,0:T(8,128)S(1)}, u32[]{:S(2)}, u32[]{:S(2)}) collective-permute-start(f32[1,16,128]{2,1,0:T(8,128)S(1)} %get-tuple-element.111), channel_id=1, source_target_pairs={{0,8},{8,16},{16,24},{1,9},{9,17},{17,25},{2,10},{10,18},{18,26},{... | collective-permute-start | bytes 24584 | tf_op jit(solution)/shard_map/ppermute | solution.py:19
  220.4 8.8 %collective-permute-start.22 = (f32[10,1,128]{2,1,0:T(1,128)S(1)}, f32[10,1,128]{2,1,0:T(1,128)S(1)}, u32[]{:S(2)}, u32[]{:S(2)}) collective-permute-start(f32[10,1,128]{2,1,0:T(1,128)S(1)} %get-tuple-element.103), channel_id=1, source_target_pairs={{1,0},{2,1},{3,2},{4,3},{5,4},{6,5},{7,6},{9,8},{10,9},{11,10},{12... | collective-permute-start | bytes 15368 | tf_op jit(solution)/shard_map/ppermute | solution.py:22
  221.7 7.5 %collective-permute-start.23 = (f32[10,1,128]{2,1,0:T(1,128)S(1)}, f32[10,1,128]{2,1,0:T(1,128)S(1)}, u32[]{:S(2)}, u32[]{:S(2)}) collective-permute-start(f32[10,1,128]{2,1,0:T(1,128)S(1)} %get-tuple-element.104), channel_id=1, source_target_pairs={{0,1},{1,2},{2,3},{3,4},{4,5},{5,6},{6,7},{8,9},{9,10},{10,11},{11... | collective-permute-start | bytes 15368 | tf_op jit(solution)/shard_map/ppermute | solution.py:19
  229.2 33.2 %copy-start.4 = (f32[8,16,128]{2,1,0:T(8,128)}, f32[8,16,128]{2,1,0:T(8,128)S(1)}, u32[]{:S(2)}) copy-start(f32[8,16,128]{2,1,0:T(8,128)S(1)} %fusion.12) | copy-start | bytes 196612
  (6 other events, 11.7 us)
where the time goes:
time: 266 us; the launch traced here: 262 us
  blocking collectives  125 us (47%)
  starting transfers between devices  67 us (25%)
  local copies, waits for them, and re-layouts  35.3 us (13%)
  other arithmetic  20.8 us (8%)
  waiting for transfers between devices  11.8 us (4%)
    ppermute x12, starting transfers between devices, padded_2(): lax.ppermute(lax.slice_in_dim(block, block.shape[dim] - width, None, axis...  51.5 us
    all_gather x1, blocking collectives, local(): lax.all_gather(sea[:, :, 0], 'tile', axis=1, tiled=True)  32 us
    all_gather x1, blocking collectives, local(): lax.all_gather(ocean[:, :, 0], 'tile', axis=1, tiled=True)  31.7 us
    all_gather x1, blocking collectives, local(): lax.all_gather(coarsen(moisture), 'tile', axis=1, tiled=True)  30.4 us
    all_gather x1, blocking collectives, local(): lax.all_gather(coarsen(heat), 'tile', axis=1, tiled=True)  30.4 us
    unnamed x42, local copies, waits for them, and re-layouts  22.9 us
    ppermute x12, starting transfers between devices, padded_2(): lax.ppermute(lax.slice_in_dim(block, 0, width, axis=dim), axis, backward)  15.5 us
    ppermute x12, waiting for transfers between devices, padded_2(): lax.ppermute(lax.slice_in_dim(block, block.shape[dim] - width, None, axis...  7.14 us
  transfers between devices with their start and end apart: 24, of which 8 were waited for; matrix products, arithmetic and copies ran while one was open for 7% of the time, Pallas kernels for 0%

commit v1 on v0

v1 whole, which is shorter than its diff:
```python
import functools

import jax
import jax.numpy as jnp
from jax import lax
from jax.experimental import pallas as pl
from jax.experimental.pallas import tpu as pltpu
from jax.sharding import PartitionSpec as P

ASTEPS = 2
OSTEPS = 4
LANES = 128

kappa_air = 0.2
kappa_sea = 0.2

f32 = jnp.float32
bf16 = jnp.bfloat16
HIGHEST = lax.Precision.HIGHEST
VMEM = pl.BlockSpec(memory_space=pltpu.VMEM)
SMEM = pl.BlockSpec(memory_space=pltpu.SMEM)
AXES = ("sec", "tile")


def exchanges(secs, tiles):
    def whole(partner):
        return [
            (s * tiles + t, partner(s, t)[0] * tiles + partner(s, t)[1])
            for s in range(secs)
            for t in range(tiles)
        ]

    def odd_sec(s, t):
        if s in (0, secs - 1):
            return secs - 1 - s, t
        return (s + 1 if s % 2 else s - 1), t

    def odd_tile(s, t):
        if t in (0, tiles - 1):
            return s ^ 1, t
        return s, (t + 1 if t % 2 else t - 1)

    return (
        whole(lambda s, t: (s ^ 1, t)),
        whole(odd_sec),
        whole(lambda s, t: (s, t ^ 1)),
        whole(odd_tile),
    )


def pack_sec(atmos, ocean, out_a, out_b):
    rows, cols, feat = atmos.shape
    sea_rows, sea_cols, _ = ocean.shape
    even = lax.axis_index("sec") % 2 == 0
    halves = feat // LANES
    for out, south in ((out_a, even), (out_b, jnp.logical_not(even))):
        first = jnp.where(south, rows - ASTEPS, 0)
        sea_first = jnp.where(south, sea_rows - OSTEPS, 0)
        for r in range(ASTEPS):
            line = atmos[first + r].astype(bf16)
            for h in range(halves):
                at = (r * halves + h) * cols
                out[at : at + cols, :] = line[:, h * LANES : (h + 1) * LANES]
        base = ASTEPS * halves * cols
        for r in range(OSTEPS):
            at = base + r * sea_cols
            out[at : at + sea_cols, :] = ocean[sea_first + r].astype(bf16)


def from_sec(recv_a, recv_b):
    even = lax.axis_index("sec") % 2 == 0
    a, b = recv_a[...].astype(f32), recv_b[...].astype(f32)
    return jnp.where(even, b, a), jnp.where(even, a, b)


def air_pad(rows):
    return -(-(rows + 2) * ASTEPS // 8) * 8


def pack_tile(atmos, ocean, sec_a, sec_b, out_a, out_b, stage):
    rows, cols, feat = atmos.shape
    sea_rows, sea_cols, _ = ocean.shape
    even = lax.axis_index("tile") % 2 == 0
    halves = feat // LANES
    north, south = from_sec(sec_a, sec_b)
    base = ASTEPS * halves * cols
    pad = air_pad(rows)
    for side in range(2):
        first = (cols - ASTEPS) if side else 0
        sea_first = (sea_cols - OSTEPS) if side else 0
        for h in range(halves):
            lanes = slice(h * LANES, (h + 1) * LANES)
            above = ((ASTEPS - 1) * halves + h) * cols + first
            below = h * cols + first
            stage[side, h * pad : h * pad + ASTEPS, :] = north[above : above + ASTEPS]
            for r in range(rows):
                at = h * pad + (r + 1) * ASTEPS
                stage[side, at : at + ASTEPS, :] = atmos[r, first : first + ASTEPS, lanes]
            at = h * pad + (rows + 1) * ASTEPS
            stage[side, at : at + ASTEPS, :] = south[below : below + ASTEPS]
        sea = halves * pad
        for r in range(sea_rows + 2 * OSTEPS):
            at = sea + r * OSTEPS
            if r < OSTEPS:
                row = base + r * sea_cols + sea_first
                line = north[row : row + OSTEPS]
            elif r < OSTEPS + sea_rows:
                line = ocean[r - OSTEPS, sea_first : sea_first + OSTEPS, :]
            else:
                row = base + (r - OSTEPS - sea_rows) * sea_cols + sea_first
                line = south[row : row + OSTEPS]
            stage[side, at : at + OSTEPS, :] = line
    west, east = stage[0].astype(bf16), stage[1].astype(bf16)
    out_a[...] = jnp.where(even, east, west)
    out_b[...] = jnp.where(even, west, east)


def silu(v):
    return v * (0.5 + 0.5 * jnp.tanh(0.5 * v))


def spots(tile):
    lane = lax.broadcasted_iota(jnp.int32, (8, LANES), 1)
    sub = lax.broadcasted_iota(jnp.int32, (8, LANES), 0)
    return lane, sub


def main(
    secs, tiles, atmos, cloudy, w_in, w_out, c_in, c_out, ocean, sec_a, sec_b, tile_a, tile_b,
    field, pay, sea, side_w, side_e, xs, hid, stage, sea_w, sea_e,
):
    rows, cols, feat = atmos.shape
    sea_rows, sea_cols, sea_feat = ocean.shape
    halves = feat // LANES
    s, t = lax.axis_index("sec"), lax.axis_index("tile")
    ok_n, ok_s, ok_w, ok_e = s > 0, s < secs - 1, t > 0, t < tiles - 1
    north, south = from_sec(sec_a, sec_b)
    north = jnp.where(ok_n, north, 0.0)
    south = jnp.where(ok_s, south, 0.0)
    even_t = t % 2 == 0
    ta, tb = tile_a[...].astype(f32), tile_b[...].astype(f32)
    stage[0] = jnp.where(ok_w, jnp.where(even_t, tb, ta), 0.0)
    stage[1] = jnp.where(ok_e, jnp.where(even_t, ta, tb), 0.0)
    pad = air_pad(rows)
    zero_w = jnp.zeros(side_w.shape, f32)
    side_w[...] = zero_w
    side_e[...] = zero_w
    for r in range(rows + 2):
        keep = ok_n if r == 0 else ok_s if r == rows + 1 else None
        for h in range(halves):
            lanes = slice(h * LANES, (h + 1) * LANES)
            at = h * pad + r * ASTEPS
            w, e = stage[0, at : at + ASTEPS, :], stage[1, at : at + ASTEPS, :]
            if keep is not None:
                w, e = jnp.where(keep, w, 0.0), jnp.where(keep, e, 0.0)
            side_w[r, 8 - ASTEPS : 8, lanes] = w
            side_e[r, 0:ASTEPS, lanes] = e

    def whole_row(r):
        if r < 0 or r >= rows:
            piece = north if r < 0 else south
            k = (r + ASTEPS) if r < 0 else (r - rows)
            core = jnp.concatenate(
                [piece[(k * halves + h) * cols : (k * halves + h + 1) * cols] for h in range(halves)],
                axis=1,
            )
        else:
            core = atmos[r]
        if -1 <= r <= rows:
            left, right = side_w[r + 1], side_e[r + 1]
        else:
            left = right = jnp.zeros((8, feat), f32)
        return jnp.concatenate([left, core, right], axis=0)

    wide = cols + 16
    sub = lax.broadcasted_iota(jnp.int32, (wide, feat), 0)
    inside = jnp.logical_and(
        jnp.logical_or(sub >= 8, ok_w), jnp.logical_or(sub < 8 + cols, ok_e)
    )

    def relax(up, mid, down, rate):
        n = mid.shape[-2]
        axis = mid.ndim - 2
        beside = up + down + pltpu.roll(mid, 1, axis) + pltpu.roll(mid, n - 1, axis)
        return mid + rate * (beside - 4.0 * mid)

    lines = [whole_row(-2), whole_row(-1), whole_row(0)]
    ones = []
    for r in range(-1, rows + 1):
        one = relax(lines[0], lines[1], lines[2], kappa_air)
        one = jnp.where(inside, one, 0.0)
        if r == -1:
            one = jnp.where(ok_n, one, 0.0)
        if r == rows:
            one = jnp.where(ok_s, one, 0.0)
        ones.append(one)
        if len(ones) == 3:
            two = relax(ones[0], ones[1], ones[2], kappa_air)[8 : 8 + cols]
            field[r - 1] = two
            xs[(r - 1) * cols : r * cols, :] = two.astype(bf16)
            ones = ones[1:]
        if r < rows:
            lines = lines[1:] + [whole_row(r + 2)]

    flags = cloudy[...].astype(f32)
    eye = lax.broadcasted_iota(jnp.int32, (cols, cols), 0) == lax.broadcasted_iota(
        jnp.int32, (cols, cols), 1
    )
    x = xs[...]
    width = w_in.shape[1]
    block = 256
    total = None
    for which, (first, second) in enumerate(((c_in, c_out), (w_in, w_out))):
        for j in range(width // block):
            piece = slice(j * block, (j + 1) * block)
            h = jnp.dot(x, first[:, piece], preferred_element_type=f32)
            hid[which, :, piece] = silu(h).astype(bf16)
    cloud = jnp.dot(hid[0], c_out[...], preferred_element_type=f32)
    clear = jnp.dot(hid[1], w_out[...], preferred_element_type=f32)
    lane8 = lax.broadcasted_iota(jnp.int32, (8, LANES), 1)
    sub8 = lax.broadcasted_iota(jnp.int32, (8, LANES), 0)
    half_cols = cols // 2
    means = [jnp.zeros((8, LANES), f32) for _ in range(halves)]
    for r in range(rows):
        flag = jnp.sum(
            jnp.where(eye, jnp.broadcast_to(flags[r : r + 1, :], (cols, cols)), 0.0),
            axis=1,
            keepdims=True,
        )
        span = slice(r * cols, (r + 1) * cols)
        tendency = (clear[span] + flag * cloud[span]).astype(bf16).astype(f32)
        new = field[r] + tendency
        field[r] = new
        for k in range(cols // 8):
            at = (r // 2) * half_cols + 4 * k
            hit = lane8 == at + sub8 // 2
            for h in range(halves):
                value = new[8 * k : 8 * k + 8, h * LANES : h * LANES + 1]
                means[h] = means[h] + jnp.where(hit, value, 0.0)
    tops = [jnp.zeros((8, LANES), f32) for _ in range(2)]
    for r in range(sea_rows):
        for k in range(sea_cols // 8):
            hit = lane8 == r * sea_cols + 8 * k + sub8
            for h in range(2):
                at = h * (sea_feat // 2)
                value = ocean[r, 8 * k : 8 * k + 8, at : at + 1]
                tops[h] = tops[h] + jnp.where(hit, value, 0.0)
    for q, part in enumerate((0.25 * means[0], 0.25 * means[1], tops[0], tops[1])):
        line = jnp.sum(part, axis=0, keepdims=True)
        pay[:, q, :] = jnp.broadcast_to(line, (pay.shape[0], LANES))

    base = ASTEPS * halves * cols
    tall = sea_rows + 2 * OSTEPS
    sea_w[...] = jnp.zeros(sea_w.shape, f32)
    sea_e[...] = jnp.zeros(sea_e.shape, f32)
    for r in range(tall):
        keep = ok_n if r < OSTEPS else ok_s if r >= OSTEPS + sea_rows else None
        at = halves * pad + r * OSTEPS
        w, e = stage[0, at : at + OSTEPS, :], stage[1, at : at + OSTEPS, :]
        if keep is not None:
            w, e = jnp.where(keep, w, 0.0), jnp.where(keep, e, 0.0)
        sea_w[r, 8 - OSTEPS : 8, :] = w
        sea_e[r, 0:OSTEPS, :] = e

    sea_wide = sea_cols + 16
    sea_sub = lax.broadcasted_iota(jnp.int32, (tall, sea_wide, sea_feat), 1)
    sea_row = lax.broadcasted_iota(jnp.int32, (tall, sea_wide, sea_feat), 0)
    sea_in = jnp.logical_and(
        jnp.logical_and(
            jnp.logical_or(sea_sub >= 8, ok_w), jnp.logical_or(sea_sub < 8 + sea_cols, ok_e)
        ),
        jnp.logical_and(
            jnp.logical_or(sea_row >= OSTEPS, ok_n),
            jnp.logical_or(sea_row < OSTEPS + sea_rows, ok_s),
        ),
    )
    core = jnp.concatenate(
        [
            north[base : base + OSTEPS * sea_cols].reshape(OSTEPS, sea_cols, sea_feat),
            ocean[...],
            south[base : base + OSTEPS * sea_cols].reshape(OSTEPS, sea_cols, sea_feat),
        ],
        axis=0,
    )
    state = jnp.concatenate([sea_w[...], core, sea_e[...]], axis=1)
    nothing = jnp.zeros((1, sea_wide, sea_feat), f32)
    for step in range(OSTEPS):
        up = jnp.concatenate([nothing, state[:-1]], axis=0)
        down = jnp.concatenate([state[1:], nothing], axis=0)
        state = jnp.where(sea_in, relax(up, state, down, kappa_sea), 0.0)
    sea[...] = state[OSTEPS : OSTEPS + sea_rows, 8 : 8 + sea_cols]


def final(secs, tiles, tile_map, gathered, field, sea, air_out, sea_out, back):
    rows, cols, feat = field.shape
    sea_rows, sea_cols, sea_feat = sea.shape
    count = secs * tiles
    s, t = lax.axis_index("sec"), lax.axis_index("tile")
    me = s * tiles + t
    halves = feat // LANES
    row1 = lax.broadcasted_iota(jnp.int32, (count, 1), 0)
    row_t = row1 % tiles
    under = jnp.zeros((count, 1), jnp.int32)
    for k in range(tiles):
        under = jnp.where(row_t == k, tile_map[k], under)
    under = row1 - row_t + under
    perm = (lax.broadcasted_iota(jnp.int32, (count, count), 1) == under).astype(f32)
    air0 = jnp.dot(perm, gathered[:, 0, :], precision=HIGHEST, preferred_element_type=f32)
    air1 = jnp.dot(perm, gathered[:, 1, :], precision=HIGHEST, preferred_element_type=f32)
    top0, top1 = gathered[:, 2, :], gathered[:, 3, :]
    state0 = top0 + 0.5 * (0.8 * (top0 - air0))
    state1 = top1 + 0.5 * (0.8 * (0.5 * top0 - air1))

    lane = lax.broadcasted_iota(jnp.int32, (count, LANES), 1)
    row = lax.broadcasted_iota(jnp.int32, (count, LANES), 0)
    lane_c = lane % sea_cols
    first_c, last_c = lane_c == 0, lane_c == sea_cols - 1
    first_r, last_r = lane < sea_cols, lane >= LANES - sea_cols
    first_t, last_t = row % tiles == 0, row % tiles == tiles - 1
    first_s, last_s = row < tiles, row >= count - tiles

    def roll(v, shift, axis):
        return pltpu.roll(v, shift % v.shape[axis], axis)

    def relax(v):
        east_t = jnp.where(last_t, 0.0, roll(v, -1, 0))
        west_t = jnp.where(first_t, 0.0, roll(v, 1, 0))
        east = jnp.where(last_c, roll(east_t, sea_cols - 1, 1), roll(v, -1, 1))
        west = jnp.where(first_c, roll(west_t, 1 - sea_cols, 1), roll(v, 1, 1))
        down, up = roll(v, -sea_cols, 1), roll(v, sea_cols, 1)
        down_s = jnp.where(last_s, 0.0, roll(down, -tiles, 0))
        up_s = jnp.where(first_s, 0.0, roll(up, tiles, 0))
        beside = jnp.where(last_r, down_s, down) + jnp.where(first_r, up_s, up) + east + west
        return v + kappa_sea * (beside - 4.0 * v)

    for step in range(OSTEPS):
        state0, state1 = relax(state0), relax(state1)

    from_me = row1 == me
    source = under == me

    def pick(mask, v):
        return jnp.sum(jnp.where(mask, v, 0.0), axis=0, keepdims=True)

    own0, own1 = pick(from_me, state0), pick(from_me, state1)
    landing, returned = pick(source, top0), pick(source, state0)

    lane8 = lax.broadcasted_iota(jnp.int32, (8, LANES), 1)
    sub8 = lax.broadcasted_iota(jnp.int32, (8, LANES), 0)
    own0, own1 = jnp.broadcast_to(own0, (8, LANES)), jnp.broadcast_to(own1, (8, LANES))
    landing = jnp.broadcast_to(landing, (8, LANES))
    for r in range(sea_rows):
        for k in range(sea_cols // 8):
            hit = lane8 == r * sea_cols + 8 * k + sub8
            v0 = jnp.sum(jnp.where(hit, own0, 0.0), axis=1, keepdims=True)
            v1 = jnp.sum(jnp.where(hit, own1, 0.0), axis=1, keepdims=True)
            old = sea[r, 8 * k : 8 * k + 8, :]
            new = jnp.where(lane8 == 0, v0, jnp.where(lane8 == sea_feat // 2, v1, old))
            sea_out[r, 8 * k : 8 * k + 8, :] = new
    half_cols = cols // 2
    for r2 in range(rows // 2):
        for k in range(cols // 8):
            hit = lane8 == r2 * half_cols + 4 * k + sub8 // 2
            value = jnp.sum(jnp.where(hit, landing, 0.0), axis=1, keepdims=True)
            for r in (2 * r2, 2 * r2 + 1):
                for h in range(halves):
                    lanes = slice(h * LANES, (h + 1) * LANES)
                    old = field[r, 8 * k : 8 * k + 8, lanes]
                    flux = 0.8 * ((1.0 if h == 0 else 0.5) * value - old)
                    air_out[r, 8 * k : 8 * k + 8, lanes] = old + jnp.where(
                        lane8 == 0, 0.5 * flux, 0.0
                    )
    lane_b = lax.broadcasted_iota(jnp.int32, (rows, LANES), 1)
    row_b = lax.broadcasted_iota(jnp.int32, (rows, LANES), 0)
    lines = jnp.where(
        lane_b // half_cols == row_b // 2, jnp.broadcast_to(returned, (rows, LANES)), 0.0
    )
    spread = (
        lax.broadcasted_iota(jnp.int32, (LANES, cols), 0) % half_cols
        == lax.broadcasted_iota(jnp.int32, (LANES, cols), 1) // 2
    ).astype(f32)
    back[...] = jnp.dot(lines, spread, precision=HIGHEST, preferred_element_type=f32)


def local(atmos, cloudy, weight_in, weight_out, cloud_in, cloud_out, ocean, tile_map):
    rows, cols, feat = atmos.shape
    sea_rows, sea_cols, sea_feat = ocean.shape
    secs, tiles = lax.axis_size("sec"), lax.axis_size("tile")
    count = secs * tiles
    halves = feat // LANES
    columns = rows * cols
    width = weight_in.shape[1]
    sec_even, sec_odd, tile_even, tile_odd = exchanges(secs, tiles)
    shape = jax.ShapeDtypeStruct
    params = pltpu.CompilerParams(vmem_limit_bytes=16 * 1024 * 1024)

    lines = ASTEPS * halves * cols + OSTEPS * sea_cols
    out = shape((lines, LANES), bf16)
    send_a, send_b = pl.pallas_call(
        pack_sec, out_shape=(out, out), in_specs=[VMEM] * 2, out_specs=(VMEM, VMEM),
        compiler_params=params, name="pack_sec",
    )(atmos, ocean)
    sec_a = lax.ppermute(send_a, AXES, sec_even)
    sec_b = lax.ppermute(send_b, AXES, sec_odd)

    lines = halves * air_pad(rows) + OSTEPS * (sea_rows + 2 * OSTEPS)
    out = shape((lines, LANES), bf16)
    send_a, send_b = pl.pallas_call(
        pack_tile, out_shape=(out, out), in_specs=[VMEM] * 4, out_specs=(VMEM, VMEM),
        scratch_shapes=[pltpu.VMEM((2, lines, LANES), f32)],
        compiler_params=params, name="pack_tile",
    )(atmos, ocean, sec_a, sec_b)
    tile_a = lax.ppermute(send_a, AXES, tile_even)
    tile_b = lax.ppermute(send_b, AXES, tile_odd)

    field, pay, sea = pl.pallas_call(
        functools.partial(main, secs, tiles),
        out_shape=(
            shape(atmos.shape, f32),
            shape((count, 4, LANES), f32),
            shape(ocean.shape, f32),
        ),
        in_specs=[VMEM] * 11,
        out_specs=(VMEM,) * 3,
        scratch_shapes=[
            pltpu.VMEM((rows + 2, 8, feat), f32),
            pltpu.VMEM((rows + 2, 8, feat), f32),
            pltpu.VMEM((columns, feat), bf16),
            pltpu.VMEM((2, columns, width), bf16),
            pltpu.VMEM((2, lines, LANES), f32),
            pltpu.VMEM((sea_rows + 2 * OSTEPS, 8, sea_feat), f32),
            pltpu.VMEM((sea_rows + 2 * OSTEPS, 8, sea_feat), f32),
        ],
        compiler_params=params,
        name="main",
    )(atmos, cloudy, weight_in, weight_out, cloud_in, cloud_out, ocean, sec_a, sec_b, tile_a, tile_b)

    gathered = lax.all_to_all(pay, AXES, 0, 0)

    return pl.pallas_call(
        functools.partial(final, secs, tiles),
        out_shape=(
            shape(atmos.shape, f32),
            shape(ocean.shape, f32),
            shape((rows, cols), f32),
        ),
        in_specs=[SMEM] + [VMEM] * 3,
        out_specs=(VMEM,) * 3,
        compiler_params=params,
        name="final",
    )(tile_map, gathered, field, sea)


def solution(mesh):
    placed = (
        P("sec", "tile", None),
        P("sec", "tile"),
        P(),
        P(),
        P(),
        P(),
        P("sec", "tile", None),
        P(),
    )
    return jax.shard_map(
        local,
        mesh=mesh,
        in_specs=placed,
        out_specs=(P("sec", "tile", None), P("sec", "tile", None), P("sec", "tile")),
        check_vma=False,
    )
```

time: 266 us -> 34.3 us (0.13); the launches traced: 262 us -> 33.9 us
  blocking collectives: 125 us -> 14.3 us
  starting transfers between devices: 67 us -> 4.84 us
  local copies, waits for them, and re-layouts: 35.3 us -> 4.62 us
  other arithmetic: 20.8 us -> 0 us
  waiting for transfers between devices: 11.8 us -> 4.34 us
  Pallas kernels: 0 us -> 5.1 us
    all_gather x4 -> x0, blocking collectives: 125 us -> none  [the longest x1 32 us: local(): lax.all_gather(sea[:, :, 0], 'tile', axis=1, tiled=True)]
    ppermute x24 -> x4, starting transfers between devices: 67 us -> 4.84 us  [the longest x1 2.61 us: local(): sec_b = lax.ppermute(send_b, AXES, sec_odd)]
    unnamed x42 -> x16, local copies, waits for them, and re-layouts: 22.9 us -> 4.62 us
    all_to_all x0 -> x1, blocking collectives: none -> 14.3 us  [local(): gathered = lax.all_to_all(pay, AXES, 0, 0)]
    ppermute x24 -> x4, waiting for transfers between devices: 11.8 us -> 4.34 us  [the longest x1 2.32 us: local(): tile_a = lax.ppermute(send_a, AXES, tile_even)]
    add x8 -> x0, other arithmetic: 6.85 us -> none  [the longest x5 4.9 us: relax(): return inner + rate * (beside - 4.0 * inner)]
    convert_element_type x2 -> x0, other arithmetic: 5.89 us -> none  [the longest x1 5.19 us: local(): inputs = field.reshape(columns, feat).astype(jnp.bfloat16)]
    pallas_call x0 -> x4, Pallas kernels: none -> 5.1 us  [the longest x1 2.66 us: local(): pl.pallas_call(functools.partial(main, secs, tiles), out_shape=(shape(atm...]
  transfers between devices with their start and end apart: 24 -> 4, of which waited for: 8 -> 2; matrix products, arithmetic and copies ran while one was open for 7% -> 0% of each run, Pallas kernels for 0% -> 0%
where the time goes in v1:
time: 34.3 us; the launch traced here: 33.9 us
  blocking collectives  14.3 us (42%)
  Pallas kernels  5.1 us (15%)
  starting transfers between devices  4.84 us (14%)
  local copies, waits for them, and re-layouts  4.62 us (13%)
  waiting for transfers between devices  4.34 us (13%)
  between operations  0.68 us (2%)
    all_to_all x1, blocking collectives, local(): gathered = lax.all_to_all(pay, AXES, 0, 0)  14.3 us
    unnamed x16, local copies, waits for them, and re-layouts  4.62 us
    pallas_call x1, Pallas kernels, local(): pl.pallas_call(functools.partial(main, secs, tiles), out_shape=(shape(atm...  2.66 us
    ppermute x1, starting transfers between devices, local(): sec_b = lax.ppermute(send_b, AXES, sec_odd)  2.61 us
    pallas_call x1, Pallas kernels, local(): pl.pallas_call(functools.partial(final, secs, tiles), out_shape=(shape(at...  2.37 us
    ppermute x1, waiting for transfers between devices, local(): tile_a = lax.ppermute(send_a, AXES, tile_even)  2.32 us
    ppermute x1, waiting for transfers between devices, local(): sec_b = lax.ppermute(send_b, AXES, sec_odd)  2.02 us
    ppermute x1, starting transfers between devices, local(): tile_a = lax.ppermute(send_a, AXES, tile_even)  1.54 us
  transfers between devices with their start and end apart: 4, of which 2 were waited for; matrix products, arithmetic and copies ran while one was open for 0% of the time, Pallas kernels for 0%

profile of v1, /device:TPU:0, one launch (start us, length us, event | category | flops | bytes accessed | tf_op | source)
XLA Modules:
  0.0 33.9 jit_solution(6390870740656244080)
XLA Ops:
  0.6 0.0 copy-start
  0.6 1.0 %copy-done = f32[16,32,256]{2,1,0:T(8,128)S(1)} copy-done((f32[16,32,256]{2,1,0:T(8,128)S(1)}, f32[16,32,256]{2,1,0:T(8,128)}, u32[]{:S(2)}) %copy-start) | copy-done | bytes 524312
  1.7 0.0 copy-start.1
  1.7 0.8 %copy-done.1 = f32[8,16,128]{2,1,0:T(8,128)S(1)} copy-done((f32[8,16,128]{2,1,0:T(8,128)S(1)}, f32[8,16,128]{2,1,0:T(8,128)}, u32[]{:S(2)}) %copy-start.1) | copy-done | bytes 65560
  2.5 0.0 copy-start.2
  2.5 0.0 copy-start.3
  2.5 0.5 %collective-permute-start = (bf16[192,128]{1,0:T(8,128)(2,1)S(1)}, bf16[192,128]{1,0:T(8,128)(2,1)S(1)}, u32[]{:S(2)}, u32[]{:S(2)}) collective-permute-start(bf16[192,128]{1,0:T(8,128)(2,1)S(1)} %get-tuple-element.10), channel_id=1, source_target_pairs={{0,8},{1,9},{2,10},{3,11},{4,12},{5,13},{6,14},{7,15},{8,0},{9,1},... | collective-permute-start | bytes 147464 | tf_op jit(solution)/shard_map/ppermute | solution.py:403
  3.1 2.6 %collective-permute-start.1 = (bf16[192,128]{1,0:T(8,128)(2,1)S(1)}, bf16[192,128]{1,0:T(8,128)(2,1)S(1)}, u32[]{:S(2)}, u32[]{:S(2)}) collective-permute-start(bf16[192,128]{1,0:T(8,128)(2,1)S(1)} %get-tuple-element.11), channel_id=1, source_target_pairs={{0,24},{1,25},{2,26},{3,27},{4,28},{5,29},{6,30},{7,31},{8,16},{9,... | collective-permute-start | bytes 147464 | tf_op jit(solution)/shard_map/ppermute | solution.py:404
  5.7 0.0 collective-permute-done.sec_a
  5.7 2.0 %collective-permute-done.1.sec_b = bf16[192,128]{1,0:T(8,128)(2,1)S(1)} collective-permute-done((bf16[192,128]{1,0:T(8,128)(2,1)S(1)}, bf16[192,128]{1,0:T(8,128)(2,1)S(1)}, u32[]{:S(2)}, u32[]{:S(2)}) %collective-permute-start.1) | collective-permute-done | bytes 49184 | tf_op jit(solution)/shard_map/ppermute | solution.py:404
  7.7 0.0 copy-start.6
  7.7 0.1 pack_tile.1
  7.7 1.5 %collective-permute-start.2 = (bf16[144,128]{1,0:T(8,128)(2,1)S(1)}, bf16[144,128]{1,0:T(8,128)(2,1)S(1)}, u32[]{:S(2)}, u32[]{:S(2)}) collective-permute-start(bf16[144,128]{1,0:T(8,128)(2,1)S(1)} %get-tuple-element.12), channel_id=1, source_target_pairs={{0,1},{1,0},{2,3},{3,2},{4,5},{5,4},{6,7},{7,6},{8,9},{9,8},{10,11... | collective-permute-start | bytes 110600 | tf_op jit(solution)/shard_map/ppermute | solution.py:413
  9.3 0.2 collective-permute-start.3
  9.5 2.3 %collective-permute-done.2.tile_a = bf16[144,128]{1,0:T(8,128)(2,1)S(1)} collective-permute-done((bf16[144,128]{1,0:T(8,128)(2,1)S(1)}, bf16[144,128]{1,0:T(8,128)(2,1)S(1)}, u32[]{:S(2)}, u32[]{:S(2)}) %collective-permute-start.2) | collective-permute-done | bytes 36896 | tf_op jit(solution)/shard_map/ppermute | solution.py:413
  11.8 0.0 collective-permute-done.3.tile_b
  11.8 0.0 copy-done.2
  11.8 0.0 copy-done.3
  11.8 0.0 copy-done.6
  11.8 0.0 copy-start.4
  11.8 1.0 %copy-done.4 = bf16[256,1024]{1,0:T(8,128)(2,1)S(1)} copy-done((bf16[256,1024]{1,0:T(8,128)(2,1)S(1)}, bf16[256,1024]{1,0:T(8,128)(2,1)}, u32[]{:S(2)}) %copy-start.4) | copy-done | bytes 524312
  12.8 0.0 copy-start.5
  12.8 1.0 %copy-done.5 = bf16[1024,256]{1,0:T(8,128)(2,1)S(1)} copy-done((bf16[1024,256]{1,0:T(8,128)(2,1)S(1)}, bf16[1024,256]{1,0:T(8,128)(2,1)}, u32[]{:S(2)}) %copy-start.5) | copy-done | bytes 524312
  13.9 2.7 %main.1 = (f32[16,32,256]{2,1,0:T(8,128)S(1)}, f32[32,4,128]{2,1,0:T(4,128)S(1)}, f32[8,16,128]{2,1,0:T(8,128)S(1)}) custom-call(f32[16,32,256]{2,1,0:T(8,128)S(1)} %copy-done, s32[16,32]{1,0:T(8,128)S(1)} %copy-done.6, bf16[256,1024]{1,0:T(8,128)(2,1)S(1)} %copy-done.2, bf16[1024,256]{1,0:T(8,128)(2,1)S(1)} %copy-done.3, bf16[256,1024]{1,0:T(8,128)(2,1)S(1)} %copy-done.4, ...), custom_call_target="tpu_custom_call" | custom-call | tf_op jit(solution)/shard_map/main/pallas_call | solution.py:416
  16.6 14.3 %all_to_all.5.gathered = f32[32,4,128]{2,1,0:T(4,128)S(1)} all-to-all(f32[32,4,128]{2,1,0:T(4,128)S(1)} %get-tuple-element.14), channel_id=1, replica_groups=mesh['sec'=4,'tile'=8] {'sec','tile'}, dimensions={0} | all-to-all | bytes 131072 | tf_op jit(solution)/shard_map/all_to_all | solution.py:438
  30.9 0.0 copy-start.7
  30.9 0.7 %copy-done.7 = s32[8]{0:T(128)S(1)} copy-done((s32[8]{0:T(128)S(1)}, s32[8]{0:T(128)}, u32[]{:S(2)}) %copy-start.7) | copy-done | bytes 56
  31.6 2.4 %final.1 = (f32[16,32,256]{2,1,0:T(8,128)}, f32[8,16,128]{2,1,0:T(8,128)}, f32[16,32]{1,0:T(8,128)}) custom-call(s32[8]{0:T(128)S(1)} %copy-done.7, f32[32,4,128]{2,1,0:T(4,128)S(1)} %all_to_all.5.gathered, f32[16,32,256]{2,1,0:T(8,128)S(1)} %get-tuple-element.15.field, f32[8,16,128]{2,1,0:T(8,128)S(1)} %get-tuple-element.16.sea), custom_call_target="tpu_custom_call" | custom-call | tf_op jit(solution)/shard_map/final/pallas_call | solution.py:440
  (1 shorter events, 0.0 us)
Async XLA Ops:
  0.6 1.0 %copy-start = (f32[16,32,256]{2,1,0:T(8,128)S(1)}, f32[16,32,256]{2,1,0:T(8,128)}, u32[]{:S(2)}) copy-start(f32[16,32,256]{2,1,0:T(8,128)} %atmos.5) | copy-start | bytes 1572868
  1.7 0.8 %copy-start.1 = (f32[8,16,128]{2,1,0:T(8,128)S(1)}, f32[8,16,128]{2,1,0:T(8,128)}, u32[]{:S(2)}) copy-start(f32[8,16,128]{2,1,0:T(8,128)} %ocean.5) | copy-start | bytes 196612
  2.5 9.3 %copy-start.2 = (bf16[256,1024]{1,0:T(8,128)(2,1)S(1)}, bf16[256,1024]{1,0:T(8,128)(2,1)}, u32[]{:S(2)}) copy-start(bf16[256,1024]{1,0:T(8,128)(2,1)} %w_in.1) | copy-start | bytes 1572868
  2.5 9.3 %copy-start.3 = (bf16[1024,256]{1,0:T(8,128)(2,1)S(1)}, bf16[1024,256]{1,0:T(8,128)(2,1)}, u32[]{:S(2)}) copy-start(bf16[1024,256]{1,0:T(8,128)(2,1)} %w_out.1) | copy-start | bytes 1572868
  2.5 3.1 %collective-permute-start = (bf16[192,128]{1,0:T(8,128)(2,1)S(1)}, bf16[192,128]{1,0:T(8,128)(2,1)S(1)}, u32[]{:S(2)}, u32[]{:S(2)}) collective-permute-start(bf16[192,128]{1,0:T(8,128)(2,1)S(1)} %get-tuple-element.10), channel_id=1, source_target_pairs={{0,8},{1,9},{2,10},{3,11},{4,12},{5,13},{6,14},{7,15},{8,0},{9,1},... | collective-permute-start | bytes 147464 | tf_op jit(solution)/shard_map/ppermute | solution.py:403
  3.1 4.6 %collective-permute-start.1 = (bf16[192,128]{1,0:T(8,128)(2,1)S(1)}, bf16[192,128]{1,0:T(8,128)(2,1)S(1)}, u32[]{:S(2)}, u32[]{:S(2)}) collective-permute-start(bf16[192,128]{1,0:T(8,128)(2,1)S(1)} %get-tuple-element.11), channel_id=1, source_target_pairs={{0,24},{1,25},{2,26},{3,27},{4,28},{5,29},{6,30},{7,31},{8,16},{9,... | collective-permute-start | bytes 147464 | tf_op jit(solution)/shard_map/ppermute | solution.py:404
  7.7 4.1 %copy-start.6 = (s32[16,32]{1,0:T(8,128)S(1)}, s32[16,32]{1,0:T(8,128)}, u32[]{:S(2)}) copy-start(s32[16,32]{1,0:T(8,128)} %cloudy.1) | copy-start | bytes 6148
  7.7 4.0 %collective-permute-start.2 = (bf16[144,128]{1,0:T(8,128)(2,1)S(1)}, bf16[144,128]{1,0:T(8,128)(2,1)S(1)}, u32[]{:S(2)}, u32[]{:S(2)}) collective-permute-start(bf16[144,128]{1,0:T(8,128)(2,1)S(1)} %get-tuple-element.12), channel_id=1, source_target_pairs={{0,1},{1,0},{2,3},{3,2},{4,5},{5,4},{6,7},{7,6},{8,9},{9,8},{10,11... | collective-permute-start | bytes 110600 | tf_op jit(solution)/shard_map/ppermute | solution.py:413
  9.3 2.5 %collective-permute-start.3 = (bf16[144,128]{1,0:T(8,128)(2,1)S(1)}, bf16[144,128]{1,0:T(8,128)(2,1)S(1)}, u32[]{:S(2)}, u32[]{:S(2)}) collective-permute-start(bf16[144,128]{1,0:T(8,128)(2,1)S(1)} %get-tuple-element.13), channel_id=1, source_target_pairs={{0,8},{1,2},{2,1},{3,4},{4,3},{5,6},{6,5},{7,15},{8,0},{9,10},{10,... | collective-permute-start | bytes 110600 | tf_op jit(solution)/shard_map/ppermute | solution.py:414
  11.8 1.0 %copy-start.4 = (bf16[256,1024]{1,0:T(8,128)(2,1)S(1)}, bf16[256,1024]{1,0:T(8,128)(2,1)}, u32[]{:S(2)}) copy-start(bf16[256,1024]{1,0:T(8,128)(2,1)} %c_in.1) | copy-start | bytes 1572868
  12.8 1.0 %copy-start.5 = (bf16[1024,256]{1,0:T(8,128)(2,1)S(1)}, bf16[1024,256]{1,0:T(8,128)(2,1)}, u32[]{:S(2)}) copy-start(bf16[1024,256]{1,0:T(8,128)(2,1)} %c_out.1) | copy-start | bytes 1572868
  30.9 0.7 %copy-start.7 = (s32[8]{0:T(128)S(1)}, s32[8]{0:T(128)}, u32[]{:S(2)}) copy-start(s32[8]{0:T(128)} %tile_map.1) | copy-start | bytes 100

commit v2 on v0

v2 whole, which is shorter than its diff:
```python
import functools

import jax
import jax.numpy as jnp
from jax import lax
from jax.experimental import pallas as pl
from jax.experimental.pallas import tpu as pltpu
from jax.sharding import PartitionSpec as P

ASTEPS = 2
OSTEPS = 4
LANES = 128

kappa_air = 0.2
kappa_sea = 0.2

f32 = jnp.float32
bf16 = jnp.bfloat16
HIGHEST = lax.Precision.HIGHEST
VMEM = pl.BlockSpec(memory_space=pltpu.VMEM)
SMEM = pl.BlockSpec(memory_space=pltpu.SMEM)
HBM = pl.BlockSpec(memory_space=pltpu.HBM)
AXES = ("sec", "tile")


def exchanges(secs, tiles):
    def whole(partner):
        return [
            (s * tiles + t, partner(s, t)[0] * tiles + partner(s, t)[1])
            for s in range(secs)
            for t in range(tiles)
        ]

    def odd_sec(s, t):
        if s in (0, secs - 1):
            return secs - 1 - s, t
        return (s + 1 if s % 2 else s - 1), t

    def odd_tile(s, t):
        if t in (0, tiles - 1):
            return s ^ 1, t
        return s, (t + 1 if t % 2 else t - 1)

    return (
        whole(lambda s, t: (s ^ 1, t)),
        whole(odd_sec),
        whole(lambda s, t: (s, t ^ 1)),
        whole(odd_tile),
    )


def sublane(shape):
    return lax.broadcasted_iota(jnp.int32, shape, len(shape) - 2)


def turn(v, shift):
    return v if shift % 8 == 0 else pltpu.roll(v, shift % 8, 0)


def halves_of(v):
    return [v[:, at : at + LANES] for at in range(0, v.shape[1], LANES)]


def pack_tile(atmos, ocean, out_a, out_b, west, east, sea, sems):
    rows, cols, feat = atmos.shape
    sea_rows, sea_cols, _ = ocean.shape
    copies = (
        pltpu.make_async_copy(atmos.at[:, 0:8, :], west, sems.at[0]),
        pltpu.make_async_copy(atmos.at[:, cols - 8 : cols, :], east, sems.at[1]),
        pltpu.make_async_copy(ocean, sea, sems.at[2]),
    )
    for copy in copies:
        copy.start()
    for copy in copies:
        copy.wait()
    to_west, to_east = [], []
    sub = sublane((8, feat))
    for g in range(rows // 4):
        tile_w, tile_e = west[4 * g], turn(east[4 * g], 2)
        for k in range(1, 4):
            tile_w = jnp.where(sub < 2 * k, tile_w, turn(west[4 * g + k], 2 * k))
            tile_e = jnp.where(sub < 2 * k, tile_e, turn(east[4 * g + k], 2 * k + 2))
        to_west += halves_of(tile_w)
        to_east += halves_of(tile_e)
    low = sublane((8, LANES)) < 4
    for r in range(0, sea_rows, 2):
        to_west.append(jnp.where(low, sea[r, 0:8], turn(sea[r + 1, 0:8], 4)))
        to_east.append(
            jnp.where(low, turn(sea[r, sea_cols - 8 :], 4), sea[r + 1, sea_cols - 8 :])
        )
    to_west = jnp.concatenate(to_west, axis=0).astype(bf16)
    to_east = jnp.concatenate(to_east, axis=0).astype(bf16)
    even = lax.axis_index("tile") % 2 == 0
    out_a[...] = jnp.where(even, to_east, to_west)
    out_b[...] = jnp.where(even, to_west, to_east)


class Sides:
    def __init__(self, tiles, rows, feat, tile_a, tile_b):
        t = lax.axis_index("tile")
        even = t % 2 == 0
        a, b = tile_a[...].astype(f32), tile_b[...].astype(f32)
        self.west = jnp.where(t > 0, jnp.where(even, b, a), 0.0)
        self.east = jnp.where(t < tiles - 1, jnp.where(even, a, b), 0.0)
        self.halves = feat // LANES
        self.sea_at = rows // 4 * self.halves
        self.low = sublane((8, LANES)) < 4

    def merge(self, tile, shift_w, shift_e):
        span = slice(8 * tile, 8 * tile + 8)
        return jnp.where(self.low, turn(self.east[span], shift_e), turn(self.west[span], shift_w))

    def air(self, r):
        g, k = r // 4, r % 4
        return jnp.concatenate(
            [self.merge(g * self.halves + h, -2 * k - 2, -2 * k) for h in range(self.halves)],
            axis=1,
        )

    def sea(self, r):
        return self.merge(self.sea_at + r // 2, 4 if r % 2 == 0 else 0, 4 * (r % 2))


def pack_sec(tiles, atmos, ocean, tile_a, tile_b, out_a, out_b):
    rows, cols, feat = atmos.shape
    sea_rows, sea_cols, _ = ocean.shape
    sides = Sides(tiles, rows, feat, tile_a, tile_b)

    def payload(first, corner, sea_first):
        parts = []
        for r in range(ASTEPS):
            parts += halves_of(atmos[first + r])
        parts += halves_of(sides.air(corner))
        parts += [ocean[sea_first + r] for r in range(OSTEPS)]
        parts += [sides.sea(sea_first + r) for r in range(OSTEPS)]
        return jnp.concatenate(parts, axis=0).astype(bf16)

    to_north = payload(0, 0, 0)
    to_south = payload(rows - ASTEPS, rows - 1, sea_rows - OSTEPS)
    even = lax.axis_index("sec") % 2 == 0
    out_a[...] = jnp.where(even, to_south, to_north)
    out_b[...] = jnp.where(even, to_north, to_south)


class Ends:
    def __init__(self, secs, cols, feat, sea_cols, sec_a, sec_b):
        s = lax.axis_index("sec")
        even = s % 2 == 0
        a, b = sec_a[...].astype(f32), sec_b[...].astype(f32)
        self.north = jnp.where(s > 0, jnp.where(even, b, a), 0.0)
        self.south = jnp.where(s < secs - 1, jnp.where(even, a, b), 0.0)
        self.halves, self.cols, self.sea_cols = feat // LANES, cols, sea_cols
        self.corner = ASTEPS * self.halves * cols
        self.sea_at = self.corner + 8 * self.halves
        self.side_at = self.sea_at + OSTEPS * sea_cols

    def air(self, piece, k):
        cut = [(k * self.halves + h) * self.cols for h in range(self.halves)]
        return jnp.concatenate([piece[at : at + self.cols] for at in cut], axis=1)

    def air_side(self, piece):
        cut = [self.corner + 8 * h for h in range(self.halves)]
        return jnp.concatenate([piece[at : at + 8] for at in cut], axis=1)

    def sea(self, piece, k):
        core = piece[self.sea_at + k * self.sea_cols : self.sea_at + (k + 1) * self.sea_cols]
        side = piece[self.side_at + 8 * k : self.side_at + 8 * k + 8]
        return core, side


def relax(up, mid, down, rate):
    axis = mid.ndim - 2
    beside = up + down + pltpu.roll(mid, 1, axis) + pltpu.roll(mid, mid.shape[axis] - 1, axis)
    return mid + rate * (beside - 4.0 * mid)


def columns_inside(tiles, shape):
    t = lax.axis_index("tile")
    sub = sublane(shape)
    return jnp.logical_and(
        jnp.logical_or(sub >= 8, t > 0), jnp.logical_or(sub < shape[-2] - 8, t < tiles - 1)
    )


def silu(v):
    return v * (0.5 + 0.5 * jnp.tanh(0.5 * v))


def physics(x, w_in, w_out, c_in, c_out, hid):
    width = w_in.shape[1]
    block = 256
    for which, first in enumerate((w_in, c_in)):
        for j in range(0, width, block):
            h = jnp.dot(x, first[:, j : j + block], preferred_element_type=f32)
            hid[which, :, j : j + block] = silu(h).astype(bf16)
    clear = jnp.dot(hid[0], w_out[...], preferred_element_type=f32)
    cloud = jnp.dot(hid[1], c_out[...], preferred_element_type=f32)
    return clear, cloud


def upright(line):
    n = line.shape[1]
    shape = (n, n)
    eye = sublane(shape) == lax.broadcasted_iota(jnp.int32, shape, 1)
    return jnp.sum(jnp.where(eye, jnp.broadcast_to(line, shape), 0.0), axis=1, keepdims=True)


def tile_iotas():
    return lax.broadcasted_iota(jnp.int32, (8, LANES), 1), sublane((8, LANES))


def add_row(means, new, r):
    lane, sub = tile_iotas()
    cols = new.shape[0]
    for k in range(cols // 8):
        hit = lane == (r // 2) * (cols // 2) + 4 * k + sub // 2
        for q in range(2):
            value = new[8 * k : 8 * k + 8, q * LANES : q * LANES + 1]
            means[q] = means[q] + jnp.where(hit, value, 0.0)


def inner(
    secs, tiles, tile_map, atmos, cloudy, w_in, w_out, c_in, c_out, ocean, tile_a, tile_b,
    field, sums, perm, source, xs, hid,
):
    rows, cols, feat = atmos.shape
    sea_rows, sea_cols, sea_feat = ocean.shape
    sides = Sides(tiles, rows, feat, tile_a, tile_b)
    inside = columns_inside(tiles, (cols + 16, feat))

    def line(r):
        side = sides.air(r)
        return jnp.concatenate([side, atmos[r], side], axis=0)

    lines, ones = [line(0), line(1)], []
    for r in range(1, rows - 1):
        lines.append(line(r + 1))
        ones.append(jnp.where(inside, relax(*lines[-3:], kappa_air), 0.0))
        if len(ones) >= 3:
            two = relax(*ones[-3:], kappa_air)[8 : 8 + cols]
            field[r - 3] = two
            xs[(r - 3) * cols : (r - 2) * cols, :] = two.astype(bf16)
    clear, cloud = physics(xs[...], w_in, w_out, c_in, c_out, hid)
    flags = cloudy[...].astype(f32)
    means = [jnp.zeros((8, LANES), f32) for _ in range(2)]
    for k in range(rows - 4):
        span = slice(k * cols, (k + 1) * cols)
        flag = upright(flags[k + 2 : k + 3, :])
        new = field[k] + (clear[span] + flag * cloud[span]).astype(bf16).astype(f32)
        field[k] = new
        add_row(means, new, k + 2)
    lane, sub = tile_iotas()
    tops = [jnp.zeros((8, LANES), f32) for _ in range(2)]
    for r in range(sea_rows):
        for k in range(sea_cols // 8):
            hit = lane == r * sea_cols + 8 * k + sub
            for q in range(2):
                at = q * (sea_feat // 2)
                value = ocean[r, 8 * k : 8 * k + 8, at : at + 1]
                tops[q] = tops[q] + jnp.where(hit, value, 0.0)
    for q, part in enumerate(means + tops):
        sums[q] = part
    count = secs * tiles
    me = lax.axis_index("sec") * tiles + lax.axis_index("tile")
    row = sublane((count, LANES))
    row_t = row % tiles
    under = jnp.zeros((count, LANES), jnp.int32)
    for k in range(tiles):
        under = jnp.where(row_t == k, tile_map[k], under)
    under = row - row_t + under
    source[...] = (under == me).astype(f32)
    perm[...] = (lax.broadcasted_iota(jnp.int32, (count, count), 1) == under[:, 0:1]).astype(f32)


def border(
    secs, tiles, atmos, cloudy, w_in, w_out, c_in, c_out, tile_a, tile_b, sec_a, sec_b, sums,
    field, pay, xs, hid,
):
    rows, cols, feat = atmos.shape
    s = lax.axis_index("sec")
    sides = Sides(tiles, rows, feat, tile_a, tile_b)
    ends = Ends(secs, cols, feat, sums.shape[2] // (rows // 2), sec_a, sec_b)
    inside = columns_inside(tiles, (cols + 16, feat))

    def line(r):
        if 0 <= r < rows:
            core, side = atmos[r], sides.air(r)
        else:
            piece = ends.north if r < 0 else ends.south
            core = ends.air(piece, r + ASTEPS if r < 0 else r - rows)
            side = ends.air_side(piece)
        return jnp.concatenate([side, core, side], axis=0)

    at = 0
    for first in (0, rows - 2):
        lines = [line(r) for r in range(first - 2, first + 4)]
        ones = [jnp.where(inside, relax(*lines[k : k + 3], kappa_air), 0.0) for k in range(4)]
        if first == 0:
            ones[0] = jnp.where(s > 0, ones[0], 0.0)
        else:
            ones[3] = jnp.where(s < secs - 1, ones[3], 0.0)
        for k in range(2):
            two = relax(*ones[k : k + 3], kappa_air)[8 : 8 + cols]
            field[at] = two
            xs[at * cols : (at + 1) * cols, :] = two.astype(bf16)
            at += 1
    clear, cloud = physics(xs[...], w_in, w_out, c_in, c_out, hid)
    flags = cloudy[...].astype(f32)
    means = [sums[0], sums[1]]
    for at, r in enumerate((0, 1, rows - 2, rows - 1)):
        span = slice(at * cols, (at + 1) * cols)
        flag = upright(flags[r : r + 1, :])
        new = field[at] + (clear[span] + flag * cloud[span]).astype(bf16).astype(f32)
        field[at] = new
        add_row(means, new, r)
    for q, part in enumerate((0.25 * means[0], 0.25 * means[1], sums[2], sums[3])):
        total = jnp.sum(part, axis=0, keepdims=True)
        pay[:, q, :] = jnp.broadcast_to(total, (pay.shape[0], LANES))


def sea_steps(secs, tiles, rows, cols, feat, ocean, tile_a, tile_b, sec_a, sec_b, out):
    sea_rows, sea_cols, sea_feat = ocean.shape
    s = lax.axis_index("sec")
    sides = Sides(tiles, rows, feat, tile_a, tile_b)
    ends = Ends(secs, cols, feat, sea_cols, sec_a, sec_b)
    inside = columns_inside(tiles, (sea_cols + 16, sea_feat))
    state = []
    for r in range(-OSTEPS, sea_rows + OSTEPS):
        if 0 <= r < sea_rows:
            core, side = ocean[r], sides.sea(r)
        elif r < 0:
            core, side = ends.sea(ends.north, r + OSTEPS)
        else:
            core, side = ends.sea(ends.south, r - sea_rows)
        state.append(jnp.concatenate([side, core, side], axis=0))
    for step in range(OSTEPS):
        state = [relax(*state[k : k + 3], kappa_sea) for k in range(len(state) - 2)]
        depth = OSTEPS - 1 - step
        for k, new in enumerate(state):
            new = jnp.where(inside, new, 0.0)
            if k < depth:
                new = jnp.where(s > 0, new, 0.0)
            elif k >= depth + sea_rows:
                new = jnp.where(s < secs - 1, new, 0.0)
            state[k] = new
    for r in range(sea_rows):
        out[r] = state[r][8 : 8 + sea_cols]


def final(
    secs, tiles, gathered, perm, source, inner_rows, border_rows, sea,
    air_out, sea_out, back, stage, sems,
):
    rows, cols, feat = air_out.shape
    sea_rows, sea_cols, sea_feat = sea.shape
    count = secs * tiles
    me = lax.axis_index("sec") * tiles + lax.axis_index("tile")
    halves = feat // LANES
    half_cols = cols // 2
    top0, top1 = gathered[:, 2, :], gathered[:, 3, :]
    lane8, sub8 = tile_iotas()

    def pick(mask, v):
        return jnp.broadcast_to(jnp.sum(mask * v, axis=0, keepdims=True), (8, LANES))

    landing = pick(source[...], top0)
    step_rows = 4
    copies = []
    for first in range(0, rows, step_rows):
        for r2 in range(first // 2, (first + step_rows) // 2):
            for k in range(cols // 8):
                cells = slice(8 * k, 8 * k + 8)
                hit = lane8 == r2 * half_cols + 4 * k + sub8 // 2
                value = jnp.sum(jnp.where(hit, landing, 0.0), axis=1, keepdims=True)
                for r in (2 * r2, 2 * r2 + 1):
                    for h in range(halves):
                        lanes = slice(h * LANES, (h + 1) * LANES)
                        if r < 2:
                            old = border_rows[r, cells, lanes]
                        elif r >= rows - 2:
                            old = border_rows[r - rows + 4, cells, lanes]
                        else:
                            old = inner_rows[r - 2, cells, lanes]
                        flux = 0.8 * ((1.0 if h == 0 else 0.5) * value - old)
                        stage[r, cells, lanes] = old + jnp.where(lane8 == 0, 0.5 * flux, 0.0)
        copy = pltpu.make_async_copy(
            stage.at[first : first + step_rows],
            air_out.at[first : first + step_rows],
            sems.at[first // step_rows],
        )
        copy.start()
        copies.append(copy)

    air0 = jnp.dot(
        perm[...], gathered[:, 0, :], precision=HIGHEST, preferred_element_type=f32
    )
    air1 = jnp.dot(
        perm[...], gathered[:, 1, :], precision=HIGHEST, preferred_element_type=f32
    )
    state0 = top0 + 0.5 * (0.8 * (top0 - air0))
    state1 = top1 + 0.5 * (0.8 * (0.5 * top0 - air1))

    lane = lax.broadcasted_iota(jnp.int32, (count, LANES), 1)
    row = sublane((count, LANES))
    lane_c = lane % sea_cols
    first_c, last_c = lane_c == 0, lane_c == sea_cols - 1
    first_r, last_r = lane < sea_cols, lane >= LANES - sea_cols
    first_t, last_t = row % tiles == 0, row % tiles == tiles - 1
    first_s, last_s = row < tiles, row >= count - tiles

    def roll(v, shift, axis):
        return pltpu.roll(v, shift % v.shape[axis], axis)

    def step(v):
        east_t = jnp.where(last_t, 0.0, roll(v, -1, 0))
        west_t = jnp.where(first_t, 0.0, roll(v, 1, 0))
        east = jnp.where(last_c, roll(east_t, sea_cols - 1, 1), roll(v, -1, 1))
        west = jnp.where(first_c, roll(west_t, 1 - sea_cols, 1), roll(v, 1, 1))
        down, up = roll(v, -sea_cols, 1), roll(v, sea_cols, 1)
        down_s = jnp.where(last_s, 0.0, roll(down, -tiles, 0))
        up_s = jnp.where(first_s, 0.0, roll(up, tiles, 0))
        beside = jnp.where(last_r, down_s, down) + jnp.where(first_r, up_s, up) + east + west
        return v + kappa_sea * (beside - 4.0 * v)

    for _ in range(OSTEPS):
        state0, state1 = step(state0), step(state1)
    from_me = (row == me).astype(f32)
    own0, own1 = pick(from_me, state0), pick(from_me, state1)
    returned = pick(source[...], state0)
    for r in range(sea_rows):
        for k in range(sea_cols // 8):
            hit = lane8 == r * sea_cols + 8 * k + sub8
            v0 = jnp.sum(jnp.where(hit, own0, 0.0), axis=1, keepdims=True)
            v1 = jnp.sum(jnp.where(hit, own1, 0.0), axis=1, keepdims=True)
            old = sea[r, 8 * k : 8 * k + 8, :]
            new = jnp.where(lane8 == 0, v0, jnp.where(lane8 == sea_feat // 2, v1, old))
            sea_out[r, 8 * k : 8 * k + 8, :] = new
    lane_b = lax.broadcasted_iota(jnp.int32, (rows, LANES), 1)
    lines = jnp.where(
        lane_b // half_cols == sublane((rows, LANES)) // 2, jnp.tile(returned, (rows // 8, 1)), 0.0
    )
    spread = (
        sublane((LANES, cols)) % half_cols
        == lax.broadcasted_iota(jnp.int32, (LANES, cols), 1) // 2
    ).astype(f32)
    back[...] = jnp.dot(lines, spread, precision=HIGHEST, preferred_element_type=f32)
    for copy in copies:
        copy.wait()


def local(atmos, cloudy, weight_in, weight_out, cloud_in, cloud_out, ocean, tile_map):
    rows, cols, feat = atmos.shape
    sea_rows, sea_cols, sea_feat = ocean.shape
    secs, tiles = lax.axis_size("sec"), lax.axis_size("tile")
    count = secs * tiles
    halves = feat // LANES
    width = weight_in.shape[1]
    sec_even, sec_odd, tile_even, tile_odd = exchanges(secs, tiles)
    shape = jax.ShapeDtypeStruct

    def call(body, name, out_shape, in_specs, out_specs, scratch=(), flops=0, args=()):
        return pl.pallas_call(
            body,
            out_shape=out_shape,
            in_specs=in_specs,
            out_specs=out_specs,
            scratch_shapes=scratch,
            compiler_params=pltpu.CompilerParams(vmem_limit_bytes=8 * 1024 * 1024),
            cost_estimate=pl.CostEstimate(flops=flops, bytes_accessed=0, transcendentals=0),
            name=name,
        )(*args)

    out = shape((8 * (rows // 4 * halves + sea_rows // 2), LANES), bf16)
    send_a, send_b = call(
        pack_tile, "pack_tile", (out, out), [HBM] * 2, (VMEM, VMEM),
        [
            pltpu.VMEM((rows, 8, feat), f32),
            pltpu.VMEM((rows, 8, feat), f32),
            pltpu.VMEM(ocean.shape, f32),
            pltpu.SemaphoreType.DMA((3,)),
        ],
        args=(atmos, ocean),
    )
    tile_a = lax.ppermute(send_a, AXES, tile_even)
    tile_b = lax.ppermute(send_b, AXES, tile_odd)

    lines = halves * (ASTEPS * cols + 8) + OSTEPS * (sea_cols + 8)
    out = shape((lines, LANES), bf16)
    send_a, send_b = call(
        functools.partial(pack_sec, tiles), "pack_sec", (out, out), [VMEM] * 4, (VMEM, VMEM),
        args=(atmos, ocean, tile_a, tile_b),
    )
    sec_a = lax.ppermute(send_a, AXES, sec_even)
    sec_b = lax.ppermute(send_b, AXES, sec_odd)

    weights = (weight_in, weight_out, cloud_in, cloud_out)
    within = (rows - 4) * cols
    inner_rows, sums, perm, source = call(
        functools.partial(inner, secs, tiles), "inner",
        (
            shape((rows - 4, cols, feat), f32),
            shape((4, 8, LANES), f32),
            shape((count, count), f32),
            shape((count, LANES), f32),
        ),
        [SMEM] + [VMEM] * 9,
        (VMEM,) * 4,
        [pltpu.VMEM((within, feat), bf16), pltpu.VMEM((2, within, width), bf16)],
        flops=within * feat * width * 8,
        args=(tile_map, atmos, cloudy, *weights, ocean, tile_a, tile_b),
    )
    border_rows, pay = call(
        functools.partial(border, secs, tiles), "border",
        (shape((4, cols, feat), f32), shape((count, 4, LANES), f32)),
        [VMEM] * 11,
        (VMEM,) * 2,
        [pltpu.VMEM((4 * cols, feat), bf16), pltpu.VMEM((2, 4 * cols, width), bf16)],
        flops=4 * cols * feat * width * 8,
        args=(atmos, cloudy, *weights, tile_a, tile_b, sec_a, sec_b, sums),
    )
    gathered = lax.all_to_all(pay, AXES, 0, 0)
    sea = call(
        functools.partial(sea_steps, secs, tiles, rows, cols, feat), "sea_steps",
        shape(ocean.shape, f32), [VMEM] * 5, VMEM,
        flops=100 * ocean.size,
        args=(ocean, tile_a, tile_b, sec_a, sec_b),
    )
    return call(
        functools.partial(final, secs, tiles), "final",
        (shape(atmos.shape, f32), shape(ocean.shape, f32), shape((rows, cols), f32)),
        [VMEM] * 6,
        (HBM, VMEM, VMEM),
        [pltpu.VMEM(atmos.shape, f32), pltpu.SemaphoreType.DMA((rows // 4,))],
        args=(gathered, perm, source, inner_rows, border_rows, sea),
    )


def solution(mesh):
    placed = (
        P("sec", "tile", None),
        P("sec", "tile"),
        P(),
        P(),
        P(),
        P(),
        P("sec", "tile", None),
        P(),
    )
    return jax.shard_map(
        local,
        mesh=mesh,
        in_specs=placed,
        out_specs=(P("sec", "tile", None), P("sec", "tile", None), P("sec", "tile")),
        check_vma=False,
    )
```

time: 266 us -> 31.9 us (0.12); the launches traced: 262 us -> 31.5 us
  blocking collectives: 125 us -> 0 us
  starting transfers between devices: 67 us -> 11.6 us
  local copies, waits for them, and re-layouts: 35.3 us -> 3.97 us
  other arithmetic: 20.8 us -> 0 us
  Pallas kernels: 0 us -> 6.4 us
  waiting for transfers between devices: 11.8 us -> 8.79 us
    all_gather x4 -> x0, blocking collectives: 125 us -> none  [the longest x1 32 us: local(): lax.all_gather(sea[:, :, 0], 'tile', axis=1, tiled=True)]
    ppermute x24 -> x4, starting transfers between devices: 67 us -> 5.21 us  [the longest x1 3.03 us: local(): tile_a = lax.ppermute(send_a, AXES, tile_even)]
    unnamed x42 -> x18, local copies, waits for them, and re-layouts: 22.9 us -> 3.97 us
    ppermute x24 -> x4, waiting for transfers between devices: 11.8 us -> 1.81 us  [the longest x1 1.8 us: local(): tile_a = lax.ppermute(send_a, AXES, tile_even)]
    all_to_all x0 -> x1, waiting for transfers between devices: none -> 6.98 us  [local(): gathered = lax.all_to_all(pay, AXES, 0, 0)]
    add x8 -> x0, other arithmetic: 6.85 us -> none  [the longest x5 4.9 us: relax(): return inner + rate * (beside - 4.0 * inner)]
    pallas_call x0 -> x6, Pallas kernels: none -> 6.4 us  [call(): pl.pallas_call(body, out_shape=out_shape, in_specs=in_specs, out_specs=ou...]
    all_to_all x0 -> x1, starting transfers between devices: none -> 6.38 us  [local(): gathered = lax.all_to_all(pay, AXES, 0, 0)]
  transfers between devices with their start and end apart: 24 -> 5, of which waited for: 8 -> 2; matrix products, arithmetic and copies ran while one was open for 7% -> 0% of each run, Pallas kernels for 0% -> 8%
where the time goes in v2:
time: 31.9 us; the launch traced here: 31.5 us
  starting transfers between devices  11.6 us (36%)
  waiting for transfers between devices  8.79 us (28%)
  Pallas kernels  6.4 us (20%)
  local copies, waits for them, and re-layouts  3.97 us (12%)
  between operations  0.73 us (2%)
    all_to_all x1, waiting for transfers between devices, local(): gathered = lax.all_to_all(pay, AXES, 0, 0)  6.98 us
    pallas_call x6, Pallas kernels, call(): pl.pallas_call(body, out_shape=out_shape, in_specs=in_specs, out_specs=ou...  6.4 us
    all_to_all x1, starting transfers between devices, local(): gathered = lax.all_to_all(pay, AXES, 0, 0)  6.38 us
    unnamed x18, local copies, waits for them, and re-layouts  3.97 us
    ppermute x1, starting transfers between devices, local(): tile_a = lax.ppermute(send_a, AXES, tile_even)  3.03 us
    ppermute x1, starting transfers between devices, local(): sec_b = lax.ppermute(send_b, AXES, sec_odd)  2.11 us
    ppermute x1, waiting for transfers between devices, local(): tile_a = lax.ppermute(send_a, AXES, tile_even)  1.8 us
  transfers between devices with their start and end apart: 5, of which 2 were waited for; matrix products, arithmetic and copies ran while one was open for 0% of the time, Pallas kernels for 8%

profile of v2, /device:TPU:0, one launch (start us, length us, event | category | flops | bytes accessed | tf_op | source)
XLA Modules:
  0.0 31.5 jit_solution(12028209246530560058)
XLA Ops:
  0.6 0.0 copy-start
  0.6 1.0 %copy-done = f32[16,32,256]{2,1,0:T(8,128)S(1)} copy-done((f32[16,32,256]{2,1,0:T(8,128)S(1)}, f32[16,32,256]{2,1,0:T(8,128)}, u32[]{:S(2)}) %copy-start) | copy-done | bytes 524312
  1.7 0.0 copy-start.1
  1.7 0.8 %copy-done.1 = f32[8,16,128]{2,1,0:T(8,128)S(1)} copy-done((f32[8,16,128]{2,1,0:T(8,128)S(1)}, f32[8,16,128]{2,1,0:T(8,128)}, u32[]{:S(2)}) %copy-start.1) | copy-done | bytes 65560
  2.5 0.0 copy-start.3
  2.5 0.0 copy-start.4
  2.5 0.2 pack_tile.1
  2.7 3.0 %collective-permute-start = (bf16[96,128]{1,0:T(8,128)(2,1)S(1)}, bf16[96,128]{1,0:T(8,128)(2,1)S(1)}, u32[]{:S(2)}, u32[]{:S(2)}) collective-permute-start(bf16[96,128]{1,0:T(8,128)(2,1)S(1)} %get-tuple-element.13), channel_id=1, source_target_pairs={{0,1},{1,0},{2,3},{3,2},{4,5},{5,4},{6,7},{7,6},{8,9},{9,8},{10,11... | collective-permute-start | bytes 73736 | tf_op jit(solution)/shard_map/ppermute | solution.py:484
  5.7 0.0 copy-start.7
  5.7 0.0 collective-permute-start.1
  5.7 1.8 %collective-permute-done.tile_a = bf16[96,128]{1,0:T(8,128)(2,1)S(1)} collective-permute-done((bf16[96,128]{1,0:T(8,128)(2,1)S(1)}, bf16[96,128]{1,0:T(8,128)(2,1)S(1)}, u32[]{:S(2)}, u32[]{:S(2)}) %collective-permute-start) | collective-permute-done | bytes 24608 | tf_op jit(solution)/shard_map/ppermute | solution.py:484
  7.5 0.0 collective-permute-done.1.tile_b
  7.6 0.0 copy-start.8
  7.6 0.1 collective-permute-start.2
  7.7 2.1 %collective-permute-start.3 = (bf16[240,128]{1,0:T(8,128)(2,1)S(1)}, bf16[240,128]{1,0:T(8,128)(2,1)S(1)}, u32[]{:S(2)}, u32[]{:S(2)}) collective-permute-start(bf16[240,128]{1,0:T(8,128)(2,1)S(1)} %get-tuple-element.16), channel_id=1, source_target_pairs={{0,24},{1,25},{2,26},{3,27},{4,28},{5,29},{6,30},{7,31},{8,16},{9,... | collective-permute-start | bytes 184328 | tf_op jit(solution)/shard_map/ppermute | solution.py:494
  9.8 0.0 copy-done.3
  9.8 0.0 copy-done.4
  9.8 0.0 copy-done.7
  9.8 0.0 copy-done.8
  9.8 0.0 copy-start.5
  9.8 1.0 %copy-done.5 = bf16[256,1024]{1,0:T(8,128)(2,1)S(1)} copy-done((bf16[256,1024]{1,0:T(8,128)(2,1)S(1)}, bf16[256,1024]{1,0:T(8,128)(2,1)}, u32[]{:S(2)}) %copy-start.5) | copy-done | bytes 524312
  10.8 0.0 copy-start.6
  10.8 1.0 %copy-done.6 = bf16[1024,256]{1,0:T(8,128)(2,1)S(1)} copy-done((bf16[1024,256]{1,0:T(8,128)(2,1)S(1)}, bf16[1024,256]{1,0:T(8,128)(2,1)}, u32[]{:S(2)}) %copy-start.6) | copy-done | bytes 524312
  11.9 2.2 %inner.1 = (f32[12,32,256]{2,1,0:T(8,128)S(1)}, f32[4,8,128]{2,1,0:T(8,128)S(1)}, f32[32,32]{1,0:T(8,128)S(1)}, f32[32,128]{1,0:T(8,128)S(1)}) custom-call(s32[8]{0:T(128)S(1)} %copy-done.8, f32[16,32,256]{2,1,0:T(8,128)S(1)} %copy-done, s32[16,32]{1,0:T(8,128)S(1)} %copy-done.7, bf16[256,1024]{1,0:T(8,128)(2,1)S(1)} %copy-done.3, ...), custom_call_target="tpu_custom_call" | custom-call | flops 805306368 | tf_op jit(solution)/shard_map/inner/pallas_call | solution.py:462
  14.1 0.0 collective-permute-done.2.sec_a
  14.1 0.0 collective-permute-done.3.sec_b
  14.1 1.5 %border.1 = (f32[4,32,256]{2,1,0:T(8,128)S(1)}, f32[32,4,128]{2,1,0:T(4,128)}) custom-call(f32[16,32,256]{2,1,0:T(8,128)S(1)} %copy-done, s32[16,32]{1,0:T(8,128)S(1)} %copy-done.7, bf16[256,1024]{1,0:T(8,128)(2,1)S(1)} %copy-done.3, bf16[1024,256]{1,0:T(8,128)(2,1)S(1)} %copy-done.4, bf16[256,1024]{1,0:T(8,128)(2,1)S(1)} %copy-done.5, ...), custom_call_target="tpu_custom_call" | custom-call | flops 268435456 | tf_op jit(solution)/shard_map/border/pallas_call | solution.py:462
  15.6 6.4 %all-to-all-start = ((f32[32,4,128]{2,1,0:T(4,128)}), f32[32,4,128]{2,1,0:T(4,128)S(1)}, u32[]{:S(2)}, u32[]{:S(2)}) async-start(f32[32,4,128]{2,1,0:T(4,128)} %get-tuple-element.18), calls=%async_computation | async-start | bytes 131072 | tf_op jit(solution)/shard_map/all_to_all | solution.py:521
  22.0 0.0 copy-done.2
  22.0 0.3 sea_steps.1.sea
  22.3 7.0 %all-to-all-done.gathered = f32[32,4,128]{2,1,0:T(4,128)S(1)} async-done(((f32[32,4,128]{2,1,0:T(4,128)}), f32[32,4,128]{2,1,0:T(4,128)S(1)}, u32[]{:S(2)}, u32[]{:S(2)}) %all-to-all-start) | async-done | bytes 65568 | tf_op jit(solution)/shard_map/all_to_all | solution.py:521
  29.2 2.2 %final.1 = (f32[16,32,256]{2,1,0:T(8,128)}, f32[8,16,128]{2,1,0:T(8,128)}, f32[16,32]{1,0:T(8,128)}) custom-call(f32[32,4,128]{2,1,0:T(4,128)S(1)} %all-to-all-done.gathered, f32[32,32]{1,0:T(8,128)S(1)} %get-tuple-element.19.perm, f32[32,128]{1,0:T(8,128)S(1)} %get-tuple-element.20.source, f32[12,32,256]{2,1,0:T(8,128)S(1)} %get-tuple-element.21.inner_rows, ...), custom_call_target="tpu_custom_call" | custom-call | tf_op jit(solution)/shard_map/final/pallas_call | solution.py:462
  (2 shorter events, 0.0 us)
Async XLA Ops:
  0.6 1.0 %copy-start = (f32[16,32,256]{2,1,0:T(8,128)S(1)}, f32[16,32,256]{2,1,0:T(8,128)}, u32[]{:S(2)}) copy-start(f32[16,32,256]{2,1,0:T(8,128)} %atmos.7) | copy-start | bytes 1572868
  1.7 0.8 %copy-start.1 = (f32[8,16,128]{2,1,0:T(8,128)S(1)}, f32[8,16,128]{2,1,0:T(8,128)}, u32[]{:S(2)}) copy-start(f32[8,16,128]{2,1,0:T(8,128)} %ocean.7) | copy-start | bytes 196612
  2.5 7.3 %copy-start.3 = (bf16[256,1024]{1,0:T(8,128)(2,1)S(1)}, bf16[256,1024]{1,0:T(8,128)(2,1)}, u32[]{:S(2)}) copy-start(bf16[256,1024]{1,0:T(8,128)(2,1)} %w_in.3) | copy-start | bytes 1572868
  2.5 7.3 %copy-start.4 = (bf16[1024,256]{1,0:T(8,128)(2,1)S(1)}, bf16[1024,256]{1,0:T(8,128)(2,1)}, u32[]{:S(2)}) copy-start(bf16[1024,256]{1,0:T(8,128)(2,1)} %w_out.3) | copy-start | bytes 1572868
  2.7 4.8 %collective-permute-start = (bf16[96,128]{1,0:T(8,128)(2,1)S(1)}, bf16[96,128]{1,0:T(8,128)(2,1)S(1)}, u32[]{:S(2)}, u32[]{:S(2)}) collective-permute-start(bf16[96,128]{1,0:T(8,128)(2,1)S(1)} %get-tuple-element.13), channel_id=1, source_target_pairs={{0,1},{1,0},{2,3},{3,2},{4,5},{5,4},{6,7},{7,6},{8,9},{9,8},{10,11... | collective-permute-start | bytes 73736 | tf_op jit(solution)/shard_map/ppermute | solution.py:484
  5.7 4.1 %copy-start.7 = (s32[16,32]{1,0:T(8,128)S(1)}, s32[16,32]{1,0:T(8,128)}, u32[]{:S(2)}) copy-start(s32[16,32]{1,0:T(8,128)} %cloudy.3) | copy-start | bytes 6148
  5.7 1.8 %collective-permute-start.1 = (bf16[96,128]{1,0:T(8,128)(2,1)S(1)}, bf16[96,128]{1,0:T(8,128)(2,1)S(1)}, u32[]{:S(2)}, u32[]{:S(2)}) collective-permute-start(bf16[96,128]{1,0:T(8,128)(2,1)S(1)} %get-tuple-element.14), channel_id=1, source_target_pairs={{0,8},{1,2},{2,1},{3,4},{4,3},{5,6},{6,5},{7,15},{8,0},{9,10},{10,... | collective-permute-start | bytes 73736 | tf_op jit(solution)/shard_map/ppermute | solution.py:485
  7.6 2.2 %copy-start.8 = (s32[8]{0:T(128)S(1)}, s32[8]{0:T(128)}, u32[]{:S(2)}) copy-start(s32[8]{0:T(128)} %tile_map.1) | copy-start | bytes 100
  7.6 6.5 %collective-permute-start.2 = (bf16[240,128]{1,0:T(8,128)(2,1)S(1)}, bf16[240,128]{1,0:T(8,128)(2,1)S(1)}, u32[]{:S(2)}, u32[]{:S(2)}) collective-permute-start(bf16[240,128]{1,0:T(8,128)(2,1)S(1)} %get-tuple-element.15), channel_id=1, source_target_pairs={{0,8},{1,9},{2,10},{3,11},{4,12},{5,13},{6,14},{7,15},{8,0},{9,1},... | collective-permute-start | bytes 184328 | tf_op jit(solution)/shard_map/ppermute | solution.py:493
  7.7 6.4 %collective-permute-start.3 = (bf16[240,128]{1,0:T(8,128)(2,1)S(1)}, bf16[240,128]{1,0:T(8,128)(2,1)S(1)}, u32[]{:S(2)}, u32[]{:S(2)}) collective-permute-start(bf16[240,128]{1,0:T(8,128)(2,1)S(1)} %get-tuple-element.16), channel_id=1, source_target_pairs={{0,24},{1,25},{2,26},{3,27},{4,28},{5,29},{6,30},{7,31},{8,16},{9,... | collective-permute-start | bytes 184328 | tf_op jit(solution)/shard_map/ppermute | solution.py:494
  9.8 1.0 %copy-start.5 = (bf16[256,1024]{1,0:T(8,128)(2,1)S(1)}, bf16[256,1024]{1,0:T(8,128)(2,1)}, u32[]{:S(2)}) copy-start(bf16[256,1024]{1,0:T(8,128)(2,1)} %c_in.3) | copy-start | bytes 1572868
  10.8 1.0 %copy-start.6 = (bf16[1024,256]{1,0:T(8,128)(2,1)S(1)}, bf16[1024,256]{1,0:T(8,128)(2,1)}, u32[]{:S(2)}) copy-start(bf16[1024,256]{1,0:T(8,128)(2,1)} %c_out.3) | copy-start | bytes 1572868
  15.6 6.4 %copy-start.2 = (f32[8,16,128]{2,1,0:T(8,128)S(1)}, f32[8,16,128]{2,1,0:T(8,128)}, u32[]{:S(2)}) copy-start(f32[8,16,128]{2,1,0:T(8,128)} %ocean.7) | copy-start | bytes 196612
  15.6 13.7 %all-to-all-start = ((f32[32,4,128]{2,1,0:T(4,128)}), f32[32,4,128]{2,1,0:T(4,128)S(1)}, u32[]{:S(2)}, u32[]{:S(2)}) async-start(f32[32,4,128]{2,1,0:T(4,128)} %get-tuple-element.18), calls=%async_computation | async-start | bytes 131072 | tf_op jit(solution)/shard_map/all_to_all | solution.py:521

commit v3 on v2

--- a/solution.py
+++ b/solution.py
@@ -16,9 +16,7 @@
 
 f32 = jnp.float32
 bf16 = jnp.bfloat16
-HIGHEST = lax.Precision.HIGHEST
 VMEM = pl.BlockSpec(memory_space=pltpu.VMEM)
-SMEM = pl.BlockSpec(memory_space=pltpu.SMEM)
 HBM = pl.BlockSpec(memory_space=pltpu.HBM)
 AXES = ("sec", "tile")
 
@@ -221,8 +219,10 @@
 
 def inner(
     secs, tiles, tile_map, atmos, cloudy, w_in, w_out, c_in, c_out, ocean, tile_a, tile_b,
-    field, sums, perm, source, xs, hid,
+    field, sums, perm, source, spots, cells, spread, xs, hid, place, place_sem,
 ):
+    map_copy = pltpu.make_async_copy(tile_map, place, place_sem)
+    map_copy.start()
     rows, cols, feat = atmos.shape
     sea_rows, sea_cols, sea_feat = ocean.shape
     sides = Sides(tiles, rows, feat, tile_a, tile_b)
@@ -260,20 +260,30 @@
                 tops[q] = tops[q] + jnp.where(hit, value, 0.0)
     for q, part in enumerate(means + tops):
         sums[q] = part
+    half_cols = cols // 2
+    cell = sublane(spots.shape)
+    at = lax.broadcasted_iota(jnp.int32, spots.shape, 1) % LANES
+    spots[...] = (at == cell // cols * half_cols + cell % cols // 2).astype(f32).astype(bf16)
+    at = lax.broadcasted_iota(jnp.int32, cells.shape, 1) % LANES
+    cells[...] = (at == sublane(cells.shape)).astype(f32).astype(bf16)
+    at = lax.broadcasted_iota(jnp.int32, spread.shape, 1) // 2
+    spread[...] = (at == sublane(spread.shape) % half_cols).astype(f32).astype(bf16)
     count = secs * tiles
     me = lax.axis_index("sec") * tiles + lax.axis_index("tile")
     row = sublane((count, LANES))
     row_t = row % tiles
     under = jnp.zeros((count, LANES), jnp.int32)
+    map_copy.wait()
     for k in range(tiles):
-        under = jnp.where(row_t == k, tile_map[k], under)
+        under = jnp.where(row_t == k, place[k], under)
     under = row - row_t + under
     source[...] = (under == me).astype(f32)
-    perm[...] = (lax.broadcasted_iota(jnp.int32, (count, count), 1) == under[:, 0:1]).astype(f32)
+    at = lax.broadcasted_iota(jnp.int32, perm.shape, 1) % count
+    perm[...] = (at == under[:, 0:1]).astype(f32).astype(bf16)
 
 
 def border(
-    secs, tiles, atmos, cloudy, w_in, w_out, c_in, c_out, tile_a, tile_b, sec_a, sec_b, sums,
+    secs, tiles, atmos, cloudy, w_in, w_out, c_in, c_out, tile_a, tile_b, sec_b, sec_a, sums,
     field, pay, xs, hid,
 ):
     rows, cols, feat = atmos.shape
@@ -318,7 +328,7 @@
         pay[:, q, :] = jnp.broadcast_to(total, (pay.shape[0], LANES))
 
 
-def sea_steps(secs, tiles, rows, cols, feat, ocean, tile_a, tile_b, sec_a, sec_b, out):
+def sea_steps(secs, tiles, rows, cols, feat, ocean, tile_a, tile_b, sec_b, sec_a, out):
     sea_rows, sea_cols, sea_feat = ocean.shape
     s = lax.axis_index("sec")
     sides = Sides(tiles, rows, feat, tile_a, tile_b)
@@ -347,9 +357,30 @@
         out[r] = state[r][8 : 8 + sea_cols]
 
 
+def fetch(*refs):
+    count = (len(refs) - 2) // 2
+    sems = refs[-1]
+    copies = [
+        pltpu.make_async_copy(refs[1 + k], refs[1 + count + k], sems.at[k]) for k in range(count)
+    ]
+    for copy in copies:
+        copy.start()
+    for copy in copies:
+        copy.wait()
+
+
+def thirds(v, axis):
+    high = v.astype(bf16)
+    rest = v - high.astype(f32)
+    middle = rest.astype(bf16)
+    low = (rest - middle.astype(f32)).astype(bf16)
+    return jnp.concatenate([high, middle, low], axis=axis)
+
+
 def final(
-    secs, tiles, gathered, perm, source, inner_rows, border_rows, sea,
-    air_out, sea_out, back, stage, sems,
+    secs, tiles, gathered, perm, source, spots, cells, spread, inner_rows, border_rows,
+    ocean, tile_a, tile_b, sec_b, sec_a,
+    air_out, sea_out, back, stage, sea, sea_stage, back_stage, sems,
 ):
     rows, cols, feat = air_out.shape
     sea_rows, sea_cols, sea_feat = sea.shape
@@ -358,48 +389,57 @@
     halves = feat // LANES
     half_cols = cols // 2
     top0, top1 = gathered[:, 2, :], gathered[:, 3, :]
-    lane8, sub8 = tile_iotas()
+    mine = source[...]
 
     def pick(mask, v):
-        return jnp.broadcast_to(jnp.sum(mask * v, axis=0, keepdims=True), (8, LANES))
-
-    landing = pick(source[...], top0)
+        return jnp.sum(mask * v, axis=0, keepdims=True)
+
+    def upright_at(line, *lanes):
+        sub = sublane((LANES, 3 * LANES))
+        out = jnp.zeros((LANES, 3 * LANES), f32)
+        for v, at in zip(line, lanes):
+            out = jnp.where(sub == at, jnp.broadcast_to(thirds(v, 1).astype(f32), out.shape), out)
+        return out.astype(bf16)
+
+    def against(one_hot, values):
+        return lax.dot_general(
+            one_hot, values, (((1,), (1,)), ((), ())), preferred_element_type=f32
+        )
+
+    landing = pick(mine, top0)
+    patch = against(spots[...], upright_at([landing], 0))
+
+    air = thirds(jnp.concatenate([gathered[:, 0, :], gathered[:, 1, :]], axis=1), 0)
+    air = jnp.dot(perm[...], air, preferred_element_type=f32)
+    state0 = top0 + 0.5 * (0.8 * (top0 - air[:, :LANES]))
+    state1 = top1 + 0.5 * (0.8 * (0.5 * top0 - air[:, LANES:]))
+
+    first_lane = lax.broadcasted_iota(jnp.int32, (cols, LANES), 1) == 0
     step_rows = 4
     copies = []
     for first in range(0, rows, step_rows):
-        for r2 in range(first // 2, (first + step_rows) // 2):
-            for k in range(cols // 8):
-                cells = slice(8 * k, 8 * k + 8)
-                hit = lane8 == r2 * half_cols + 4 * k + sub8 // 2
-                value = jnp.sum(jnp.where(hit, landing, 0.0), axis=1, keepdims=True)
-                for r in (2 * r2, 2 * r2 + 1):
-                    for h in range(halves):
-                        lanes = slice(h * LANES, (h + 1) * LANES)
-                        if r < 2:
-                            old = border_rows[r, cells, lanes]
-                        elif r >= rows - 2:
-                            old = border_rows[r - rows + 4, cells, lanes]
-                        else:
-                            old = inner_rows[r - 2, cells, lanes]
-                        flux = 0.8 * ((1.0 if h == 0 else 0.5) * value - old)
-                        stage[r, cells, lanes] = old + jnp.where(lane8 == 0, 0.5 * flux, 0.0)
-        copy = pltpu.make_async_copy(
-            stage.at[first : first + step_rows],
-            air_out.at[first : first + step_rows],
-            sems.at[first // step_rows],
+        for r in range(first, first + step_rows):
+            value = patch[(r // 2) * cols : (r // 2 + 1) * cols]
+            for h in range(halves):
+                lanes = slice(h * LANES, (h + 1) * LANES)
+                if r < 2:
+                    old = border_rows[r, :, lanes]
+                elif r >= rows - 2:
+                    old = border_rows[r - rows + 4, :, lanes]
+                else:
+                    old = inner_rows[r - 2, :, lanes]
+                flux = 0.8 * ((1.0 if h == 0 else 0.5) * value - old)
+                stage[r, :, lanes] = old + jnp.where(first_lane, 0.5 * flux, 0.0)
+        copies.append(
+            pltpu.make_async_copy(
+                stage.at[first : first + step_rows],
+                air_out.at[first : first + step_rows],
+                sems.at[first // step_rows],
+            )
         )
-        copy.start()
-        copies.append(copy)
-
-    air0 = jnp.dot(
-        perm[...], gathered[:, 0, :], precision=HIGHEST, preferred_element_type=f32
-    )
-    air1 = jnp.dot(
-        perm[...], gathered[:, 1, :], precision=HIGHEST, preferred_element_type=f32
-    )
-    state0 = top0 + 0.5 * (0.8 * (top0 - air0))
-    state1 = top1 + 0.5 * (0.8 * (0.5 * top0 - air1))
-
+        copies[-1].start()
+
+    sea_steps(secs, tiles, rows, cols, feat, ocean, tile_a, tile_b, sec_b, sec_a, sea)
     lane = lax.broadcasted_iota(jnp.int32, (count, LANES), 1)
     row = sublane((count, LANES))
     lane_c = lane % sea_cols
@@ -425,25 +465,22 @@
     for _ in range(OSTEPS):
         state0, state1 = step(state0), step(state1)
     from_me = (row == me).astype(f32)
-    own0, own1 = pick(from_me, state0), pick(from_me, state1)
-    returned = pick(source[...], state0)
+    own = upright_at([pick(from_me, state0), pick(from_me, state1)], 0, sea_feat // 2)
+    own = against(cells[...], own)
+    lane_s = lax.broadcasted_iota(jnp.int32, (sea_cols, sea_feat), 1)
+    surface = jnp.logical_or(lane_s == 0, lane_s == sea_feat // 2)
     for r in range(sea_rows):
-        for k in range(sea_cols // 8):
-            hit = lane8 == r * sea_cols + 8 * k + sub8
-            v0 = jnp.sum(jnp.where(hit, own0, 0.0), axis=1, keepdims=True)
-            v1 = jnp.sum(jnp.where(hit, own1, 0.0), axis=1, keepdims=True)
-            old = sea[r, 8 * k : 8 * k + 8, :]
-            new = jnp.where(lane8 == 0, v0, jnp.where(lane8 == sea_feat // 2, v1, old))
-            sea_out[r, 8 * k : 8 * k + 8, :] = new
+        new = own[r * sea_cols : (r + 1) * sea_cols]
+        sea_stage[r] = jnp.where(surface, new, sea[r])
+    copies.append(pltpu.make_async_copy(sea_stage, sea_out, sems.at[rows // step_rows]))
+    copies[-1].start()
+
+    returned = jnp.broadcast_to(pick(mine, state0), (rows, LANES))
     lane_b = lax.broadcasted_iota(jnp.int32, (rows, LANES), 1)
-    lines = jnp.where(
-        lane_b // half_cols == sublane((rows, LANES)) // 2, jnp.tile(returned, (rows // 8, 1)), 0.0
-    )
-    spread = (
-        sublane((LANES, cols)) % half_cols
-        == lax.broadcasted_iota(jnp.int32, (LANES, cols), 1) // 2
-    ).astype(f32)
-    back[...] = jnp.dot(lines, spread, precision=HIGHEST, preferred_element_type=f32)
+    lines = jnp.where(lane_b // half_cols == sublane((rows, LANES)) // 2, returned, 0.0)
+    back_stage[...] = jnp.dot(thirds(lines, 1), spread[...], preferred_element_type=f32)
+    copies.append(pltpu.make_async_copy(back_stage, back, sems.at[rows // step_rows + 1]))
+    copies[-1].start()
     for copy in copies:
         copy.wait()
 
@@ -470,6 +507,9 @@
             name=name,
         )(*args)
 
+    def hbm(a):
+        return pltpu.with_memory_space_constraint(a, pltpu.HBM)
+
     out = shape((8 * (rows // 4 * halves + sea_rows // 2), LANES), bf16)
     send_a, send_b = call(
         pack_tile, "pack_tile", (out, out), [HBM] * 2, (VMEM, VMEM),
@@ -479,10 +519,20 @@
             pltpu.VMEM(ocean.shape, f32),
             pltpu.SemaphoreType.DMA((3,)),
         ],
-        args=(atmos, ocean),
+        args=(hbm(atmos), hbm(ocean)),
     )
     tile_a = lax.ppermute(send_a, AXES, tile_even)
     tile_b = lax.ppermute(send_b, AXES, tile_odd)
+    wanted = (weight_in, cloud_in, weight_out, cloud_out, atmos, ocean, cloudy)
+    weight_in, cloud_in, weight_out, cloud_out, atmos, ocean, cloudy = call(
+        fetch, "fetch",
+        tuple(pltpu.VMEM(a.shape, a.dtype) for a in wanted),
+        [pl.BlockSpec(memory_space=pl.ANY)] + [HBM] * len(wanted),
+        (VMEM,) * len(wanted),
+        [pltpu.SemaphoreType.DMA((len(wanted),))],
+        flops=1 << 30,
+        args=(send_a, *(hbm(a) for a in wanted)),
+    )
 
     lines = halves * (ASTEPS * cols + 8) + OSTEPS * (sea_cols + 8)
     out = shape((lines, LANES), bf16)
@@ -495,19 +545,27 @@
 
     weights = (weight_in, weight_out, cloud_in, cloud_out)
     within = (rows - 4) * cols
-    inner_rows, sums, perm, source = call(
+    inner_rows, sums, *plan = call(
         functools.partial(inner, secs, tiles), "inner",
         (
             shape((rows - 4, cols, feat), f32),
             shape((4, 8, LANES), f32),
-            shape((count, count), f32),
+            shape((count, 3 * count), bf16),
             shape((count, LANES), f32),
+            shape((rows // 2 * cols, 3 * LANES), bf16),
+            shape((LANES, 3 * LANES), bf16),
+            shape((3 * LANES, cols), bf16),
         ),
-        [SMEM] + [VMEM] * 9,
-        (VMEM,) * 4,
-        [pltpu.VMEM((within, feat), bf16), pltpu.VMEM((2, within, width), bf16)],
+        [HBM] + [VMEM] * 9,
+        (VMEM,) * 7,
+        [
+            pltpu.VMEM((within, feat), bf16),
+            pltpu.VMEM((2, within, width), bf16),
+            pltpu.SMEM(tile_map.shape, jnp.int32),
+            pltpu.SemaphoreType.DMA,
+        ],
         flops=within * feat * width * 8,
-        args=(tile_map, atmos, cloudy, *weights, ocean, tile_a, tile_b),
+        args=(hbm(tile_map), atmos, cloudy, *weights, ocean, tile_a, tile_b),
     )
     border_rows, pay = call(
         functools.partial(border, secs, tiles), "border",
@@ -516,22 +574,22 @@
         (VMEM,) * 2,
         [pltpu.VMEM((4 * cols, feat), bf16), pltpu.VMEM((2, 4 * cols, width), bf16)],
         flops=4 * cols * feat * width * 8,
-        args=(atmos, cloudy, *weights, tile_a, tile_b, sec_a, sec_b, sums),
+        args=(atmos, cloudy, *weights, tile_a, tile_b, sec_b, sec_a, sums),
     )
     gathered = lax.all_to_all(pay, AXES, 0, 0)
-    sea = call(
-        functools.partial(sea_steps, secs, tiles, rows, cols, feat), "sea_steps",
-        shape(ocean.shape, f32), [VMEM] * 5, VMEM,
-        flops=100 * ocean.size,
-        args=(ocean, tile_a, tile_b, sec_a, sec_b),
-    )
     return call(
         functools.partial(final, secs, tiles), "final",
         (shape(atmos.shape, f32), shape(ocean.shape, f32), shape((rows, cols), f32)),
-        [VMEM] * 6,
-        (HBM, VMEM, VMEM),
-        [pltpu.VMEM(atmos.shape, f32), pltpu.SemaphoreType.DMA((rows // 4,))],
-        args=(gathered, perm, source, inner_rows, border_rows, sea),
+        [VMEM] * 13,
+        (HBM,) * 3,
+        [
+            pltpu.VMEM(atmos.shape, f32),
+            pltpu.VMEM(ocean.shape, f32),
+            pltpu.VMEM(ocean.shape, f32),
+            pltpu.VMEM((rows, cols), f32),
+            pltpu.SemaphoreType.DMA((rows // 4 + 2,)),
+        ],
+        args=(gathered, *plan, inner_rows, border_rows, ocean, tile_a, tile_b, sec_b, sec_a),
     )
 
 

time: 31.9 us -> 27 us (0.85)
  blocking collectives: 0 us -> 11.8 us
  waiting for transfers between devices: 8.79 us -> 1.03 us
  starting transfers between devices: 11.6 us -> 6.22 us
  local copies, waits for them, and re-layouts: 3.97 us -> 0 us
  Pallas kernels: 6.4 us -> 7.03 us
    all_to_all x0 -> x1, blocking collectives: none -> 11.8 us  [local(): gathered = lax.all_to_all(pay, AXES, 0, 0)]
    all_to_all x1 -> x0, waiting for transfers between devices: 6.98 us -> none  [local(): gathered = lax.all_to_all(pay, AXES, 0, 0)]
    all_to_all x1 -> x0, starting transfers between devices: 6.38 us -> none  [local(): gathered = lax.all_to_all(pay, AXES, 0, 0)]
    unnamed x18 -> x0, local copies, waits for them, and re-layouts: 3.97 us -> none
    ppermute x1, waiting for transfers between devices: 1.8 us -> 0.05 us  [local(): tile_a = lax.ppermute(send_a, AXES, tile_even)]
    ppermute x1, starting transfers between devices: 2.11 us -> 0.4 us  [local(): sec_b = lax.ppermute(send_b, AXES, sec_odd)]
    ppermute x1, starting transfers between devices: 0.07 us -> 1.27 us  [local(): sec_a = lax.ppermute(send_a, AXES, sec_even)]
    ppermute x1, starting transfers between devices: 3.03 us -> 4.03 us  [local(): tile_a = lax.ppermute(send_a, AXES, tile_even)]
  transfers between devices with their start and end apart: 5 -> 4, of which waited for: 2 -> 1; matrix products, arithmetic and copies ran while one was open for 0% -> 0% of each run, Pallas kernels for 8% -> 13%
where the time goes in v3:
time: 27 us; the launch traced here: 26.8 us
  blocking collectives  11.8 us (44%)
  Pallas kernels  7.03 us (26%)
  starting transfers between devices  6.22 us (23%)
  waiting for transfers between devices  1.03 us (4%)
  between operations  0.68 us (3%)
    all_to_all x1, blocking collectives, local(): gathered = lax.all_to_all(pay, AXES, 0, 0)  11.8 us
    pallas_call x6, Pallas kernels, call(): pl.pallas_call(body, out_shape=out_shape, in_specs=in_specs, out_specs=ou...  7.03 us
    ppermute x1, starting transfers between devices, local(): tile_a = lax.ppermute(send_a, AXES, tile_even)  4.03 us
    ppermute x1, starting transfers between devices, local(): sec_a = lax.ppermute(send_a, AXES, sec_even)  1.27 us
    ppermute x1, waiting for transfers between devices, local(): sec_b = lax.ppermute(send_b, AXES, sec_odd)  0.98 us
  transfers between devices with their start and end apart: 4, of which 1 were waited for; matrix products, arithmetic and copies ran while one was open for 0% of the time, Pallas kernels for 13%

profile of v3, /device:TPU:0, one launch (start us, length us, event | category | flops | bytes accessed | tf_op | source)
XLA Modules:
  0.0 26.8 jit_solution(6911155101412466896)
XLA Ops:
  0.6 1.0 %pack_tile.1 = (bf16[96,128]{1,0:T(8,128)(2,1)S(1)}, bf16[96,128]{1,0:T(8,128)(2,1)S(1)}) custom-call(f32[16,32,256]{2,1,0:T(8,128)} %refs_5_.1, f32[8,16,128]{2,1,0:T(8,128)} %refs_6_.1), custom_call_target="tpu_custom_call" | custom-call | tf_op jit(solution)/shard_map/pack_tile/pallas_call | solution.py:499
  1.7 0.5 %collective-permute-start.1 = (bf16[96,128]{1,0:T(8,128)(2,1)S(1)}, bf16[96,128]{1,0:T(8,128)(2,1)S(1)}, u32[]{:S(2)}, u32[]{:S(2)}) collective-permute-start(bf16[96,128]{1,0:T(8,128)(2,1)S(1)} %get-tuple-element.30), channel_id=1, source_target_pairs={{0,8},{1,2},{2,1},{3,4},{4,3},{5,6},{6,5},{7,15},{8,0},{9,10},{10,... | collective-permute-start | bytes 73736 | tf_op jit(solution)/shard_map/ppermute | solution.py:525
  2.2 4.0 %collective-permute-start = (bf16[96,128]{1,0:T(8,128)(2,1)S(1)}, bf16[96,128]{1,0:T(8,128)(2,1)S(1)}, u32[]{:S(2)}, u32[]{:S(2)}) collective-permute-start(bf16[96,128]{1,0:T(8,128)(2,1)S(1)} %get-tuple-element.23.refs_0_), channel_id=1, source_target_pairs={{0,1},{1,0},{2,3},{3,2},{4,5},{5,4},{6,7},{7,6},{8,9},{9,8},{10,11... | collective-permute-start | bytes 73736 | tf_op jit(solution)/shard_map/ppermute | solution.py:524
  6.2 1.7 %fetch.1 = (bf16[256,1024]{1,0:T(8,128)(2,1)S(1)}, bf16[256,1024]{1,0:T(8,128)(2,1)S(1)}, bf16[1024,256]{1,0:T(8,128)(2,1)S(1)}, bf16[1024,256]{1,0:T(8,128)(2,1...) custom-call(bf16[96,128]{1,0:T(8,128)(2,1)S(1)} %get-tuple-element.23.refs_0_, ...), custom_call_target="tpu_custom_call" | custom-call | flops 1073741824 | tf_op jit(solution)/shard_map/fetch/pallas_call | solution.py:499
  8.0 0.0 collective-permute-done.1.tile_b
  8.0 0.0 collective-permute-done.tile_a
  8.1 0.4 %collective-permute-start.2 = (bf16[240,128]{1,0:T(8,128)(2,1)S(1)}, bf16[240,128]{1,0:T(8,128)(2,1)S(1)}, u32[]{:S(2)}, u32[]{:S(2)}) collective-permute-start(bf16[240,128]{1,0:T(8,128)(2,1)S(1)} %get-tuple-element.32), channel_id=1, source_target_pairs={{0,24},{1,25},{2,26},{3,27},{4,28},{5,29},{6,30},{7,31},{8,16},{9,... | collective-permute-start | bytes 184328 | tf_op jit(solution)/shard_map/ppermute | solution.py:544
  8.5 1.3 %collective-permute-start.3 = (bf16[240,128]{1,0:T(8,128)(2,1)S(1)}, bf16[240,128]{1,0:T(8,128)(2,1)S(1)}, u32[]{:S(2)}, u32[]{:S(2)}) collective-permute-start(bf16[240,128]{1,0:T(8,128)(2,1)S(1)} %get-tuple-element.33), channel_id=1, source_target_pairs={{0,8},{1,9},{2,10},{3,11},{4,12},{5,13},{6,14},{7,15},{8,0},{9,1},... | collective-permute-start | bytes 184328 | tf_op jit(solution)/shard_map/ppermute | solution.py:543
  9.7 1.7 %inner.1 = (f32[12,32,256]{2,1,0:T(8,128)S(1)}, f32[4,8,128]{2,1,0:T(8,128)S(1)}, bf16[32,96]{1,0:T(8,128)(2,1)S(1)}, f32[32,128]{1,0:T(8,128)S(1)}, bf16[256,38...) custom-call(s32[8]{0:T(128)} %tile_map.1, ...), custom_call_target="tpu_custom_call" | custom-call | flops 805306368 | tf_op jit(solution)/shard_map/inner/pallas_call | solution.py:499
  11.4 1.0 %collective-permute-done.2.sec_b = bf16[240,128]{1,0:T(8,128)(2,1)S(1)} collective-permute-done((bf16[240,128]{1,0:T(8,128)(2,1)S(1)}, bf16[240,128]{1,0:T(8,128)(2,1)S(1)}, u32[]{:S(2)}, u32[]{:S(2)}) %collective-permute-start.2) | collective-permute-done | bytes 61472 | tf_op jit(solution)/shard_map/ppermute | solution.py:544
  12.4 0.0 collective-permute-done.3.sec_a
  12.4 0.8 %border.1 = (f32[4,32,256]{2,1,0:T(8,128)S(1)}, f32[32,4,128]{2,1,0:T(4,128)S(1)}) custom-call(f32[16,32,256]{2,1,0:T(8,128)S(1)} %get-tuple-element.24.atmos, s32[16,32]{1,0:T(8,128)S(1)} %get-tuple-element.25.cloudy, bf16[256,1024]{1,0:T(8,128)(2,1)S(1)} %get-tuple-element.26.w_in, bf16[1024,256]{1,0:T(8,128)(2,1)S(1)} %get-tuple-element.27.w_out, ...), custom_call_target="tpu_custom_call" | custom-call | flops 268435456 | tf_op jit(solution)/shard_map/border/pallas_call | solution.py:499
  13.2 11.8 %all_to_all.5.gathered = f32[32,4,128]{2,1,0:T(4,128)S(1)} all-to-all(f32[32,4,128]{2,1,0:T(4,128)S(1)} %get-tuple-element.35), channel_id=1, replica_groups=mesh['sec'=4,'tile'=8] {'sec','tile'}, dimensions={0} | all-to-all | bytes 131072 | tf_op jit(solution)/shard_map/all_to_all | solution.py:579
  25.0 1.8 %final.1 = (f32[16,32,256]{2,1,0:T(8,128)}, f32[8,16,128]{2,1,0:T(8,128)}, f32[16,32]{1,0:T(8,128)}) custom-call(f32[32,4,128]{2,1,0:T(4,128)S(1)} %all_to_all.5.gathered, bf16[32,96]{1,0:T(8,128)(2,1)S(1)} %get-tuple-element.36.perm, f32[32,128]{1,0:T(8,128)S(1)} %get-tuple-element.37.source, bf16[256,384]{1,0:T(8,128)(2,1)S(1)} %get-tuple-element.38.spots, ...), custom_call_target="tpu_custom_call" | custom-call | tf_op jit(solution)/shard_map/final/pallas_call | solution.py:499
  (1 shorter events, 0.0 us)
Async XLA Ops:
  1.7 6.3 %collective-permute-start.1 = (bf16[96,128]{1,0:T(8,128)(2,1)S(1)}, bf16[96,128]{1,0:T(8,128)(2,1)S(1)}, u32[]{:S(2)}, u32[]{:S(2)}) collective-permute-start(bf16[96,128]{1,0:T(8,128)(2,1)S(1)} %get-tuple-element.30), channel_id=1, source_target_pairs={{0,8},{1,2},{2,1},{3,4},{4,3},{5,6},{6,5},{7,15},{8,0},{9,10},{10,... | collective-permute-start | bytes 73736 | tf_op jit(solution)/shard_map/ppermute | solution.py:525
  2.2 5.8 %collective-permute-start = (bf16[96,128]{1,0:T(8,128)(2,1)S(1)}, bf16[96,128]{1,0:T(8,128)(2,1)S(1)}, u32[]{:S(2)}, u32[]{:S(2)}) collective-permute-start(bf16[96,128]{1,0:T(8,128)(2,1)S(1)} %get-tuple-element.23.refs_0_), channel_id=1, source_target_pairs={{0,1},{1,0},{2,3},{3,2},{4,5},{5,4},{6,7},{7,6},{8,9},{9,8},{10,11... | collective-permute-start | bytes 73736 | tf_op jit(solution)/shard_map/ppermute | solution.py:524
  8.1 4.3 %collective-permute-start.2 = (bf16[240,128]{1,0:T(8,128)(2,1)S(1)}, bf16[240,128]{1,0:T(8,128)(2,1)S(1)}, u32[]{:S(2)}, u32[]{:S(2)}) collective-permute-start(bf16[240,128]{1,0:T(8,128)(2,1)S(1)} %get-tuple-element.32), channel_id=1, source_target_pairs={{0,24},{1,25},{2,26},{3,27},{4,28},{5,29},{6,30},{7,31},{8,16},{9,... | collective-permute-start | bytes 184328 | tf_op jit(solution)/shard_map/ppermute | solution.py:544
  8.5 3.9 %collective-permute-start.3 = (bf16[240,128]{1,0:T(8,128)(2,1)S(1)}, bf16[240,128]{1,0:T(8,128)(2,1)S(1)}, u32[]{:S(2)}, u32[]{:S(2)}) collective-permute-start(bf16[240,128]{1,0:T(8,128)(2,1)S(1)} %get-tuple-element.33), channel_id=1, source_target_pairs={{0,8},{1,9},{2,10},{3,11},{4,12},{5,13},{6,14},{7,15},{8,0},{9,1},... | collective-permute-start | bytes 184328 | tf_op jit(solution)/shard_map/ppermute | solution.py:543

commit v4 on v3

--- a/solution.py
+++ b/solution.py
@@ -166,18 +166,17 @@
         return core, side
 
 
-def relax(up, mid, down, rate):
+def five(up, mid, down):
     axis = mid.ndim - 2
-    beside = up + down + pltpu.roll(mid, 1, axis) + pltpu.roll(mid, mid.shape[axis] - 1, axis)
-    return mid + rate * (beside - 4.0 * mid)
-
-
-def columns_inside(tiles, shape):
+    return mid + up + down + (pltpu.roll(mid, 1, axis) + pltpu.roll(mid, mid.shape[axis] - 1, axis))
+
+
+def on_grid(tiles, row, own):
     t = lax.axis_index("tile")
-    sub = sublane(shape)
-    return jnp.logical_and(
-        jnp.logical_or(sub >= 8, t > 0), jnp.logical_or(sub < shape[-2] - 8, t < tiles - 1)
-    )
+    side = row[own:]
+    sub = sublane(side.shape)
+    ok = ((sub >= 4) | (t < tiles - 1)) & ((sub < 4) | (t > 0))
+    return jnp.concatenate([row[:own], jnp.where(ok, side, 0.0)], axis=0)
 
 
 def silu(v):
@@ -219,25 +218,23 @@
 
 def inner(
     secs, tiles, tile_map, atmos, cloudy, w_in, w_out, c_in, c_out, ocean, tile_a, tile_b,
-    field, sums, perm, source, spots, cells, spread, xs, hid, place, place_sem,
+    field, sums, blend, present, spots, cells, spread, xs, hid, place, place_sem,
 ):
     map_copy = pltpu.make_async_copy(tile_map, place, place_sem)
     map_copy.start()
     rows, cols, feat = atmos.shape
     sea_rows, sea_cols, sea_feat = ocean.shape
     sides = Sides(tiles, rows, feat, tile_a, tile_b)
-    inside = columns_inside(tiles, (cols + 16, feat))
 
     def line(r):
-        side = sides.air(r)
-        return jnp.concatenate([side, atmos[r], side], axis=0)
+        return jnp.concatenate([atmos[r], sides.air(r)], axis=0)
 
     lines, ones = [line(0), line(1)], []
     for r in range(1, rows - 1):
         lines.append(line(r + 1))
-        ones.append(jnp.where(inside, relax(*lines[-3:], kappa_air), 0.0))
+        ones.append(on_grid(tiles, five(*lines[-3:]), cols))
         if len(ones) >= 3:
-            two = relax(*ones[-3:], kappa_air)[8 : 8 + cols]
+            two = kappa_air**ASTEPS * five(*ones[-3:])[:cols]
             field[r - 3] = two
             xs[(r - 3) * cols : (r - 2) * cols, :] = two.astype(bf16)
     clear, cloud = physics(xs[...], w_in, w_out, c_in, c_out, hid)
@@ -269,17 +266,42 @@
     at = lax.broadcasted_iota(jnp.int32, spread.shape, 1) // 2
     spread[...] = (at == sublane(spread.shape) % half_cols).astype(f32).astype(bf16)
     count = secs * tiles
-    me = lax.axis_index("sec") * tiles + lax.axis_index("tile")
-    row = sublane((count, LANES))
-    row_t = row % tiles
-    under = jnp.zeros((count, LANES), jnp.int32)
+    s, t = lax.axis_index("sec"), lax.axis_index("tile")
     map_copy.wait()
+    under = jnp.int32(0)
     for k in range(tiles):
-        under = jnp.where(row_t == k, place[k], under)
-    under = row - row_t + under
-    source[...] = (under == me).astype(f32)
-    at = lax.broadcasted_iota(jnp.int32, perm.shape, 1) % count
-    perm[...] = (at == under[:, 0:1]).astype(f32).astype(bf16)
+        under = jnp.where(place[k] == t, k, under)
+
+    def device(shape):
+        row = sublane(shape)
+        block, kind = row // 8, row % 8
+        at_s = s + block // 3 - 1
+        at_t = jnp.where(kind < 2, t, under) + block % 3 - 1
+        ok = (at_s >= 0) & (at_s < secs) & (at_t >= 0) & (at_t < tiles)
+        return kind, at_s * tiles, at_t, ok
+
+    present[...] = device(present.shape)[3].astype(f32)
+    shape = (blend.shape[0], blend.shape[1] // 3)
+    kind, base, at_t, ok = device(shape)
+    above = jnp.zeros(shape, jnp.int32)
+    for k in range(tiles):
+        above = jnp.where(at_t == k, place[k], above)
+    column = lax.broadcasted_iota(jnp.int32, shape, 1)
+    which, column = column // count, column % count
+    here = jnp.where(column == base + at_t, 1.0, 0.0)
+    there = jnp.where(column == base + above, 1.0, 0.0)
+    top = jnp.where(kind == 1, 0.2, jnp.where(kind == 3, 1.0, 1.4))
+    parts = (
+        jnp.where((kind == 0) | (kind == 2), -0.4, 0.0) * there,
+        jnp.where(kind == 1, -0.4, 0.0) * there,
+        top * here,
+        jnp.where(kind == 1, 1.0, 0.0) * here,
+    )
+    total = jnp.zeros(shape, f32)
+    for q, part in enumerate(parts):
+        total = jnp.where(which == q, part, total)
+    high, low = parts_of(jnp.where(ok & (kind < 4), total, 0.0), 2)
+    blend[...] = jnp.concatenate([high, high, low], axis=1)
 
 
 def border(
@@ -290,7 +312,6 @@
     s = lax.axis_index("sec")
     sides = Sides(tiles, rows, feat, tile_a, tile_b)
     ends = Ends(secs, cols, feat, sums.shape[2] // (rows // 2), sec_a, sec_b)
-    inside = columns_inside(tiles, (cols + 16, feat))
 
     def line(r):
         if 0 <= r < rows:
@@ -299,18 +320,18 @@
             piece = ends.north if r < 0 else ends.south
             core = ends.air(piece, r + ASTEPS if r < 0 else r - rows)
             side = ends.air_side(piece)
-        return jnp.concatenate([side, core, side], axis=0)
+        return jnp.concatenate([core, side], axis=0)
 
     at = 0
     for first in (0, rows - 2):
         lines = [line(r) for r in range(first - 2, first + 4)]
-        ones = [jnp.where(inside, relax(*lines[k : k + 3], kappa_air), 0.0) for k in range(4)]
+        ones = [on_grid(tiles, five(*lines[k : k + 3]), cols) for k in range(4)]
         if first == 0:
             ones[0] = jnp.where(s > 0, ones[0], 0.0)
         else:
             ones[3] = jnp.where(s < secs - 1, ones[3], 0.0)
         for k in range(2):
-            two = relax(*ones[k : k + 3], kappa_air)[8 : 8 + cols]
+            two = kappa_air**ASTEPS * five(*ones[k : k + 3])[:cols]
             field[at] = two
             xs[at * cols : (at + 1) * cols, :] = two.astype(bf16)
             at += 1
@@ -333,7 +354,6 @@
     s = lax.axis_index("sec")
     sides = Sides(tiles, rows, feat, tile_a, tile_b)
     ends = Ends(secs, cols, feat, sea_cols, sec_a, sec_b)
-    inside = columns_inside(tiles, (sea_cols + 16, sea_feat))
     state = []
     for r in range(-OSTEPS, sea_rows + OSTEPS):
         if 0 <= r < sea_rows:
@@ -342,19 +362,20 @@
             core, side = ends.sea(ends.north, r + OSTEPS)
         else:
             core, side = ends.sea(ends.south, r - sea_rows)
-        state.append(jnp.concatenate([side, core, side], axis=0))
-    for step in range(OSTEPS):
-        state = [relax(*state[k : k + 3], kappa_sea) for k in range(len(state) - 2)]
-        depth = OSTEPS - 1 - step
+        state.append(jnp.concatenate([core, side], axis=0))
+    for depth in reversed(range(OSTEPS)):
+        state = [five(*state[k : k + 3]) for k in range(len(state) - 2)]
+        if depth == 0:
+            break
         for k, new in enumerate(state):
-            new = jnp.where(inside, new, 0.0)
+            new = on_grid(tiles, new, sea_cols)
             if k < depth:
                 new = jnp.where(s > 0, new, 0.0)
             elif k >= depth + sea_rows:
                 new = jnp.where(s < secs - 1, new, 0.0)
             state[k] = new
     for r in range(sea_rows):
-        out[r] = state[r][8 : 8 + sea_cols]
+        out[r] = kappa_sea**OSTEPS * state[r][:sea_cols]
 
 
 def fetch(*refs):
@@ -369,57 +390,61 @@
         copy.wait()
 
 
-def thirds(v, axis):
-    high = v.astype(bf16)
-    rest = v - high.astype(f32)
-    middle = rest.astype(bf16)
-    low = (rest - middle.astype(f32)).astype(bf16)
-    return jnp.concatenate([high, middle, low], axis=axis)
+def parts_of(v, count):
+    parts = []
+    for _ in range(count):
+        part = v.astype(bf16)
+        v = v - part.astype(f32)
+        parts.append(part)
+    return parts
 
 
 def final(
-    secs, tiles, gathered, perm, source, spots, cells, spread, inner_rows, border_rows,
+    secs, tiles, gathered, blend, inside, spots, cells, spread, inner_rows, border_rows,
     ocean, tile_a, tile_b, sec_b, sec_a,
     air_out, sea_out, back, stage, sea, sea_stage, back_stage, sems,
 ):
     rows, cols, feat = air_out.shape
     sea_rows, sea_cols, sea_feat = sea.shape
-    count = secs * tiles
-    me = lax.axis_index("sec") * tiles + lax.axis_index("tile")
     halves = feat // LANES
     half_cols = cols // 2
-    top0, top1 = gathered[:, 2, :], gathered[:, 3, :]
-    mine = source[...]
-
-    def pick(mask, v):
-        return jnp.sum(mask * v, axis=0, keepdims=True)
-
-    def upright_at(line, *lanes):
-        sub = sublane((LANES, 3 * LANES))
-        out = jnp.zeros((LANES, 3 * LANES), f32)
-        for v, at in zip(line, lanes):
-            out = jnp.where(sub == at, jnp.broadcast_to(thirds(v, 1).astype(f32), out.shape), out)
-        return out.astype(bf16)
+
+    def upright_at(lines, *lanes):
+        first = sublane((16, LANES)) == 0
+        groups = [jnp.zeros((16, 2 * LANES), bf16)] * (LANES // 16)
+        for line, at in zip(lines, lanes):
+            whole = jnp.where(first, jnp.broadcast_to(line, first.shape), 0.0)
+            groups[at // 16] = jnp.concatenate(parts_of(whole, 2), axis=1)
+        return jnp.concatenate(groups, axis=0)
 
     def against(one_hot, values):
         return lax.dot_general(
             one_hot, values, (((1,), (1,)), ((), ())), preferred_element_type=f32
         )
 
-    landing = pick(mine, top0)
-    patch = against(spots[...], upright_at([landing], 0))
-
-    air = thirds(jnp.concatenate([gathered[:, 0, :], gathered[:, 1, :]], axis=1), 0)
-    air = jnp.dot(perm[...], air, preferred_element_type=f32)
-    state0 = top0 + 0.5 * (0.8 * (top0 - air[:, :LANES]))
-    state1 = top1 + 0.5 * (0.8 * (0.5 * top0 - air[:, LANES:]))
-
-    first_lane = lax.broadcasted_iota(jnp.int32, (cols, LANES), 1) == 0
+    everything = jnp.concatenate([gathered[:, q, :] for q in range(4)], axis=0)
+    high, low = parts_of(everything, 2)
+    blocks = jnp.dot(
+        blend[...],
+        jnp.concatenate([high, low, high], axis=0),
+        preferred_element_type=f32,
+    )
+    keep = inside[...]
+    blocks = {
+        (k // 3, k % 3): (blocks[8 * k : 8 * k + 8], keep[8 * k : 8 * k + 8] > 0.0)
+        for k in range(9)
+    }
+    landing = blocks[1, 1][0][3:4]
+    patch = against(spots[...], upright_at([0.4 * landing], 0))
+    rest = jnp.where(lax.broadcasted_iota(jnp.int32, (cols, LANES), 1) == 0, 0.6, 1.0)
+
     step_rows = 4
     copies = []
     for first in range(0, rows, step_rows):
         for r in range(first, first + step_rows):
-            value = patch[(r // 2) * cols : (r // 2 + 1) * cols]
+            if r % 2 == 0:
+                value = patch[(r // 2) * cols : (r // 2 + 1) * cols]
+                added = (value, 0.5 * value)
             for h in range(halves):
                 lanes = slice(h * LANES, (h + 1) * LANES)
                 if r < 2:
@@ -428,8 +453,7 @@
                     old = border_rows[r - rows + 4, :, lanes]
                 else:
                     old = inner_rows[r - 2, :, lanes]
-                flux = 0.8 * ((1.0 if h == 0 else 0.5) * value - old)
-                stage[r, :, lanes] = old + jnp.where(first_lane, 0.5 * flux, 0.0)
+                stage[r, :, lanes] = old * rest + added[h]
         copies.append(
             pltpu.make_async_copy(
                 stage.at[first : first + step_rows],
@@ -440,32 +464,36 @@
         copies[-1].start()
 
     sea_steps(secs, tiles, rows, cols, feat, ocean, tile_a, tile_b, sec_b, sec_a, sea)
-    lane = lax.broadcasted_iota(jnp.int32, (count, LANES), 1)
-    row = sublane((count, LANES))
-    lane_c = lane % sea_cols
-    first_c, last_c = lane_c == 0, lane_c == sea_cols - 1
+    lane = tile_iotas()[0]
+    first_c, last_c = lane % sea_cols == 0, lane % sea_cols == sea_cols - 1
     first_r, last_r = lane < sea_cols, lane >= LANES - sea_cols
-    first_t, last_t = row % tiles == 0, row % tiles == tiles - 1
-    first_s, last_s = row < tiles, row >= count - tiles
-
-    def roll(v, shift, axis):
-        return pltpu.roll(v, shift % v.shape[axis], axis)
-
-    def step(v):
-        east_t = jnp.where(last_t, 0.0, roll(v, -1, 0))
-        west_t = jnp.where(first_t, 0.0, roll(v, 1, 0))
-        east = jnp.where(last_c, roll(east_t, sea_cols - 1, 1), roll(v, -1, 1))
-        west = jnp.where(first_c, roll(west_t, 1 - sea_cols, 1), roll(v, 1, 1))
-        down, up = roll(v, -sea_cols, 1), roll(v, sea_cols, 1)
-        down_s = jnp.where(last_s, 0.0, roll(down, -tiles, 0))
-        up_s = jnp.where(first_s, 0.0, roll(up, tiles, 0))
-        beside = jnp.where(last_r, down_s, down) + jnp.where(first_r, up_s, up) + east + west
-        return v + kappa_sea * (beside - 4.0 * v)
-
-    for _ in range(OSTEPS):
-        state0, state1 = step(state0), step(state1)
-    from_me = (row == me).astype(f32)
-    own = upright_at([pick(from_me, state0), pick(from_me, state1)], 0, sea_feat // 2)
+
+    def roll(v, shift):
+        return pltpu.roll(v, shift % LANES, 1)
+
+    def step(old, wanted):
+        def side(at, edge, shift, cross):
+            near = roll(old[at][0], shift)
+            return lambda other: (
+                jnp.where(edge, roll(old[other][0], cross), near) if other in old else near
+            )
+
+        new = {}
+        for i, j in wanted:
+            v, ok = old[i, j]
+            up = side((i, j), first_r, sea_cols, sea_cols)((i - 1, j))
+            down = side((i, j), last_r, -sea_cols, -sea_cols)((i + 1, j))
+            west = side((i, j), first_c, 1, 1 - sea_cols)((i, j - 1))
+            east = side((i, j), last_c, -1, sea_cols - 1)((i, j + 1))
+            v = v + (up + down) + (west + east)
+            new[i, j] = jnp.where(ok, v, 0.0), ok
+        return new
+
+    plus = [(0, 1), (1, 0), (1, 1), (1, 2), (2, 1)]
+    for wanted in [list(blocks)] * (OSTEPS - 2) + [plus, [(1, 1)]]:
+        blocks = step(blocks, wanted)
+    mine = kappa_sea**OSTEPS * blocks[1, 1][0]
+    own = upright_at([mine[0:1], mine[1:2]], 0, sea_feat // 2)
     own = against(cells[...], own)
     lane_s = lax.broadcasted_iota(jnp.int32, (sea_cols, sea_feat), 1)
     surface = jnp.logical_or(lane_s == 0, lane_s == sea_feat // 2)
@@ -475,10 +503,11 @@
     copies.append(pltpu.make_async_copy(sea_stage, sea_out, sems.at[rows // step_rows]))
     copies[-1].start()
 
-    returned = jnp.broadcast_to(pick(mine, state0), (rows, LANES))
+    returned = jnp.broadcast_to(mine[2:3], (rows, LANES))
     lane_b = lax.broadcasted_iota(jnp.int32, (rows, LANES), 1)
     lines = jnp.where(lane_b // half_cols == sublane((rows, LANES)) // 2, returned, 0.0)
-    back_stage[...] = jnp.dot(thirds(lines, 1), spread[...], preferred_element_type=f32)
+    lines = jnp.concatenate(parts_of(lines, 2), axis=1)
+    back_stage[...] = jnp.dot(lines, spread[...], preferred_element_type=f32)
     copies.append(pltpu.make_async_copy(back_stage, back, sems.at[rows // step_rows + 1]))
     copies[-1].start()
     for copy in copies:
@@ -550,11 +579,11 @@
         (
             shape((rows - 4, cols, feat), f32),
             shape((4, 8, LANES), f32),
-            shape((count, 3 * count), bf16),
-            shape((count, LANES), f32),
-            shape((rows // 2 * cols, 3 * LANES), bf16),
-            shape((LANES, 3 * LANES), bf16),
-            shape((3 * LANES, cols), bf16),
+            shape((80, 12 * count), bf16),
+            shape((72, LANES), f32),
+            shape((rows // 2 * cols, 2 * LANES), bf16),
+            shape((LANES, 2 * LANES), bf16),
+            shape((2 * LANES, cols), bf16),
         ),
         [HBM] + [VMEM] * 9,
         (VMEM,) * 7,

time: 27 us -> 26.7 us (0.989)
  Pallas kernels: 7.03 us -> 6.75 us
    pallas_call x6, Pallas kernels: 7.03 us -> 6.75 us  [call(): pl.pallas_call(body, out_shape=out_shape, in_specs=in_specs, out_specs=ou...]
where the time goes in v4:
time: 26.7 us; the launch traced here: 26.5 us
  blocking collectives  11.8 us (44%)
  Pallas kernels  6.75 us (25%)
  starting transfers between devices  6.22 us (23%)
  waiting for transfers between devices  1.03 us (4%)
  between operations  0.68 us (3%)
    all_to_all x1, blocking collectives, local(): gathered = lax.all_to_all(pay, AXES, 0, 0)  11.8 us
    pallas_call x6, Pallas kernels, call(): pl.pallas_call(body, out_shape=out_shape, in_specs=in_specs, out_specs=ou...  6.75 us
    ppermute x1, starting transfers between devices, local(): tile_a = lax.ppermute(send_a, AXES, tile_even)  4.03 us
    ppermute x1, starting transfers between devices, local(): sec_a = lax.ppermute(send_a, AXES, sec_even)  1.27 us
    ppermute x1, waiting for transfers between devices, local(): sec_b = lax.ppermute(send_b, AXES, sec_odd)  0.97 us
  transfers between devices with their start and end apart: 4, of which 1 were waited for; matrix products, arithmetic and copies ran while one was open for 0% of the time, Pallas kernels for 13%

profile of v4, /device:TPU:0, one launch (start us, length us, event | category | flops | bytes accessed | tf_op | source)
XLA Modules:
  0.0 26.5 jit_solution(7195443838135810096)
XLA Ops:
  0.6 1.0 %pack_tile.1 = (bf16[96,128]{1,0:T(8,128)(2,1)S(1)}, bf16[96,128]{1,0:T(8,128)(2,1)S(1)}) custom-call(f32[16,32,256]{2,1,0:T(8,128)} %refs_5_.1, f32[8,16,128]{2,1,0:T(8,128)} %refs_6_.1), custom_call_target="tpu_custom_call" | custom-call | tf_op jit(solution)/shard_map/pack_tile/pallas_call | solution.py:528
  1.7 0.5 %collective-permute-start.1 = (bf16[96,128]{1,0:T(8,128)(2,1)S(1)}, bf16[96,128]{1,0:T(8,128)(2,1)S(1)}, u32[]{:S(2)}, u32[]{:S(2)}) collective-permute-start(bf16[96,128]{1,0:T(8,128)(2,1)S(1)} %get-tuple-element.30), channel_id=1, source_target_pairs={{0,8},{1,2},{2,1},{3,4},{4,3},{5,6},{6,5},{7,15},{8,0},{9,10},{10,... | collective-permute-start | bytes 73736 | tf_op jit(solution)/shard_map/ppermute | solution.py:554
  2.2 4.0 %collective-permute-start = (bf16[96,128]{1,0:T(8,128)(2,1)S(1)}, bf16[96,128]{1,0:T(8,128)(2,1)S(1)}, u32[]{:S(2)}, u32[]{:S(2)}) collective-permute-start(bf16[96,128]{1,0:T(8,128)(2,1)S(1)} %get-tuple-element.23.refs_0_), channel_id=1, source_target_pairs={{0,1},{1,0},{2,3},{3,2},{4,5},{5,4},{6,7},{7,6},{8,9},{9,8},{10,11... | collective-permute-start | bytes 73736 | tf_op jit(solution)/shard_map/ppermute | solution.py:553
  6.2 1.7 %fetch.1 = (bf16[256,1024]{1,0:T(8,128)(2,1)S(1)}, bf16[256,1024]{1,0:T(8,128)(2,1)S(1)}, bf16[1024,256]{1,0:T(8,128)(2,1)S(1)}, bf16[1024,256]{1,0:T(8,128)(2,1...) custom-call(bf16[96,128]{1,0:T(8,128)(2,1)S(1)} %get-tuple-element.23.refs_0_, ...), custom_call_target="tpu_custom_call" | custom-call | flops 1073741824 | tf_op jit(solution)/shard_map/fetch/pallas_call | solution.py:528
  8.0 0.0 collective-permute-done.1.tile_b
  8.0 0.0 collective-permute-done.tile_a
  8.1 0.4 %collective-permute-start.2 = (bf16[240,128]{1,0:T(8,128)(2,1)S(1)}, bf16[240,128]{1,0:T(8,128)(2,1)S(1)}, u32[]{:S(2)}, u32[]{:S(2)}) collective-permute-start(bf16[240,128]{1,0:T(8,128)(2,1)S(1)} %get-tuple-element.32), channel_id=1, source_target_pairs={{0,24},{1,25},{2,26},{3,27},{4,28},{5,29},{6,30},{7,31},{8,16},{9,... | collective-permute-start | bytes 184328 | tf_op jit(solution)/shard_map/ppermute | solution.py:573
  8.5 1.3 %collective-permute-start.3 = (bf16[240,128]{1,0:T(8,128)(2,1)S(1)}, bf16[240,128]{1,0:T(8,128)(2,1)S(1)}, u32[]{:S(2)}, u32[]{:S(2)}) collective-permute-start(bf16[240,128]{1,0:T(8,128)(2,1)S(1)} %get-tuple-element.33), channel_id=1, source_target_pairs={{0,8},{1,9},{2,10},{3,11},{4,12},{5,13},{6,14},{7,15},{8,0},{9,1},... | collective-permute-start | bytes 184328 | tf_op jit(solution)/shard_map/ppermute | solution.py:572
  9.7 1.7 %inner.1 = (f32[12,32,256]{2,1,0:T(8,128)S(1)}, f32[4,8,128]{2,1,0:T(8,128)S(1)}, bf16[80,384]{1,0:T(8,128)(2,1)S(1)}, f32[72,128]{1,0:T(8,128)S(1)}, bf16[256,2...) custom-call(s32[8]{0:T(128)} %tile_map.1, ...), custom_call_target="tpu_custom_call" | custom-call | flops 805306368 | tf_op jit(solution)/shard_map/inner/pallas_call | solution.py:528
  11.4 1.0 %collective-permute-done.2.sec_b = bf16[240,128]{1,0:T(8,128)(2,1)S(1)} collective-permute-done((bf16[240,128]{1,0:T(8,128)(2,1)S(1)}, bf16[240,128]{1,0:T(8,128)(2,1)S(1)}, u32[]{:S(2)}, u32[]{:S(2)}) %collective-permute-start.2) | collective-permute-done | bytes 61472 | tf_op jit(solution)/shard_map/ppermute | solution.py:573
  12.4 0.0 collective-permute-done.3.sec_a
  12.4 0.8 %border.1 = (f32[4,32,256]{2,1,0:T(8,128)S(1)}, f32[32,4,128]{2,1,0:T(4,128)S(1)}) custom-call(f32[16,32,256]{2,1,0:T(8,128)S(1)} %get-tuple-element.24.atmos, s32[16,32]{1,0:T(8,128)S(1)} %get-tuple-element.25.cloudy, bf16[256,1024]{1,0:T(8,128)(2,1)S(1)} %get-tuple-element.26.w_in, bf16[1024,256]{1,0:T(8,128)(2,1)S(1)} %get-tuple-element.27.w_out, ...), custom_call_target="tpu_custom_call" | custom-call | flops 268435456 | tf_op jit(solution)/shard_map/border/pallas_call | solution.py:528
  13.2 11.8 %all_to_all.5.gathered = f32[32,4,128]{2,1,0:T(4,128)S(1)} all-to-all(f32[32,4,128]{2,1,0:T(4,128)S(1)} %get-tuple-element.35), channel_id=1, replica_groups=mesh['sec'=4,'tile'=8] {'sec','tile'}, dimensions={0} | all-to-all | bytes 131072 | tf_op jit(solution)/shard_map/all_to_all | solution.py:608
  25.0 1.5 %final.1 = (f32[16,32,256]{2,1,0:T(8,128)}, f32[8,16,128]{2,1,0:T(8,128)}, f32[16,32]{1,0:T(8,128)}) custom-call(f32[32,4,128]{2,1,0:T(4,128)S(1)} %all_to_all.5.gathered, bf16[80,384]{1,0:T(8,128)(2,1)S(1)} %get-tuple-element.36.blend, f32[72,128]{1,0:T(8,128)S(1)} %get-tuple-element.37.inside, bf16[256,256]{1,0:T(8,128)(2,1)S(1)} %get-tuple-element.38.spots, ...), custom_call_target="tpu_custom_call" | custom-call | tf_op jit(solution)/shard_map/final/pallas_call | solution.py:528
  (1 shorter events, 0.0 us)
Async XLA Ops:
  1.7 6.3 %collective-permute-start.1 = (bf16[96,128]{1,0:T(8,128)(2,1)S(1)}, bf16[96,128]{1,0:T(8,128)(2,1)S(1)}, u32[]{:S(2)}, u32[]{:S(2)}) collective-permute-start(bf16[96,128]{1,0:T(8,128)(2,1)S(1)} %get-tuple-element.30), channel_id=1, source_target_pairs={{0,8},{1,2},{2,1},{3,4},{4,3},{5,6},{6,5},{7,15},{8,0},{9,10},{10,... | collective-permute-start | bytes 73736 | tf_op jit(solution)/shard_map/ppermute | solution.py:554
  2.2 5.8 %collective-permute-start = (bf16[96,128]{1,0:T(8,128)(2,1)S(1)}, bf16[96,128]{1,0:T(8,128)(2,1)S(1)}, u32[]{:S(2)}, u32[]{:S(2)}) collective-permute-start(bf16[96,128]{1,0:T(8,128)(2,1)S(1)} %get-tuple-element.23.refs_0_), channel_id=1, source_target_pairs={{0,1},{1,0},{2,3},{3,2},{4,5},{5,4},{6,7},{7,6},{8,9},{9,8},{10,11... | collective-permute-start | bytes 73736 | tf_op jit(solution)/shard_map/ppermute | solution.py:553
  8.1 4.3 %collective-permute-start.2 = (bf16[240,128]{1,0:T(8,128)(2,1)S(1)}, bf16[240,128]{1,0:T(8,128)(2,1)S(1)}, u32[]{:S(2)}, u32[]{:S(2)}) collective-permute-start(bf16[240,128]{1,0:T(8,128)(2,1)S(1)} %get-tuple-element.32), channel_id=1, source_target_pairs={{0,24},{1,25},{2,26},{3,27},{4,28},{5,29},{6,30},{7,31},{8,16},{9,... | collective-permute-start | bytes 184328 | tf_op jit(solution)/shard_map/ppermute | solution.py:573
  8.5 3.9 %collective-permute-start.3 = (bf16[240,128]{1,0:T(8,128)(2,1)S(1)}, bf16[240,128]{1,0:T(8,128)(2,1)S(1)}, u32[]{:S(2)}, u32[]{:S(2)}) collective-permute-start(bf16[240,128]{1,0:T(8,128)(2,1)S(1)} %get-tuple-element.33), channel_id=1, source_target_pairs={{0,8},{1,9},{2,10},{3,11},{4,12},{5,13},{6,14},{7,15},{8,0},{9,1},... | collective-permute-start | bytes 184328 | tf_op jit(solution)/shard_map/ppermute | solution.py:572

commit v5 on v4

--- a/solution.py
+++ b/solution.py
@@ -59,10 +59,12 @@
     return [v[:, at : at + LANES] for at in range(0, v.shape[1], LANES)]
 
 
-def pack_tile(atmos, ocean, out_a, out_b, west, east, sea, sems):
+def pack_first(atmos, ocean, out_a, out_b, rows_a, rows_b, west, east, ends, sea, sems):
     rows, cols, feat = atmos.shape
     sea_rows, sea_cols, _ = ocean.shape
     copies = (
+        pltpu.make_async_copy(atmos.at[0:ASTEPS], ends.at[0], sems.at[3]),
+        pltpu.make_async_copy(atmos.at[rows - ASTEPS : rows], ends.at[1], sems.at[4]),
         pltpu.make_async_copy(atmos.at[:, 0:8, :], west, sems.at[0]),
         pltpu.make_async_copy(atmos.at[:, cols - 8 : cols, :], east, sems.at[1]),
         pltpu.make_async_copy(ocean, sea, sems.at[2]),
@@ -91,6 +93,13 @@
     even = lax.axis_index("tile") % 2 == 0
     out_a[...] = jnp.where(even, to_east, to_west)
     out_b[...] = jnp.where(even, to_west, to_east)
+    south = 1 - lax.axis_index("sec") % 2
+    for out, end in ((rows_a, south), (rows_b, 1 - south)):
+        parts = []
+        for r in range(ASTEPS):
+            parts += halves_of(ends[end, r])
+        parts += [sea[end * (sea_rows - OSTEPS) + r] for r in range(OSTEPS)]
+        out[...] = jnp.concatenate(parts, axis=0).astype(bf16)
 
 
 class Sides:
@@ -119,38 +128,33 @@
         return self.merge(self.sea_at + r // 2, 4 if r % 2 == 0 else 0, 4 * (r % 2))
 
 
-def pack_sec(tiles, atmos, ocean, tile_a, tile_b, out_a, out_b):
-    rows, cols, feat = atmos.shape
-    sea_rows, sea_cols, _ = ocean.shape
+def pack_sec(tiles, rows, feat, sea_rows, tile_a, tile_b, rows_a, last, out_a, out_b):
     sides = Sides(tiles, rows, feat, tile_a, tile_b)
 
-    def payload(first, corner, sea_first):
-        parts = []
-        for r in range(ASTEPS):
-            parts += halves_of(atmos[first + r])
-        parts += halves_of(sides.air(corner))
-        parts += [ocean[sea_first + r] for r in range(OSTEPS)]
-        parts += [sides.sea(sea_first + r) for r in range(OSTEPS)]
-        return jnp.concatenate(parts, axis=0).astype(bf16)
-
-    to_north = payload(0, 0, 0)
-    to_south = payload(rows - ASTEPS, rows - 1, sea_rows - OSTEPS)
+    def corners(corner, sea_first):
+        sea = [sides.sea(sea_first + r) for r in range(OSTEPS)]
+        return jnp.concatenate(halves_of(sides.air(corner)) + sea, axis=0).astype(bf16)
+
     even = lax.axis_index("sec") % 2 == 0
-    out_a[...] = jnp.where(even, to_south, to_north)
-    out_b[...] = jnp.where(even, to_north, to_south)
+    north, south = corners(0, 0), corners(rows - 1, sea_rows - OSTEPS)
+    out_b[...] = jnp.where(even, north, south)
+    lines = rows_a.shape[0]
+    out_a[:lines, :] = rows_a[...]
+    out_a[lines:, :] = jnp.where(even, south, north)
 
 
 class Ends:
-    def __init__(self, secs, cols, feat, sea_cols, sec_a, sec_b):
+    def __init__(self, secs, cols, feat, sea_cols, sec_a, sec_b, sec_rows):
         s = lax.axis_index("sec")
         even = s % 2 == 0
-        a, b = sec_a[...].astype(f32), sec_b[...].astype(f32)
+        a = sec_a[...].astype(f32)
+        b = jnp.concatenate([sec_rows[...].astype(f32), sec_b[...].astype(f32)], axis=0)
         self.north = jnp.where(s > 0, jnp.where(even, b, a), 0.0)
         self.south = jnp.where(s < secs - 1, jnp.where(even, a, b), 0.0)
         self.halves, self.cols, self.sea_cols = feat // LANES, cols, sea_cols
-        self.corner = ASTEPS * self.halves * cols
-        self.sea_at = self.corner + 8 * self.halves
-        self.side_at = self.sea_at + OSTEPS * sea_cols
+        self.sea_at = ASTEPS * self.halves * cols
+        self.corner = self.sea_at + OSTEPS * sea_cols
+        self.side_at = self.corner + 8 * self.halves
 
     def air(self, piece, k):
         cut = [(k * self.halves + h) * self.cols for h in range(self.halves)]
@@ -216,12 +220,61 @@
             means[q] = means[q] + jnp.where(hit, value, 0.0)
 
 
-def inner(
-    secs, tiles, tile_map, atmos, cloudy, w_in, w_out, c_in, c_out, ocean, tile_a, tile_b,
-    field, sums, blend, present, spots, cells, spread, xs, hid, place, place_sem,
+def plan(
+    secs, tiles, cols, first, tile_map, blend, present, spots, cells, spread, place, place_sem
 ):
     map_copy = pltpu.make_async_copy(tile_map, place, place_sem)
     map_copy.start()
+    half_cols = cols // 2
+    cell = sublane(spots.shape)
+    at = lax.broadcasted_iota(jnp.int32, spots.shape, 1) % LANES
+    spots[...] = (at == cell // cols * half_cols + cell % cols // 2).astype(f32).astype(bf16)
+    at = lax.broadcasted_iota(jnp.int32, cells.shape, 1) % LANES
+    cells[...] = (at == sublane(cells.shape)).astype(f32).astype(bf16)
+    at = lax.broadcasted_iota(jnp.int32, spread.shape, 1) // 2
+    spread[...] = (at == sublane(spread.shape) % half_cols).astype(f32).astype(bf16)
+    count = secs * tiles
+    s, t = lax.axis_index("sec"), lax.axis_index("tile")
+    map_copy.wait()
+    under = jnp.int32(0)
+    for k in range(tiles):
+        under = jnp.where(place[k] == t, k, under)
+
+    def device(shape):
+        row = sublane(shape)
+        block, kind = row // 8, row % 8
+        at_s = s + block // 3 - 1
+        at_t = jnp.where(kind < 2, t, under) + block % 3 - 1
+        ok = (at_s >= 0) & (at_s < secs) & (at_t >= 0) & (at_t < tiles)
+        return kind, at_s * tiles, at_t, ok
+
+    present[...] = device(present.shape)[3].astype(f32)
+    shape = (blend.shape[0], blend.shape[1] // 3)
+    kind, base, at_t, ok = device(shape)
+    above = jnp.zeros(shape, jnp.int32)
+    for k in range(tiles):
+        above = jnp.where(at_t == k, place[k], above)
+    column = lax.broadcasted_iota(jnp.int32, shape, 1)
+    which, column = column // count, column % count
+    here = jnp.where(column == base + at_t, 1.0, 0.0)
+    there = jnp.where(column == base + above, 1.0, 0.0)
+    top = jnp.where(kind == 1, 0.2, jnp.where(kind == 3, 1.0, 1.4))
+    parts = (
+        jnp.where((kind == 0) | (kind == 2), -0.4, 0.0) * there,
+        jnp.where(kind == 1, -0.4, 0.0) * there,
+        top * here,
+        jnp.where(kind == 1, 1.0, 0.0) * here,
+    )
+    total = jnp.zeros(shape, f32)
+    for q, part in enumerate(parts):
+        total = jnp.where(which == q, part, total)
+    high, low = parts_of(jnp.where(ok & (kind < 4), total, 0.0), 2)
+    blend[...] = jnp.concatenate([high, high, low], axis=1)
+
+
+def inner(
+    tiles, atmos, cloudy, w_in, w_out, c_in, c_out, ocean, tile_a, tile_b, field, sums, xs, hid
+):
     rows, cols, feat = atmos.shape
     sea_rows, sea_cols, sea_feat = ocean.shape
     sides = Sides(tiles, rows, feat, tile_a, tile_b)
@@ -257,61 +310,16 @@
                 tops[q] = tops[q] + jnp.where(hit, value, 0.0)
     for q, part in enumerate(means + tops):
         sums[q] = part
-    half_cols = cols // 2
-    cell = sublane(spots.shape)
-    at = lax.broadcasted_iota(jnp.int32, spots.shape, 1) % LANES
-    spots[...] = (at == cell // cols * half_cols + cell % cols // 2).astype(f32).astype(bf16)
-    at = lax.broadcasted_iota(jnp.int32, cells.shape, 1) % LANES
-    cells[...] = (at == sublane(cells.shape)).astype(f32).astype(bf16)
-    at = lax.broadcasted_iota(jnp.int32, spread.shape, 1) // 2
-    spread[...] = (at == sublane(spread.shape) % half_cols).astype(f32).astype(bf16)
-    count = secs * tiles
-    s, t = lax.axis_index("sec"), lax.axis_index("tile")
-    map_copy.wait()
-    under = jnp.int32(0)
-    for k in range(tiles):
-        under = jnp.where(place[k] == t, k, under)
-
-    def device(shape):
-        row = sublane(shape)
-        block, kind = row // 8, row % 8
-        at_s = s + block // 3 - 1
-        at_t = jnp.where(kind < 2, t, under) + block % 3 - 1
-        ok = (at_s >= 0) & (at_s < secs) & (at_t >= 0) & (at_t < tiles)
-        return kind, at_s * tiles, at_t, ok
-
-    present[...] = device(present.shape)[3].astype(f32)
-    shape = (blend.shape[0], blend.shape[1] // 3)
-    kind, base, at_t, ok = device(shape)
-    above = jnp.zeros(shape, jnp.int32)
-    for k in range(tiles):
-        above = jnp.where(at_t == k, place[k], above)
-    column = lax.broadcasted_iota(jnp.int32, shape, 1)
-    which, column = column // count, column % count
-    here = jnp.where(column == base + at_t, 1.0, 0.0)
-    there = jnp.where(column == base + above, 1.0, 0.0)
-    top = jnp.where(kind == 1, 0.2, jnp.where(kind == 3, 1.0, 1.4))
-    parts = (
-        jnp.where((kind == 0) | (kind == 2), -0.4, 0.0) * there,
-        jnp.where(kind == 1, -0.4, 0.0) * there,
-        top * here,
-        jnp.where(kind == 1, 1.0, 0.0) * here,
-    )
-    total = jnp.zeros(shape, f32)
-    for q, part in enumerate(parts):
-        total = jnp.where(which == q, part, total)
-    high, low = parts_of(jnp.where(ok & (kind < 4), total, 0.0), 2)
-    blend[...] = jnp.concatenate([high, high, low], axis=1)
 
 
 def border(
-    secs, tiles, atmos, cloudy, w_in, w_out, c_in, c_out, tile_a, tile_b, sec_b, sec_a, sums,
+    secs, tiles, atmos, cloudy, w_in, w_out, c_in, c_out, tile_a, tile_b, sec_b, sec_a, sec_rows, sums,
     field, pay, xs, hid,
 ):
     rows, cols, feat = atmos.shape
     s = lax.axis_index("sec")
     sides = Sides(tiles, rows, feat, tile_a, tile_b)
-    ends = Ends(secs, cols, feat, sums.shape[2] // (rows // 2), sec_a, sec_b)
+    ends = Ends(secs, cols, feat, sums.shape[2] // (rows // 2), sec_a, sec_b, sec_rows)
 
     def line(r):
         if 0 <= r < rows:
@@ -349,11 +357,11 @@
         pay[:, q, :] = jnp.broadcast_to(total, (pay.shape[0], LANES))
 
 
-def sea_steps(secs, tiles, rows, cols, feat, ocean, tile_a, tile_b, sec_b, sec_a, out):
+def sea_steps(secs, tiles, rows, cols, feat, ocean, tile_a, tile_b, sec_b, sec_a, sec_rows, out):
     sea_rows, sea_cols, sea_feat = ocean.shape
     s = lax.axis_index("sec")
     sides = Sides(tiles, rows, feat, tile_a, tile_b)
-    ends = Ends(secs, cols, feat, sea_cols, sec_a, sec_b)
+    ends = Ends(secs, cols, feat, sea_cols, sec_a, sec_b, sec_rows)
     state = []
     for r in range(-OSTEPS, sea_rows + OSTEPS):
         if 0 <= r < sea_rows:
@@ -378,18 +386,6 @@
         out[r] = kappa_sea**OSTEPS * state[r][:sea_cols]
 
 
-def fetch(*refs):
-    count = (len(refs) - 2) // 2
-    sems = refs[-1]
-    copies = [
-        pltpu.make_async_copy(refs[1 + k], refs[1 + count + k], sems.at[k]) for k in range(count)
-    ]
-    for copy in copies:
-        copy.start()
-    for copy in copies:
-        copy.wait()
-
-
 def parts_of(v, count):
     parts = []
     for _ in range(count):
@@ -401,7 +397,7 @@
 
 def final(
     secs, tiles, gathered, blend, inside, spots, cells, spread, inner_rows, border_rows,
-    ocean, tile_a, tile_b, sec_b, sec_a,
+    ocean, tile_a, tile_b, sec_b, sec_a, sec_rows,
     air_out, sea_out, back, stage, sea, sea_stage, back_stage, sems,
 ):
     rows, cols, feat = air_out.shape
@@ -463,7 +459,7 @@
         )
         copies[-1].start()
 
-    sea_steps(secs, tiles, rows, cols, feat, ocean, tile_a, tile_b, sec_b, sec_a, sea)
+    sea_steps(secs, tiles, rows, cols, feat, ocean, tile_a, tile_b, sec_b, sec_a, sec_rows, sea)
     lane = tile_iotas()[0]
     first_c, last_c = lane % sea_cols == 0, lane % sea_cols == sea_cols - 1
     first_r, last_r = lane < sea_cols, lane >= LANES - sea_cols
@@ -539,77 +535,77 @@
     def hbm(a):
         return pltpu.with_memory_space_constraint(a, pltpu.HBM)
 
+    lines = ASTEPS * halves * cols + OSTEPS * sea_cols
     out = shape((8 * (rows // 4 * halves + sea_rows // 2), LANES), bf16)
-    send_a, send_b = call(
-        pack_tile, "pack_tile", (out, out), [HBM] * 2, (VMEM, VMEM),
+    ends = shape((lines, LANES), bf16)
+    send_a, send_b, rows_a, rows_b = call(
+        pack_first, "pack_first", (out, out, ends, ends),
+        [HBM] * 2, (VMEM,) * 4,
         [
             pltpu.VMEM((rows, 8, feat), f32),
             pltpu.VMEM((rows, 8, feat), f32),
+            pltpu.VMEM((2, ASTEPS, cols, feat), f32),
             pltpu.VMEM(ocean.shape, f32),
-            pltpu.SemaphoreType.DMA((3,)),
+            pltpu.SemaphoreType.DMA((5,)),
         ],
         args=(hbm(atmos), hbm(ocean)),
     )
     tile_a = lax.ppermute(send_a, AXES, tile_even)
     tile_b = lax.ppermute(send_b, AXES, tile_odd)
-    wanted = (weight_in, cloud_in, weight_out, cloud_out, atmos, ocean, cloudy)
-    weight_in, cloud_in, weight_out, cloud_out, atmos, ocean, cloudy = call(
-        fetch, "fetch",
-        tuple(pltpu.VMEM(a.shape, a.dtype) for a in wanted),
-        [pl.BlockSpec(memory_space=pl.ANY)] + [HBM] * len(wanted),
-        (VMEM,) * len(wanted),
-        [pltpu.SemaphoreType.DMA((len(wanted),))],
-        flops=1 << 30,
-        args=(send_a, *(hbm(a) for a in wanted)),
-    )
-
-    lines = halves * (ASTEPS * cols + 8) + OSTEPS * (sea_cols + 8)
-    out = shape((lines, LANES), bf16)
-    send_a, send_b = call(
-        functools.partial(pack_sec, tiles), "pack_sec", (out, out), [VMEM] * 4, (VMEM, VMEM),
-        args=(atmos, ocean, tile_a, tile_b),
-    )
-    sec_a = lax.ppermute(send_a, AXES, sec_even)
-    sec_b = lax.ppermute(send_b, AXES, sec_odd)
-
-    weights = (weight_in, weight_out, cloud_in, cloud_out)
-    within = (rows - 4) * cols
-    inner_rows, sums, *plan = call(
-        functools.partial(inner, secs, tiles), "inner",
+    sec_rows = lax.ppermute(rows_b, AXES, sec_odd)
+    planned = call(
+        functools.partial(plan, secs, tiles, cols), "plan",
         (
-            shape((rows - 4, cols, feat), f32),
-            shape((4, 8, LANES), f32),
             shape((80, 12 * count), bf16),
             shape((72, LANES), f32),
             shape((rows // 2 * cols, 2 * LANES), bf16),
             shape((LANES, 2 * LANES), bf16),
             shape((2 * LANES, cols), bf16),
         ),
-        [HBM] + [VMEM] * 9,
-        (VMEM,) * 7,
-        [
-            pltpu.VMEM((within, feat), bf16),
-            pltpu.VMEM((2, within, width), bf16),
-            pltpu.SMEM(tile_map.shape, jnp.int32),
-            pltpu.SemaphoreType.DMA,
-        ],
+        [pl.BlockSpec(memory_space=pl.ANY), HBM],
+        (VMEM,) * 5,
+        [pltpu.SMEM(tile_map.shape, jnp.int32), pltpu.SemaphoreType.DMA],
+        flops=1 << 30,
+        args=(send_a, hbm(tile_map)),
+    )
+    corners = 8 * (halves + OSTEPS)
+    send_a, send_b = call(
+        functools.partial(pack_sec, tiles, rows, feat, sea_rows), "pack_sec",
+        (shape((lines + corners, LANES), bf16), shape((corners, LANES), bf16)),
+        [VMEM] * 3 + [pl.BlockSpec(memory_space=pl.ANY)], (VMEM, VMEM),
+        args=(tile_a, tile_b, rows_a, planned[1]),
+    )
+    sec_a = lax.ppermute(send_a, AXES, sec_even)
+    sec_b = lax.ppermute(send_b, AXES, sec_odd)
+
+    weights = (weight_in, weight_out, cloud_in, cloud_out)
+    within = (rows - 4) * cols
+    inner_rows, sums = call(
+        functools.partial(inner, tiles), "inner",
+        (
+            shape((rows - 4, cols, feat), f32),
+            shape((4, 8, LANES), f32),
+        ),
+        [VMEM] * 9,
+        (VMEM,) * 2,
+        [pltpu.VMEM((within, feat), bf16), pltpu.VMEM((2, within, width), bf16)],
         flops=within * feat * width * 8,
-        args=(hbm(tile_map), atmos, cloudy, *weights, ocean, tile_a, tile_b),
+        args=(atmos, cloudy, *weights, ocean, tile_a, tile_b),
     )
     border_rows, pay = call(
         functools.partial(border, secs, tiles), "border",
         (shape((4, cols, feat), f32), shape((count, 4, LANES), f32)),
-        [VMEM] * 11,
+        [VMEM] * 12,
         (VMEM,) * 2,
         [pltpu.VMEM((4 * cols, feat), bf16), pltpu.VMEM((2, 4 * cols, width), bf16)],
         flops=4 * cols * feat * width * 8,
-        args=(atmos, cloudy, *weights, tile_a, tile_b, sec_b, sec_a, sums),
+        args=(atmos, cloudy, *weights, tile_a, tile_b, sec_b, sec_a, sec_rows, sums),
     )
     gathered = lax.all_to_all(pay, AXES, 0, 0)
     return call(
         functools.partial(final, secs, tiles), "final",
         (shape(atmos.shape, f32), shape(ocean.shape, f32), shape((rows, cols), f32)),
-        [VMEM] * 13,
+        [VMEM] * 14,
         (HBM,) * 3,
         [
             pltpu.VMEM(atmos.shape, f32),
@@ -618,7 +614,7 @@
             pltpu.VMEM((rows, cols), f32),
             pltpu.SemaphoreType.DMA((rows // 4 + 2,)),
         ],
-        args=(gathered, *plan, inner_rows, border_rows, ocean, tile_a, tile_b, sec_b, sec_a),
+        args=(gathered, *planned, inner_rows, border_rows, ocean, tile_a, tile_b, sec_b, sec_a, sec_rows),
     )
 
 

time: 26.7 us -> 26.2 us (0.981)
  Pallas kernels: 6.75 us -> 5.89 us
  waiting for transfers between devices: 1.03 us -> 0.43 us
  blocking collectives: 11.8 us -> 12.3 us
  starting transfers between devices: 6.22 us -> 6.66 us
    ppermute x1, waiting for transfers between devices: 0.97 us -> 0.01 us  [local(): sec_b = lax.ppermute(send_b, AXES, sec_odd)]
    pallas_call x6, Pallas kernels: 6.75 us -> 5.89 us  [call(): pl.pallas_call(body, out_shape=out_shape, in_specs=in_specs, out_specs=ou...]
    ppermute x1, starting transfers between devices: 0.4 us -> 0.93 us  [local(): sec_b = lax.ppermute(send_b, AXES, sec_odd)]
    ppermute x1, starting transfers between devices: 1.27 us -> 0.74 us  [local(): sec_a = lax.ppermute(send_a, AXES, sec_even)]
    all_to_all x1, blocking collectives: 11.8 us -> 12.3 us  [local(): gathered = lax.all_to_all(pay, AXES, 0, 0)]
    ppermute x0 -> x1, starting transfers between devices: none -> 0.44 us  [local(): sec_rows = lax.ppermute(rows_b, AXES, sec_odd)]
    ppermute x1, waiting for transfers between devices: 0.05 us -> 0.42 us  [local(): tile_a = lax.ppermute(send_a, AXES, tile_even)]
  transfers between devices with their start and end apart: 4 -> 5, of which waited for: 1 -> 1; matrix products, arithmetic and copies ran while one was open for 0% -> 0% of each run, Pallas kernels for 13% -> 9%
where the time goes in v5:
time: 26.2 us; the launch traced here: 26.1 us
  blocking collectives  12.3 us (47%)
  starting transfers between devices  6.66 us (25%)
  Pallas kernels  5.89 us (22%)
  between operations  0.74 us (3%)
  waiting for transfers between devices  0.43 us (2%)
    all_to_all x1, blocking collectives, local(): gathered = lax.all_to_all(pay, AXES, 0, 0)  12.3 us
    pallas_call x6, Pallas kernels, call(): pl.pallas_call(body, out_shape=out_shape, in_specs=in_specs, out_specs=ou...  5.89 us
    ppermute x1, starting transfers between devices, local(): tile_a = lax.ppermute(send_a, AXES, tile_even)  4.03 us
    ppermute x1, starting transfers between devices, local(): sec_b = lax.ppermute(send_b, AXES, sec_odd)  0.93 us
    ppermute x1, starting transfers between devices, local(): sec_a = lax.ppermute(send_a, AXES, sec_even)  0.74 us
  transfers between devices with their start and end apart: 5, of which 1 were waited for; matrix products, arithmetic and copies ran while one was open for 0% of the time, Pallas kernels for 9%

profile of v5, /device:TPU:0, one launch (start us, length us, event | category | flops | bytes accessed | tf_op | source)
XLA Modules:
  0.0 26.1 jit_solution(13756945178417449381)
XLA Ops:
  0.6 1.1 %pack_first.1 = (bf16[96,128]{1,0:T(8,128)(2,1)S(1)}, bf16[96,128]{1,0:T(8,128)(2,1)S(1)}, bf16[192,128]{1,0:T(8,128)(2,1)S(1)}, bf16[192,128]{1,0:T(8,128)(2,1)S(1)}) custom-call(f32[16,32,256]{2,1,0:T(8,128)} %atmos.5, f32[8,16,128]{2,1,0:T(8,128)} %ocean.5), custom_call_target="tpu_custom_call" | custom-call | tf_op jit(solution)/shard_map/pack_first/pallas_call | solution.py:524
  1.8 0.5 %collective-permute-start.1 = (bf16[96,128]{1,0:T(8,128)(2,1)S(1)}, bf16[96,128]{1,0:T(8,128)(2,1)S(1)}, u32[]{:S(2)}, u32[]{:S(2)}) collective-permute-start(bf16[96,128]{1,0:T(8,128)(2,1)S(1)} %get-tuple-element.19), channel_id=1, source_target_pairs={{0,8},{1,2},{2,1},{3,4},{4,3},{5,6},{6,5},{7,15},{8,0},{9,10},{10,... | collective-permute-start | bytes 73736 | tf_op jit(solution)/shard_map/ppermute | solution.py:554
  2.3 4.0 %collective-permute-start = (bf16[96,128]{1,0:T(8,128)(2,1)S(1)}, bf16[96,128]{1,0:T(8,128)(2,1)S(1)}, u32[]{:S(2)}, u32[]{:S(2)}) collective-permute-start(bf16[96,128]{1,0:T(8,128)(2,1)S(1)} %get-tuple-element.18.first), channel_id=1, source_target_pairs={{0,1},{1,0},{2,3},{3,2},{4,5},{5,4},{6,7},{7,6},{8,9},{9,8},{10,11... | collective-permute-start | bytes 73736 | tf_op jit(solution)/shard_map/ppermute | solution.py:553
  6.3 0.0 copy-start
  6.3 0.0 copy-start.1
  6.3 0.0 copy-start.2
  6.3 0.0 copy-start.3
  6.3 0.0 copy-start.4
  6.3 0.4 %collective-permute-start.4 = (bf16[192,128]{1,0:T(8,128)(2,1)S(1)}, bf16[192,128]{1,0:T(8,128)(2,1)S(1)}, u32[]{:S(2)}, u32[]{:S(2)}) collective-permute-start(bf16[192,128]{1,0:T(8,128)(2,1)S(1)} %get-tuple-element.24), channel_id=1, source_target_pairs={{0,24},{1,25},{2,26},{3,27},{4,28},{5,29},{6,30},{7,31},{8,16},{9,... | collective-permute-start | bytes 147464 | tf_op jit(solution)/shard_map/ppermute | solution.py:555
  6.8 0.9 %plan.1 = (bf16[80,384]{1,0:T(8,128)(2,1)S(1)}, f32[72,128]{1,0:T(8,128)S(1)}, bf16[256,256]{1,0:T(8,128)(2,1)S(1)}, bf16[128,256]{1,0:T(8,128)(2,1)S(1)}, bf16[256,32]{1,0:T(8,128)(2,1)S(1)}) custom-call(bf16[96,128]{1,0:T(8,128)(2,1)S(1)} %get-tuple-element.18.first, s32[8]{0:T(128)} %tile_map.1), custom_call_target="tpu_custom_call" | custom-call | flops 1073741824 | tf_op jit(solution)/shard_map/plan/pallas_call | solution.py:524
  7.7 0.0 collective-permute-done.1.tile_b
  7.7 0.4 %collective-permute-done.tile_a = bf16[96,128]{1,0:T(8,128)(2,1)S(1)} collective-permute-done((bf16[96,128]{1,0:T(8,128)(2,1)S(1)}, bf16[96,128]{1,0:T(8,128)(2,1)S(1)}, u32[]{:S(2)}, u32[]{:S(2)}) %collective-permute-start) | collective-permute-done | bytes 24608 | tf_op jit(solution)/shard_map/ppermute | solution.py:553
  8.1 0.0 copy-start.5
  8.1 0.0 copy-start.6
  8.2 0.9 %collective-permute-start.2 = (bf16[48,128]{1,0:T(8,128)(2,1)S(1)}, bf16[48,128]{1,0:T(8,128)(2,1)S(1)}, u32[]{:S(2)}, u32[]{:S(2)}) collective-permute-start(bf16[48,128]{1,0:T(8,128)(2,1)S(1)} %get-tuple-element.22), channel_id=1, source_target_pairs={{0,24},{1,25},{2,26},{3,27},{4,28},{5,29},{6,30},{7,31},{8,16},{9,... | collective-permute-start | bytes 36872 | tf_op jit(solution)/shard_map/ppermute | solution.py:579
  9.1 0.7 %collective-permute-start.3 = (bf16[240,128]{1,0:T(8,128)(2,1)S(1)}, bf16[240,128]{1,0:T(8,128)(2,1)S(1)}, u32[]{:S(2)}, u32[]{:S(2)}) collective-permute-start(bf16[240,128]{1,0:T(8,128)(2,1)S(1)} %get-tuple-element.23), channel_id=1, source_target_pairs={{0,8},{1,9},{2,10},{3,11},{4,12},{5,13},{6,14},{7,15},{8,0},{9,1},... | collective-permute-start | bytes 184328 | tf_op jit(solution)/shard_map/ppermute | solution.py:578
  9.8 0.0 copy-done
  9.8 0.0 copy-done.1
  9.8 0.0 copy-done.2
  9.8 0.0 copy-done.3
  9.8 0.0 copy-done.4
  9.8 0.0 copy-done.5
  9.9 0.0 copy-done.6
  9.9 1.5 %inner.1 = (f32[12,32,256]{2,1,0:T(8,128)S(1)}, f32[4,8,128]{2,1,0:T(8,128)S(1)}) custom-call(f32[16,32,256]{2,1,0:T(8,128)S(1)} %copy-done, s32[16,32]{1,0:T(8,128)S(1)} %copy-done.6, bf16[256,1024]{1,0:T(8,128)(2,1)S(1)} %copy-done.1, bf16[1024,256]{1,0:T(8,128)(2,1)S(1)} %copy-done.2, bf16[256,1024]{1,0:T(8,128)(2,1)S(1)} %copy-done.3, ...), custom_call_target="tpu_custom_call" | custom-call | flops 805306368 | tf_op jit(solution)/shard_map/inner/pallas_call | solution.py:524
  11.4 0.0 collective-permute-done.2.sec_b
  11.4 0.0 collective-permute-done.4.sec_rows
  11.4 0.0 collective-permute-done.3.sec_a
  11.4 0.8 %border.1 = (f32[4,32,256]{2,1,0:T(8,128)S(1)}, f32[32,4,128]{2,1,0:T(4,128)S(1)}) custom-call(f32[16,32,256]{2,1,0:T(8,128)S(1)} %copy-done, s32[16,32]{1,0:T(8,128)S(1)} %copy-done.6, bf16[256,1024]{1,0:T(8,128)(2,1)S(1)} %copy-done.1, bf16[1024,256]{1,0:T(8,128)(2,1)S(1)} %copy-done.2, bf16[256,1024]{1,0:T(8,128)(2,1)S(1)} %copy-done.3, ...), custom_call_target="tpu_custom_call" | custom-call | flops 268435456 | tf_op jit(solution)/shard_map/border/pallas_call | solution.py:524
  12.2 12.3 %all_to_all.5.gathered = f32[32,4,128]{2,1,0:T(4,128)S(1)} all-to-all(f32[32,4,128]{2,1,0:T(4,128)S(1)} %get-tuple-element.26), channel_id=1, replica_groups=mesh['sec'=4,'tile'=8] {'sec','tile'}, dimensions={0} | all-to-all | bytes 131072 | tf_op jit(solution)/shard_map/all_to_all | solution.py:604
  24.6 1.5 %final.1 = (f32[16,32,256]{2,1,0:T(8,128)}, f32[8,16,128]{2,1,0:T(8,128)}, f32[16,32]{1,0:T(8,128)}) custom-call(f32[32,4,128]{2,1,0:T(4,128)S(1)} %all_to_all.5.gathered, bf16[80,384]{1,0:T(8,128)(2,1)S(1)} %get-tuple-element.27.blend, f32[72,128]{1,0:T(8,128)S(1)} %get-tuple-element.21.last.inside, bf16[256,256]{1,0:T(8,128)(2,1)S(1)} %get-tuple-element.28.spots, ...), custom_call_target="tpu_custom_call" | custom-call | tf_op jit(solution)/shard_map/final/pallas_call | solution.py:524
  (1 shorter events, 0.0 us)
Async XLA Ops:
  1.8 5.9 %collective-permute-start.1 = (bf16[96,128]{1,0:T(8,128)(2,1)S(1)}, bf16[96,128]{1,0:T(8,128)(2,1)S(1)}, u32[]{:S(2)}, u32[]{:S(2)}) collective-permute-start(bf16[96,128]{1,0:T(8,128)(2,1)S(1)} %get-tuple-element.19), channel_id=1, source_target_pairs={{0,8},{1,2},{2,1},{3,4},{4,3},{5,6},{6,5},{7,15},{8,0},{9,10},{10,... | collective-permute-start | bytes 73736 | tf_op jit(solution)/shard_map/ppermute | solution.py:554
  2.3 5.8 %collective-permute-start = (bf16[96,128]{1,0:T(8,128)(2,1)S(1)}, bf16[96,128]{1,0:T(8,128)(2,1)S(1)}, u32[]{:S(2)}, u32[]{:S(2)}) collective-permute-start(bf16[96,128]{1,0:T(8,128)(2,1)S(1)} %get-tuple-element.18.first), channel_id=1, source_target_pairs={{0,1},{1,0},{2,3},{3,2},{4,5},{5,4},{6,7},{7,6},{8,9},{9,8},{10,11... | collective-permute-start | bytes 73736 | tf_op jit(solution)/shard_map/ppermute | solution.py:553
  6.3 3.5 %copy-start = (f32[16,32,256]{2,1,0:T(8,128)S(1)}, f32[16,32,256]{2,1,0:T(8,128)}, u32[]{:S(2)}) copy-start(f32[16,32,256]{2,1,0:T(8,128)} %atmos.5) | copy-start | bytes 1572868
  6.3 3.5 %copy-start.1 = (bf16[256,1024]{1,0:T(8,128)(2,1)S(1)}, bf16[256,1024]{1,0:T(8,128)(2,1)}, u32[]{:S(2)}) copy-start(bf16[256,1024]{1,0:T(8,128)(2,1)} %w_in.3) | copy-start | bytes 1572868
  6.3 3.5 %copy-start.2 = (bf16[1024,256]{1,0:T(8,128)(2,1)S(1)}, bf16[1024,256]{1,0:T(8,128)(2,1)}, u32[]{:S(2)}) copy-start(bf16[1024,256]{1,0:T(8,128)(2,1)} %w_out.3) | copy-start | bytes 1572868
  6.3 3.5 %copy-start.3 = (bf16[256,1024]{1,0:T(8,128)(2,1)S(1)}, bf16[256,1024]{1,0:T(8,128)(2,1)}, u32[]{:S(2)}) copy-start(bf16[256,1024]{1,0:T(8,128)(2,1)} %c_in.3) | copy-start | bytes 1572868
  6.3 3.5 %copy-start.4 = (bf16[1024,256]{1,0:T(8,128)(2,1)S(1)}, bf16[1024,256]{1,0:T(8,128)(2,1)}, u32[]{:S(2)}) copy-start(bf16[1024,256]{1,0:T(8,128)(2,1)} %c_out.3) | copy-start | bytes 1572868
  6.3 5.1 %collective-permute-start.4 = (bf16[192,128]{1,0:T(8,128)(2,1)S(1)}, bf16[192,128]{1,0:T(8,128)(2,1)S(1)}, u32[]{:S(2)}, u32[]{:S(2)}) collective-permute-start(bf16[192,128]{1,0:T(8,128)(2,1)S(1)} %get-tuple-element.24), channel_id=1, source_target_pairs={{0,24},{1,25},{2,26},{3,27},{4,28},{5,29},{6,30},{7,31},{8,16},{9,... | collective-permute-start | bytes 147464 | tf_op jit(solution)/shard_map/ppermute | solution.py:555
  8.1 1.7 %copy-start.5 = (f32[8,16,128]{2,1,0:T(8,128)S(1)}, f32[8,16,128]{2,1,0:T(8,128)}, u32[]{:S(2)}) copy-start(f32[8,16,128]{2,1,0:T(8,128)} %ocean.5) | copy-start | bytes 196612
  8.1 1.7 %copy-start.6 = (s32[16,32]{1,0:T(8,128)S(1)}, s32[16,32]{1,0:T(8,128)}, u32[]{:S(2)}) copy-start(s32[16,32]{1,0:T(8,128)} %cloudy.3) | copy-start | bytes 6148
  8.2 3.3 %collective-permute-start.2 = (bf16[48,128]{1,0:T(8,128)(2,1)S(1)}, bf16[48,128]{1,0:T(8,128)(2,1)S(1)}, u32[]{:S(2)}, u32[]{:S(2)}) collective-permute-start(bf16[48,128]{1,0:T(8,128)(2,1)S(1)} %get-tuple-element.22), channel_id=1, source_target_pairs={{0,24},{1,25},{2,26},{3,27},{4,28},{5,29},{6,30},{7,31},{8,16},{9,... | collective-permute-start | bytes 36872 | tf_op jit(solution)/shard_map/ppermute | solution.py:579
  9.1 2.4 %collective-permute-start.3 = (bf16[240,128]{1,0:T(8,128)(2,1)S(1)}, bf16[240,128]{1,0:T(8,128)(2,1)S(1)}, u32[]{:S(2)}, u32[]{:S(2)}) collective-permute-start(bf16[240,128]{1,0:T(8,128)(2,1)S(1)} %get-tuple-element.23), channel_id=1, source_target_pairs={{0,8},{1,9},{2,10},{3,11},{4,12},{5,13},{6,14},{7,15},{8,0},{9,1},... | collective-permute-start | bytes 184328 | tf_op jit(solution)/shard_map/ppermute | solution.py:578

commit v6 on v5

--- a/solution.py
+++ b/solution.py
@@ -65,8 +65,10 @@
     copies = (
         pltpu.make_async_copy(atmos.at[0:ASTEPS], ends.at[0], sems.at[3]),
         pltpu.make_async_copy(atmos.at[rows - ASTEPS : rows], ends.at[1], sems.at[4]),
-        pltpu.make_async_copy(atmos.at[:, 0:8, :], west, sems.at[0]),
-        pltpu.make_async_copy(atmos.at[:, cols - 8 : cols, :], east, sems.at[1]),
+        pltpu.make_async_copy(atmos.at[:, 0:ASTEPS], west.at[:, 0:ASTEPS], sems.at[0]),
+        pltpu.make_async_copy(
+            atmos.at[:, cols - ASTEPS : cols], east.at[:, 8 - ASTEPS : 8], sems.at[1]
+        ),
         pltpu.make_async_copy(ocean, sea, sems.at[2]),
     )
     for copy in copies:
@@ -128,7 +130,7 @@
         return self.merge(self.sea_at + r // 2, 4 if r % 2 == 0 else 0, 4 * (r % 2))
 
 
-def pack_sec(tiles, rows, feat, sea_rows, tile_a, tile_b, rows_a, last, out_a, out_b):
+def pack_corners(tiles, rows, feat, sea_rows, tile_a, tile_b, last, out_a, out_b):
     sides = Sides(tiles, rows, feat, tile_a, tile_b)
 
     def corners(corner, sea_first):
@@ -137,37 +139,22 @@
 
     even = lax.axis_index("sec") % 2 == 0
     north, south = corners(0, 0), corners(rows - 1, sea_rows - OSTEPS)
+    out_a[...] = jnp.where(even, south, north)
     out_b[...] = jnp.where(even, north, south)
-    lines = rows_a.shape[0]
-    out_a[:lines, :] = rows_a[...]
-    out_a[lines:, :] = jnp.where(even, south, north)
-
-
-class Ends:
-    def __init__(self, secs, cols, feat, sea_cols, sec_a, sec_b, sec_rows):
-        s = lax.axis_index("sec")
-        even = s % 2 == 0
-        a = sec_a[...].astype(f32)
-        b = jnp.concatenate([sec_rows[...].astype(f32), sec_b[...].astype(f32)], axis=0)
-        self.north = jnp.where(s > 0, jnp.where(even, b, a), 0.0)
-        self.south = jnp.where(s < secs - 1, jnp.where(even, a, b), 0.0)
-        self.halves, self.cols, self.sea_cols = feat // LANES, cols, sea_cols
-        self.sea_at = ASTEPS * self.halves * cols
-        self.corner = self.sea_at + OSTEPS * sea_cols
-        self.side_at = self.corner + 8 * self.halves
-
-    def air(self, piece, k):
-        cut = [(k * self.halves + h) * self.cols for h in range(self.halves)]
-        return jnp.concatenate([piece[at : at + self.cols] for at in cut], axis=1)
-
-    def air_side(self, piece):
-        cut = [self.corner + 8 * h for h in range(self.halves)]
-        return jnp.concatenate([piece[at : at + 8] for at in cut], axis=1)
-
-    def sea(self, piece, k):
-        core = piece[self.sea_at + k * self.sea_cols : self.sea_at + (k + 1) * self.sea_cols]
-        side = piece[self.side_at + 8 * k : self.side_at + 8 * k + 8]
-        return core, side
+
+
+def from_ends(secs, a, b):
+    s = lax.axis_index("sec")
+    even = s % 2 == 0
+    a, b = a[...].astype(f32), b[...].astype(f32)
+    north = jnp.where(s > 0, jnp.where(even, b, a), 0.0)
+    south = jnp.where(s < secs - 1, jnp.where(even, a, b), 0.0)
+    return north, south
+
+
+def halves_beside(piece, at, count, halves):
+    cut = [piece[at + h * count : at + (h + 1) * count] for h in range(halves)]
+    return jnp.concatenate(cut, axis=1)
 
 
 def five(up, mid, down):
@@ -272,33 +259,53 @@
     blend[...] = jnp.concatenate([high, high, low], axis=1)
 
 
-def inner(
-    tiles, atmos, cloudy, w_in, w_out, c_in, c_out, ocean, tile_a, tile_b, field, sums, xs, hid
+def main(
+    secs, tiles, atmos, cloudy, w_in, w_out, c_in, c_out, ocean, tile_a, tile_b, rows_b, rows_a,
+    field, sums, ends, xs, hid,
 ):
     rows, cols, feat = atmos.shape
     sea_rows, sea_cols, sea_feat = ocean.shape
+    halves = feat // LANES
+    s = lax.axis_index("sec")
     sides = Sides(tiles, rows, feat, tile_a, tile_b)
+    north, south = from_ends(secs, rows_a, rows_b)
 
     def line(r):
-        return jnp.concatenate([atmos[r], sides.air(r)], axis=0)
-
-    lines, ones = [line(0), line(1)], []
-    for r in range(1, rows - 1):
+        if 0 <= r < rows:
+            return jnp.concatenate([atmos[r], sides.air(r)], axis=0)
+        piece, k = (north, r + ASTEPS) if r < 0 else (south, r - rows)
+        core = halves_beside(piece, k * halves * cols, cols, halves)
+        return jnp.concatenate([core, jnp.zeros((8, feat), f32)], axis=0)
+
+    lines, ones = [line(-2), line(-1)], []
+    for r in range(-1, rows + 1):
         lines.append(line(r + 1))
-        ones.append(on_grid(tiles, five(*lines[-3:]), cols))
+        one = on_grid(tiles, five(*lines[-3:]), cols)
+        if r == -1:
+            one = jnp.where(s > 0, one, 0.0)
+        if r == rows:
+            one = jnp.where(s < secs - 1, one, 0.0)
+        ones.append(one)
         if len(ones) >= 3:
             two = kappa_air**ASTEPS * five(*ones[-3:])[:cols]
-            field[r - 3] = two
-            xs[(r - 3) * cols : (r - 2) * cols, :] = two.astype(bf16)
+            field[r - 1] = two
+            xs[(r - 1) * cols : r * cols, :] = two.astype(bf16)
+    ends[...] = jnp.zeros(ends.shape, f32)
+    for k, r in enumerate((0, rows - 1)):
+        ends[2 * k : 2 * k + 1, :] = field[r, 0:1, :]
+        ends[2 * k + 1 : 2 * k + 2, :] = field[r, cols - 1 : cols, :]
     clear, cloud = physics(xs[...], w_in, w_out, c_in, c_out, hid)
     flags = cloudy[...].astype(f32)
     means = [jnp.zeros((8, LANES), f32) for _ in range(2)]
-    for k in range(rows - 4):
-        span = slice(k * cols, (k + 1) * cols)
-        flag = upright(flags[k + 2 : k + 3, :])
-        new = field[k] + (clear[span] + flag * cloud[span]).astype(bf16).astype(f32)
-        field[k] = new
-        add_row(means, new, k + 2)
+    for r in range(rows):
+        span = slice(r * cols, (r + 1) * cols)
+        flag = upright(flags[r : r + 1, :])
+        new = field[r] + (clear[span] + flag * cloud[span]).astype(bf16).astype(f32)
+        field[r] = new
+        if r in (0, rows - 1):
+            sub = sublane(new.shape)
+            new = jnp.where((sub > 0) & (sub < cols - 1), new, 0.0)
+        add_row(means, new, r)
     lane, sub = tile_iotas()
     tops = [jnp.zeros((8, LANES), f32) for _ in range(2)]
     for r in range(sea_rows):
@@ -312,64 +319,61 @@
         sums[q] = part
 
 
-def border(
-    secs, tiles, atmos, cloudy, w_in, w_out, c_in, c_out, tile_a, tile_b, sec_b, sec_a, sec_rows, sums,
-    field, pay, xs, hid,
+def finish(
+    secs, old, cloudy, w_in, w_out, c_in, c_out, ends, corner_b, corner_a, sums,
+    field, pay, hid,
 ):
-    rows, cols, feat = atmos.shape
-    s = lax.axis_index("sec")
-    sides = Sides(tiles, rows, feat, tile_a, tile_b)
-    ends = Ends(secs, cols, feat, sums.shape[2] // (rows // 2), sec_a, sec_b, sec_rows)
-
-    def line(r):
-        if 0 <= r < rows:
-            core, side = atmos[r], sides.air(r)
-        else:
-            piece = ends.north if r < 0 else ends.south
-            core = ends.air(piece, r + ASTEPS if r < 0 else r - rows)
-            side = ends.air_side(piece)
-        return jnp.concatenate([core, side], axis=0)
-
-    at = 0
-    for first in (0, rows - 2):
-        lines = [line(r) for r in range(first - 2, first + 4)]
-        ones = [on_grid(tiles, five(*lines[k : k + 3]), cols) for k in range(4)]
-        if first == 0:
-            ones[0] = jnp.where(s > 0, ones[0], 0.0)
-        else:
-            ones[3] = jnp.where(s < secs - 1, ones[3], 0.0)
-        for k in range(2):
-            two = kappa_air**ASTEPS * five(*ones[k : k + 3])[:cols]
-            field[at] = two
-            xs[at * cols : (at + 1) * cols, :] = two.astype(bf16)
-            at += 1
-    clear, cloud = physics(xs[...], w_in, w_out, c_in, c_out, hid)
+    rows, cols, feat = field.shape
+    halves = feat // LANES
+    half_cols = cols // 2
+    north, south = from_ends(secs, corner_a, corner_b)
+    north = halves_beside(north, 0, 8, halves)
+    south = halves_beside(south, 0, 8, halves)
+    sub = sublane((8, feat))
+    diagonal = jnp.zeros((8, feat), f32)
+    for k, cell in enumerate((north[7:8], north[0:1], south[7:8], south[0:1])):
+        diagonal = jnp.where(sub == k, cell, diagonal)
+    state = ends[...] + 2.0 * kappa_air**ASTEPS * diagonal
+    x = jnp.concatenate([state, jnp.zeros((8, feat), f32)], axis=0).astype(bf16)
+    clear, cloud = physics(x, w_in, w_out, c_in, c_out, hid)
+    places = ((0, 0), (0, cols - 1), (rows - 1, 0), (rows - 1, cols - 1))
     flags = cloudy[...].astype(f32)
-    means = [sums[0], sums[1]]
-    for at, r in enumerate((0, 1, rows - 2, rows - 1)):
-        span = slice(at * cols, (at + 1) * cols)
-        flag = upright(flags[r : r + 1, :])
-        new = field[at] + (clear[span] + flag * cloud[span]).astype(bf16).astype(f32)
-        field[at] = new
-        add_row(means, new, r)
+    flag = jnp.zeros((8, feat), f32)
+    lane, sub_lane = tile_iotas()
+    at = jnp.zeros((8, LANES), jnp.int32)
+    for k, (r, c) in enumerate(places):
+        flag = jnp.where(sub == k, flags[r : r + 1, c : c + 1], flag)
+        at = jnp.where(sub_lane == k, (r // 2) * half_cols + c // 2, at)
+    new = state + (clear[:8] + flag * cloud[:8]).astype(bf16).astype(f32)
+    for k, (r, c) in enumerate(places):
+        field[r, c : c + 1, :] = new[k : k + 1]
+    hit = (lane == at) & (sub_lane < 4)
+    means = [
+        sums[q] + jnp.where(hit, new[:, q * LANES : q * LANES + 1], 0.0) for q in range(2)
+    ]
     for q, part in enumerate((0.25 * means[0], 0.25 * means[1], sums[2], sums[3])):
         total = jnp.sum(part, axis=0, keepdims=True)
         pay[:, q, :] = jnp.broadcast_to(total, (pay.shape[0], LANES))
 
 
-def sea_steps(secs, tiles, rows, cols, feat, ocean, tile_a, tile_b, sec_b, sec_a, sec_rows, out):
+def sea_steps(secs, tiles, rows, cols, feat, ocean, halos, out):
     sea_rows, sea_cols, sea_feat = ocean.shape
+    tile_a, tile_b, rows_a, rows_b, corner_a, corner_b = halos
     s = lax.axis_index("sec")
     sides = Sides(tiles, rows, feat, tile_a, tile_b)
-    ends = Ends(secs, cols, feat, sea_cols, sec_a, sec_b, sec_rows)
+    cores = from_ends(secs, rows_a, rows_b)
+    corners = from_ends(secs, corner_a, corner_b)
+    halves = feat // LANES
     state = []
     for r in range(-OSTEPS, sea_rows + OSTEPS):
         if 0 <= r < sea_rows:
             core, side = ocean[r], sides.sea(r)
-        elif r < 0:
-            core, side = ends.sea(ends.north, r + OSTEPS)
         else:
-            core, side = ends.sea(ends.south, r - sea_rows)
+            end, k = (0, r + OSTEPS) if r < 0 else (1, r - sea_rows)
+            at = ASTEPS * halves * cols + k * sea_cols
+            core = cores[end][at : at + sea_cols]
+            at = 8 * (halves + k)
+            side = corners[end][at : at + 8]
         state.append(jnp.concatenate([core, side], axis=0))
     for depth in reversed(range(OSTEPS)):
         state = [five(*state[k : k + 3]) for k in range(len(state) - 2)]
@@ -396,8 +400,8 @@
 
 
 def final(
-    secs, tiles, gathered, blend, inside, spots, cells, spread, inner_rows, border_rows,
-    ocean, tile_a, tile_b, sec_b, sec_a, sec_rows,
+    secs, tiles, gathered, blend, inside, spots, cells, spread, field, ocean,
+    tile_a, tile_b, rows_b, rows_a, corner_b, corner_a,
     air_out, sea_out, back, stage, sea, sea_stage, back_stage, sems,
 ):
     rows, cols, feat = air_out.shape
@@ -443,13 +447,7 @@
                 added = (value, 0.5 * value)
             for h in range(halves):
                 lanes = slice(h * LANES, (h + 1) * LANES)
-                if r < 2:
-                    old = border_rows[r, :, lanes]
-                elif r >= rows - 2:
-                    old = border_rows[r - rows + 4, :, lanes]
-                else:
-                    old = inner_rows[r - 2, :, lanes]
-                stage[r, :, lanes] = old * rest + added[h]
+                stage[r, :, lanes] = field[r, :, lanes] * rest + added[h]
         copies.append(
             pltpu.make_async_copy(
                 stage.at[first : first + step_rows],
@@ -459,7 +457,8 @@
         )
         copies[-1].start()
 
-    sea_steps(secs, tiles, rows, cols, feat, ocean, tile_a, tile_b, sec_b, sec_a, sec_rows, sea)
+    halos = tile_a, tile_b, rows_a, rows_b, corner_a, corner_b
+    sea_steps(secs, tiles, rows, cols, feat, ocean, halos, sea)
     lane = tile_iotas()[0]
     first_c, last_c = lane % sea_cols == 0, lane % sea_cols == sea_cols - 1
     first_r, last_r = lane < sea_cols, lane >= LANES - sea_cols
@@ -520,13 +519,16 @@
     sec_even, sec_odd, tile_even, tile_odd = exchanges(secs, tiles)
     shape = jax.ShapeDtypeStruct
 
-    def call(body, name, out_shape, in_specs, out_specs, scratch=(), flops=0, args=()):
+    def call(
+        body, name, out_shape, in_specs, out_specs, scratch=(), flops=0, args=(), aliases={}
+    ):
         return pl.pallas_call(
             body,
             out_shape=out_shape,
             in_specs=in_specs,
             out_specs=out_specs,
             scratch_shapes=scratch,
+            input_output_aliases=aliases,
             compiler_params=pltpu.CompilerParams(vmem_limit_bytes=8 * 1024 * 1024),
             cost_estimate=pl.CostEstimate(flops=flops, bytes_accessed=0, transcendentals=0),
             name=name,
@@ -538,7 +540,7 @@
     lines = ASTEPS * halves * cols + OSTEPS * sea_cols
     out = shape((8 * (rows // 4 * halves + sea_rows // 2), LANES), bf16)
     ends = shape((lines, LANES), bf16)
-    send_a, send_b, rows_a, rows_b = call(
+    send_a, send_b, ends_a, ends_b = call(
         pack_first, "pack_first", (out, out, ends, ends),
         [HBM] * 2, (VMEM,) * 4,
         [
@@ -552,7 +554,8 @@
     )
     tile_a = lax.ppermute(send_a, AXES, tile_even)
     tile_b = lax.ppermute(send_b, AXES, tile_odd)
-    sec_rows = lax.ppermute(rows_b, AXES, sec_odd)
+    rows_b = lax.ppermute(ends_b, AXES, sec_odd)
+    rows_a = lax.ppermute(ends_a, AXES, sec_even)
     planned = call(
         functools.partial(plan, secs, tiles, cols), "plan",
         (
@@ -568,38 +571,34 @@
         flops=1 << 30,
         args=(send_a, hbm(tile_map)),
     )
-    corners = 8 * (halves + OSTEPS)
+    out = shape((8 * (halves + OSTEPS), LANES), bf16)
     send_a, send_b = call(
-        functools.partial(pack_sec, tiles, rows, feat, sea_rows), "pack_sec",
-        (shape((lines + corners, LANES), bf16), shape((corners, LANES), bf16)),
-        [VMEM] * 3 + [pl.BlockSpec(memory_space=pl.ANY)], (VMEM, VMEM),
-        args=(tile_a, tile_b, rows_a, planned[1]),
-    )
-    sec_a = lax.ppermute(send_a, AXES, sec_even)
-    sec_b = lax.ppermute(send_b, AXES, sec_odd)
+        functools.partial(pack_corners, tiles, rows, feat, sea_rows), "pack_corners", (out, out),
+        [VMEM] * 2 + [pl.BlockSpec(memory_space=pl.ANY)], (VMEM, VMEM),
+        args=(tile_a, tile_b, planned[1]),
+    )
+    corner_b = lax.ppermute(send_b, AXES, sec_odd)
+    corner_a = lax.ppermute(send_a, AXES, sec_even)
 
     weights = (weight_in, weight_out, cloud_in, cloud_out)
-    within = (rows - 4) * cols
-    inner_rows, sums = call(
-        functools.partial(inner, tiles), "inner",
-        (
-            shape((rows - 4, cols, feat), f32),
-            shape((4, 8, LANES), f32),
-        ),
-        [VMEM] * 9,
+    field, sums, ends = call(
+        functools.partial(main, secs, tiles), "main",
+        (shape(atmos.shape, f32), shape((4, 8, LANES), f32), shape((8, feat), f32)),
+        [VMEM] * 11,
+        (VMEM,) * 3,
+        [pltpu.VMEM((rows * cols, feat), bf16), pltpu.VMEM((2, rows * cols, width), bf16)],
+        flops=rows * cols * feat * width * 8,
+        args=(atmos, cloudy, *weights, ocean, tile_a, tile_b, rows_b, rows_a),
+    )
+    field, pay = call(
+        functools.partial(finish, secs), "finish",
+        (shape(atmos.shape, f32), shape((count, 4, LANES), f32)),
+        [VMEM] * 10,
         (VMEM,) * 2,
-        [pltpu.VMEM((within, feat), bf16), pltpu.VMEM((2, within, width), bf16)],
-        flops=within * feat * width * 8,
-        args=(atmos, cloudy, *weights, ocean, tile_a, tile_b),
-    )
-    border_rows, pay = call(
-        functools.partial(border, secs, tiles), "border",
-        (shape((4, cols, feat), f32), shape((count, 4, LANES), f32)),
-        [VMEM] * 12,
-        (VMEM,) * 2,
-        [pltpu.VMEM((4 * cols, feat), bf16), pltpu.VMEM((2, 4 * cols, width), bf16)],
-        flops=4 * cols * feat * width * 8,
-        args=(atmos, cloudy, *weights, tile_a, tile_b, sec_b, sec_a, sec_rows, sums),
+        [pltpu.VMEM((2, 16, width), bf16)],
+        flops=16 * feat * width * 8,
+        args=(field, cloudy, *weights, ends, corner_b, corner_a, sums),
+        aliases={0: 0},
     )
     gathered = lax.all_to_all(pay, AXES, 0, 0)
     return call(
@@ -614,7 +613,7 @@
             pltpu.VMEM((rows, cols), f32),
             pltpu.SemaphoreType.DMA((rows // 4 + 2,)),
         ],
-        args=(gathered, *planned, inner_rows, border_rows, ocean, tile_a, tile_b, sec_b, sec_a, sec_rows),
+        args=(gathered, *planned, field, ocean, tile_a, tile_b, rows_b, rows_a, corner_b, corner_a),
     )
 
 

time: 26.2 us -> 25.9 us (0.989)
  blocking collectives: 12.3 us -> 11.3 us
  starting transfers between devices: 6.66 us -> 7.16 us
    all_to_all x1, blocking collectives: 12.3 us -> 11.3 us  [local(): gathered = lax.all_to_all(pay, AXES, 0, 0)]
    ppermute x3 -> x4, starting transfers between devices: 2.11 us -> 2.61 us  [the longest x1 1.3 us: local(): rows_a = lax.ppermute(ends_a, AXES, sec_even)]
    ppermute x3 -> x4, waiting for transfers between devices: 0.01 us -> 0.5 us  [the longest x1 0.49 us: local(): rows_b = lax.ppermute(ends_b, AXES, sec_odd)]
    ppermute x1, waiting for transfers between devices: 0.42 us -> 0.01 us  [local(): tile_a = lax.ppermute(send_a, AXES, tile_even)]
  transfers between devices with their start and end apart: 5 -> 6, of which waited for: 1 -> 1; matrix products, arithmetic and copies ran while one was open for 0% -> 0% of each run, Pallas kernels for 9% -> 11%
where the time goes in v6:
time: 25.9 us; the launch traced here: 25.7 us
  blocking collectives  11.3 us (44%)
  starting transfers between devices  7.16 us (28%)
  Pallas kernels  5.94 us (23%)
  between operations  0.77 us (3%)
  waiting for transfers between devices  0.51 us (2%)
    all_to_all x1, blocking collectives, local(): gathered = lax.all_to_all(pay, AXES, 0, 0)  11.3 us
    pallas_call x6, Pallas kernels, call(): pl.pallas_call(body, out_shape=out_shape, in_specs=in_specs, out_specs=ou...  5.94 us
    ppermute x1, starting transfers between devices, local(): tile_a = lax.ppermute(send_a, AXES, tile_even)  4.03 us
    ppermute x1, starting transfers between devices, local(): rows_a = lax.ppermute(ends_a, AXES, sec_even)  1.3 us
    ppermute x1, starting transfers between devices, local(): corner_a = lax.ppermute(send_a, AXES, sec_even)  0.59 us
  transfers between devices with their start and end apart: 6, of which 1 were waited for; matrix products, arithmetic and copies ran while one was open for 0% of the time, Pallas kernels for 11%

profile of v6, /device:TPU:0, one launch (start us, length us, event | category | flops | bytes accessed | tf_op | source)
XLA Modules:
  0.0 25.7 jit_solution(6725356329683987659)
XLA Ops:
  0.6 1.0 %pack_first.1 = (bf16[96,128]{1,0:T(8,128)(2,1)S(1)}, bf16[96,128]{1,0:T(8,128)(2,1)S(1)}, bf16[192,128]{1,0:T(8,128)(2,1)S(1)}, bf16[192,128]{1,0:T(8,128)(2,1)S(1)}) custom-call(f32[16,32,256]{2,1,0:T(8,128)} %atmos.3, f32[8,16,128]{2,1,0:T(8,128)} %ocean.5), custom_call_target="tpu_custom_call" | custom-call | tf_op jit(solution)/shard_map/pack_first/pallas_call | solution.py:525
  1.7 0.5 %collective-permute-start.1 = (bf16[96,128]{1,0:T(8,128)(2,1)S(1)}, bf16[96,128]{1,0:T(8,128)(2,1)S(1)}, u32[]{:S(2)}, u32[]{:S(2)}) collective-permute-start(bf16[96,128]{1,0:T(8,128)(2,1)S(1)} %get-tuple-element.20), channel_id=1, source_target_pairs={{0,8},{1,2},{2,1},{3,4},{4,3},{5,6},{6,5},{7,15},{8,0},{9,10},{10,... | collective-permute-start | bytes 73736 | tf_op jit(solution)/shard_map/ppermute | solution.py:556
  2.2 4.0 %collective-permute-start = (bf16[96,128]{1,0:T(8,128)(2,1)S(1)}, bf16[96,128]{1,0:T(8,128)(2,1)S(1)}, u32[]{:S(2)}, u32[]{:S(2)}) collective-permute-start(bf16[96,128]{1,0:T(8,128)(2,1)S(1)} %get-tuple-element.19.first), channel_id=1, source_target_pairs={{0,1},{1,0},{2,3},{3,2},{4,5},{5,4},{6,7},{7,6},{8,9},{9,8},{10,11... | collective-permute-start | bytes 73736 | tf_op jit(solution)/shard_map/ppermute | solution.py:555
  6.2 0.4 %collective-permute-start.2 = (bf16[192,128]{1,0:T(8,128)(2,1)S(1)}, bf16[192,128]{1,0:T(8,128)(2,1)S(1)}, u32[]{:S(2)}, u32[]{:S(2)}) collective-permute-start(bf16[192,128]{1,0:T(8,128)(2,1)S(1)} %get-tuple-element.21), channel_id=1, source_target_pairs={{0,24},{1,25},{2,26},{3,27},{4,28},{5,29},{6,30},{7,31},{8,16},{9,... | collective-permute-start | bytes 147464 | tf_op jit(solution)/shard_map/ppermute | solution.py:557
  6.6 0.0 copy-start
  6.6 0.0 copy-start.1
  6.6 0.0 copy-start.2
  6.6 0.0 copy-start.3
  6.6 0.0 copy-start.4
  6.6 1.3 %collective-permute-start.3 = (bf16[192,128]{1,0:T(8,128)(2,1)S(1)}, bf16[192,128]{1,0:T(8,128)(2,1)S(1)}, u32[]{:S(2)}, u32[]{:S(2)}) collective-permute-start(bf16[192,128]{1,0:T(8,128)(2,1)S(1)} %get-tuple-element.22), channel_id=1, source_target_pairs={{0,8},{1,9},{2,10},{3,11},{4,12},{5,13},{6,14},{7,15},{8,0},{9,1},... | collective-permute-start | bytes 147464 | tf_op jit(solution)/shard_map/ppermute | solution.py:558
  7.9 0.8 %plan.1 = (bf16[80,384]{1,0:T(8,128)(2,1)S(1)}, f32[72,128]{1,0:T(8,128)S(1)}, bf16[256,256]{1,0:T(8,128)(2,1)S(1)}, bf16[128,256]{1,0:T(8,128)(2,1)S(1)}, bf16[256,32]{1,0:T(8,128)(2,1)S(1)}) custom-call(bf16[96,128]{1,0:T(8,128)(2,1)S(1)} %get-tuple-element.19.first, s32[8]{0:T(128)} %tile_map.1), custom_call_target="tpu_custom_call" | custom-call | flops 1073741824 | tf_op jit(solution)/shard_map/plan/pallas_call | solution.py:525
  8.7 0.0 copy-start.5
  8.7 0.0 collective-permute-done.1.tile_b
  8.7 0.0 collective-permute-done.tile_a
  8.7 0.0 copy-start.6
  8.8 0.4 %collective-permute-start.4 = (bf16[48,128]{1,0:T(8,128)(2,1)S(1)}, bf16[48,128]{1,0:T(8,128)(2,1)S(1)}, u32[]{:S(2)}, u32[]{:S(2)}) collective-permute-start(bf16[48,128]{1,0:T(8,128)(2,1)S(1)} %get-tuple-element.26), channel_id=1, source_target_pairs={{0,24},{1,25},{2,26},{3,27},{4,28},{5,29},{6,30},{7,31},{8,16},{9,... | collective-permute-start | bytes 36872 | tf_op jit(solution)/shard_map/ppermute | solution.py:580
  9.1 0.6 %collective-permute-start.5 = (bf16[48,128]{1,0:T(8,128)(2,1)S(1)}, bf16[48,128]{1,0:T(8,128)(2,1)S(1)}, u32[]{:S(2)}, u32[]{:S(2)}) collective-permute-start(bf16[48,128]{1,0:T(8,128)(2,1)S(1)} %get-tuple-element.27), channel_id=1, source_target_pairs={{0,8},{1,9},{2,10},{3,11},{4,12},{5,13},{6,14},{7,15},{8,0},{9,1},... | collective-permute-start | bytes 36872 | tf_op jit(solution)/shard_map/ppermute | solution.py:581
  9.7 0.5 %collective-permute-done.2.rows_b = bf16[192,128]{1,0:T(8,128)(2,1)S(1)} collective-permute-done((bf16[192,128]{1,0:T(8,128)(2,1)S(1)}, bf16[192,128]{1,0:T(8,128)(2,1)S(1)}, u32[]{:S(2)}, u32[]{:S(2)}) %collective-permute-start.2) | collective-permute-done | bytes 49184 | tf_op jit(solution)/shard_map/ppermute | solution.py:557
  10.2 0.0 collective-permute-done.3.rows_a
  10.2 0.0 copy-done
  10.2 0.0 copy-done.1
  10.2 0.0 copy-done.2
  10.2 0.0 copy-done.3
  10.2 0.0 copy-done.4
  10.2 0.0 copy-done.5
  10.3 0.0 copy-done.6
  10.3 2.0 %main.1 = (f32[16,32,256]{2,1,0:T(8,128)S(1)}, f32[4,8,128]{2,1,0:T(8,128)S(1)}, f32[8,256]{1,0:T(8,128)S(1)}) custom-call(f32[16,32,256]{2,1,0:T(8,128)S(1)} %copy-done, s32[16,32]{1,0:T(8,128)S(1)} %copy-done.6, bf16[256,1024]{1,0:T(8,128)(2,1)S(1)} %copy-done.1, bf16[1024,256]{1,0:T(8,128)(2,1)S(1)} %copy-done.2, bf16[256,1024]{1,0:T(8,128)(2,1)S(1)} %copy-done.3, ...), custom_call_target="tpu_custom_call" | custom-call | flops 1073741824 | tf_op jit(solution)/shard_map/main/pallas_call | solution.py:525
  12.3 0.0 collective-permute-done.4.corner_b
  12.3 0.0 collective-permute-done.5.corner_a
  12.3 0.6 %finish.1 = (f32[16,32,256]{2,1,0:T(8,128)S(1)}, f32[32,4,128]{2,1,0:T(4,128)S(1)}) custom-call(f32[16,32,256]{2,1,0:T(8,128)S(1)} %get-tuple-element.23.old, s32[16,32]{1,0:T(8,128)S(1)} %copy-done.6, bf16[256,1024]{1,0:T(8,128)(2,1)S(1)} %copy-done.1, bf16[1024,256]{1,0:T(8,128)(2,1)S(1)} %copy-done.2, ...), custom_call_target="tpu_custom_call", output_to_operand_aliasing={{0}: (0, {})} | custom-call | flops 33554432 | tf_op jit(solution)/shard_map/finish/pallas_call | solution.py:525
  12.9 11.3 %all_to_all.5.gathered = f32[32,4,128]{2,1,0:T(4,128)S(1)} all-to-all(f32[32,4,128]{2,1,0:T(4,128)S(1)} %get-tuple-element.29), channel_id=1, replica_groups=mesh['sec'=4,'tile'=8] {'sec','tile'}, dimensions={0} | all-to-all | bytes 131072 | tf_op jit(solution)/shard_map/all_to_all | solution.py:603
  24.2 1.5 %final.1 = (f32[16,32,256]{2,1,0:T(8,128)}, f32[8,16,128]{2,1,0:T(8,128)}, f32[16,32]{1,0:T(8,128)}) custom-call(f32[32,4,128]{2,1,0:T(4,128)S(1)} %all_to_all.5.gathered, bf16[80,384]{1,0:T(8,128)(2,1)S(1)} %get-tuple-element.30.blend, f32[72,128]{1,0:T(8,128)S(1)} %get-tuple-element.25.last.inside, bf16[256,256]{1,0:T(8,128)(2,1)S(1)} %get-tuple-element.31.spots, ...), custom_call_target="tpu_custom_call" | custom-call | tf_op jit(solution)/shard_map/final/pallas_call | solution.py:525
  (1 shorter events, 0.0 us)
Async XLA Ops:
  1.7 7.0 %collective-permute-start.1 = (bf16[96,128]{1,0:T(8,128)(2,1)S(1)}, bf16[96,128]{1,0:T(8,128)(2,1)S(1)}, u32[]{:S(2)}, u32[]{:S(2)}) collective-permute-start(bf16[96,128]{1,0:T(8,128)(2,1)S(1)} %get-tuple-element.20), channel_id=1, source_target_pairs={{0,8},{1,2},{2,1},{3,4},{4,3},{5,6},{6,5},{7,15},{8,0},{9,10},{10,... | collective-permute-start | bytes 73736 | tf_op jit(solution)/shard_map/ppermute | solution.py:556
  2.2 6.5 %collective-permute-start = (bf16[96,128]{1,0:T(8,128)(2,1)S(1)}, bf16[96,128]{1,0:T(8,128)(2,1)S(1)}, u32[]{:S(2)}, u32[]{:S(2)}) collective-permute-start(bf16[96,128]{1,0:T(8,128)(2,1)S(1)} %get-tuple-element.19.first), channel_id=1, source_target_pairs={{0,1},{1,0},{2,3},{3,2},{4,5},{5,4},{6,7},{7,6},{8,9},{9,8},{10,11... | collective-permute-start | bytes 73736 | tf_op jit(solution)/shard_map/ppermute | solution.py:555
  6.2 4.0 %collective-permute-start.2 = (bf16[192,128]{1,0:T(8,128)(2,1)S(1)}, bf16[192,128]{1,0:T(8,128)(2,1)S(1)}, u32[]{:S(2)}, u32[]{:S(2)}) collective-permute-start(bf16[192,128]{1,0:T(8,128)(2,1)S(1)} %get-tuple-element.21), channel_id=1, source_target_pairs={{0,24},{1,25},{2,26},{3,27},{4,28},{5,29},{6,30},{7,31},{8,16},{9,... | collective-permute-start | bytes 147464 | tf_op jit(solution)/shard_map/ppermute | solution.py:557
  6.6 3.6 %copy-start = (f32[16,32,256]{2,1,0:T(8,128)S(1)}, f32[16,32,256]{2,1,0:T(8,128)}, u32[]{:S(2)}) copy-start(f32[16,32,256]{2,1,0:T(8,128)} %atmos.3) | copy-start | bytes 1572868
  6.6 3.6 %copy-start.1 = (bf16[256,1024]{1,0:T(8,128)(2,1)S(1)}, bf16[256,1024]{1,0:T(8,128)(2,1)}, u32[]{:S(2)}) copy-start(bf16[256,1024]{1,0:T(8,128)(2,1)} %w_in.3) | copy-start | bytes 1572868
  6.6 3.6 %copy-start.2 = (bf16[1024,256]{1,0:T(8,128)(2,1)S(1)}, bf16[1024,256]{1,0:T(8,128)(2,1)}, u32[]{:S(2)}) copy-start(bf16[1024,256]{1,0:T(8,128)(2,1)} %w_out.3) | copy-start | bytes 1572868
  6.6 3.6 %copy-start.3 = (bf16[256,1024]{1,0:T(8,128)(2,1)S(1)}, bf16[256,1024]{1,0:T(8,128)(2,1)}, u32[]{:S(2)}) copy-start(bf16[256,1024]{1,0:T(8,128)(2,1)} %c_in.3) | copy-start | bytes 1572868
  6.6 3.6 %copy-start.4 = (bf16[1024,256]{1,0:T(8,128)(2,1)S(1)}, bf16[1024,256]{1,0:T(8,128)(2,1)}, u32[]{:S(2)}) copy-start(bf16[1024,256]{1,0:T(8,128)(2,1)} %c_out.3) | copy-start | bytes 1572868
  6.6 3.6 %collective-permute-start.3 = (bf16[192,128]{1,0:T(8,128)(2,1)S(1)}, bf16[192,128]{1,0:T(8,128)(2,1)S(1)}, u32[]{:S(2)}, u32[]{:S(2)}) collective-permute-start(bf16[192,128]{1,0:T(8,128)(2,1)S(1)} %get-tuple-element.22), channel_id=1, source_target_pairs={{0,8},{1,9},{2,10},{3,11},{4,12},{5,13},{6,14},{7,15},{8,0},{9,1},... | collective-permute-start | bytes 147464 | tf_op jit(solution)/shard_map/ppermute | solution.py:558
  8.7 1.6 %copy-start.5 = (f32[8,16,128]{2,1,0:T(8,128)S(1)}, f32[8,16,128]{2,1,0:T(8,128)}, u32[]{:S(2)}) copy-start(f32[8,16,128]{2,1,0:T(8,128)} %ocean.5) | copy-start | bytes 196612
  8.7 1.5 %copy-start.6 = (s32[16,32]{1,0:T(8,128)S(1)}, s32[16,32]{1,0:T(8,128)}, u32[]{:S(2)}) copy-start(s32[16,32]{1,0:T(8,128)} %cloudy.3) | copy-start | bytes 6148
  8.8 3.5 %collective-permute-start.4 = (bf16[48,128]{1,0:T(8,128)(2,1)S(1)}, bf16[48,128]{1,0:T(8,128)(2,1)S(1)}, u32[]{:S(2)}, u32[]{:S(2)}) collective-permute-start(bf16[48,128]{1,0:T(8,128)(2,1)S(1)} %get-tuple-element.26), channel_id=1, source_target_pairs={{0,24},{1,25},{2,26},{3,27},{4,28},{5,29},{6,30},{7,31},{8,16},{9,... | collective-permute-start | bytes 36872 | tf_op jit(solution)/shard_map/ppermute | solution.py:580
  9.1 3.2 %collective-permute-start.5 = (bf16[48,128]{1,0:T(8,128)(2,1)S(1)}, bf16[48,128]{1,0:T(8,128)(2,1)S(1)}, u32[]{:S(2)}, u32[]{:S(2)}) collective-permute-start(bf16[48,128]{1,0:T(8,128)(2,1)S(1)} %get-tuple-element.27), channel_id=1, source_target_pairs={{0,8},{1,9},{2,10},{3,11},{4,12},{5,13},{6,14},{7,15},{8,0},{9,1},... | collective-permute-start | bytes 36872 | tf_op jit(solution)/shard_map/ppermute | solution.py:581

commit v7 on v6

--- a/solution.py
+++ b/solution.py
@@ -208,10 +208,14 @@
 
 
 def plan(
-    secs, tiles, cols, first, tile_map, blend, present, spots, cells, spread, place, place_sem
+    secs, tiles, first, tile_map, cloudy, blend, present, spots, cells, spread, flags,
+    place, cloudy_here, sems,
 ):
-    map_copy = pltpu.make_async_copy(tile_map, place, place_sem)
+    map_copy = pltpu.make_async_copy(tile_map, place, sems.at[0])
     map_copy.start()
+    flags_copy = pltpu.make_async_copy(cloudy, cloudy_here, sems.at[1])
+    flags_copy.start()
+    rows, cols = cloudy.shape
     half_cols = cols // 2
     cell = sublane(spots.shape)
     at = lax.broadcasted_iota(jnp.int32, spots.shape, 1) % LANES
@@ -257,10 +261,15 @@
         total = jnp.where(which == q, part, total)
     high, low = parts_of(jnp.where(ok & (kind < 4), total, 0.0), 2)
     blend[...] = jnp.concatenate([high, high, low], axis=1)
+    flags_copy.wait()
+    values = cloudy_here[...].astype(f32)
+    for r in range(rows):
+        flag = upright(values[r : r + 1, :])
+        flags[r * cols : (r + 1) * cols, :] = jnp.broadcast_to(flag, (cols, LANES))
 
 
 def main(
-    secs, tiles, atmos, cloudy, w_in, w_out, c_in, c_out, ocean, tile_a, tile_b, rows_b, rows_a,
+    secs, tiles, atmos, flags, w_in, w_out, c_in, c_out, ocean, tile_a, tile_b, rows_b, rows_a,
     field, sums, ends, xs, hid,
 ):
     rows, cols, feat = atmos.shape
@@ -295,11 +304,10 @@
         ends[2 * k : 2 * k + 1, :] = field[r, 0:1, :]
         ends[2 * k + 1 : 2 * k + 2, :] = field[r, cols - 1 : cols, :]
     clear, cloud = physics(xs[...], w_in, w_out, c_in, c_out, hid)
-    flags = cloudy[...].astype(f32)
     means = [jnp.zeros((8, LANES), f32) for _ in range(2)]
     for r in range(rows):
         span = slice(r * cols, (r + 1) * cols)
-        flag = upright(flags[r : r + 1, :])
+        flag = jnp.concatenate([flags[span, :]] * halves, axis=1)
         new = field[r] + (clear[span] + flag * cloud[span]).astype(bf16).astype(f32)
         field[r] = new
         if r in (0, rows - 1):
@@ -320,7 +328,7 @@
 
 
 def finish(
-    secs, old, cloudy, w_in, w_out, c_in, c_out, ends, corner_b, corner_a, sums,
+    secs, old, all_flags, w_in, w_out, c_in, c_out, ends, corner_b, corner_a, sums,
     field, pay, hid,
 ):
     rows, cols, feat = field.shape
@@ -337,13 +345,14 @@
     x = jnp.concatenate([state, jnp.zeros((8, feat), f32)], axis=0).astype(bf16)
     clear, cloud = physics(x, w_in, w_out, c_in, c_out, hid)
     places = ((0, 0), (0, cols - 1), (rows - 1, 0), (rows - 1, cols - 1))
-    flags = cloudy[...].astype(f32)
-    flag = jnp.zeros((8, feat), f32)
+    flag = jnp.zeros((8, LANES), f32)
     lane, sub_lane = tile_iotas()
     at = jnp.zeros((8, LANES), jnp.int32)
     for k, (r, c) in enumerate(places):
-        flag = jnp.where(sub == k, flags[r : r + 1, c : c + 1], flag)
+        cell = r * cols + c
+        flag = jnp.where(sub_lane == k, all_flags[cell : cell + 1, :], flag)
         at = jnp.where(sub_lane == k, (r // 2) * half_cols + c // 2, at)
+    flag = jnp.concatenate([flag] * halves, axis=1)
     new = state + (clear[:8] + flag * cloud[:8]).astype(bf16).astype(f32)
     for k, (r, c) in enumerate(places):
         field[r, c : c + 1, :] = new[k : k + 1]
@@ -351,9 +360,9 @@
     means = [
         sums[q] + jnp.where(hit, new[:, q * LANES : q * LANES + 1], 0.0) for q in range(2)
     ]
-    for q, part in enumerate((0.25 * means[0], 0.25 * means[1], sums[2], sums[3])):
-        total = jnp.sum(part, axis=0, keepdims=True)
-        pay[:, q, :] = jnp.broadcast_to(total, (pay.shape[0], LANES))
+    parts = (0.25 * means[0], 0.25 * means[1], sums[2], sums[3])
+    total = jnp.concatenate([jnp.sum(part, axis=0, keepdims=True) for part in parts], axis=0)
+    pay[...] = jnp.broadcast_to(total[None], pay.shape)
 
 
 def sea_steps(secs, tiles, rows, cols, feat, ocean, halos, out):
@@ -556,20 +565,25 @@
     tile_b = lax.ppermute(send_b, AXES, tile_odd)
     rows_b = lax.ppermute(ends_b, AXES, sec_odd)
     rows_a = lax.ppermute(ends_a, AXES, sec_even)
-    planned = call(
-        functools.partial(plan, secs, tiles, cols), "plan",
+    *planned, flags = call(
+        functools.partial(plan, secs, tiles), "plan",
         (
             shape((80, 12 * count), bf16),
             shape((72, LANES), f32),
             shape((rows // 2 * cols, 2 * LANES), bf16),
             shape((LANES, 2 * LANES), bf16),
             shape((2 * LANES, cols), bf16),
+            shape((rows * cols, LANES), f32),
         ),
-        [pl.BlockSpec(memory_space=pl.ANY), HBM],
-        (VMEM,) * 5,
-        [pltpu.SMEM(tile_map.shape, jnp.int32), pltpu.SemaphoreType.DMA],
+        [pl.BlockSpec(memory_space=pl.ANY), HBM, HBM],
+        (VMEM,) * 6,
+        [
+            pltpu.SMEM(tile_map.shape, jnp.int32),
+            pltpu.VMEM(cloudy.shape, jnp.int32),
+            pltpu.SemaphoreType.DMA((2,)),
+        ],
         flops=1 << 30,
-        args=(send_a, hbm(tile_map)),
+        args=(send_a, hbm(tile_map), hbm(cloudy)),
     )
     out = shape((8 * (halves + OSTEPS), LANES), bf16)
     send_a, send_b = call(
@@ -588,7 +602,7 @@
         (VMEM,) * 3,
         [pltpu.VMEM((rows * cols, feat), bf16), pltpu.VMEM((2, rows * cols, width), bf16)],
         flops=rows * cols * feat * width * 8,
-        args=(atmos, cloudy, *weights, ocean, tile_a, tile_b, rows_b, rows_a),
+        args=(atmos, flags, *weights, ocean, tile_a, tile_b, rows_b, rows_a),
     )
     field, pay = call(
         functools.partial(finish, secs), "finish",
@@ -597,7 +611,7 @@
         (VMEM,) * 2,
         [pltpu.VMEM((2, 16, width), bf16)],
         flops=16 * feat * width * 8,
-        args=(field, cloudy, *weights, ends, corner_b, corner_a, sums),
+        args=(field, flags, *weights, ends, corner_b, corner_a, sums),
         aliases={0: 0},
     )
     gathered = lax.all_to_all(pay, AXES, 0, 0)

time: 25.9 us -> 25.9 us (level)
  no operation moved by 1% of the time
where the time goes in v7:
time: 25.9 us; the launch traced here: 25.7 us
  blocking collectives  11.4 us (44%)
  starting transfers between devices  7.07 us (27%)
  Pallas kernels  6 us (23%)
  between operations  0.76 us (3%)
  waiting for transfers between devices  0.46 us (2%)
    all_to_all x1, blocking collectives, local(): gathered = lax.all_to_all(pay, AXES, 0, 0)  11.4 us
    pallas_call x6, Pallas kernels, call(): pl.pallas_call(body, out_shape=out_shape, in_specs=in_specs, out_specs=ou...  6 us
    ppermute x1, starting transfers between devices, local(): tile_a = lax.ppermute(send_a, AXES, tile_even)  4.03 us
    ppermute x1, starting transfers between devices, local(): rows_a = lax.ppermute(ends_a, AXES, sec_even)  1.3 us
  transfers between devices with their start and end apart: 6, of which 1 were waited for; matrix products, arithmetic and copies ran while one was open for 0% of the time, Pallas kernels for 11%

profile of v7, /device:TPU:0, one launch (start us, length us, event | category | flops | bytes accessed | tf_op | source)
XLA Modules:
  0.0 25.7 jit_solution(13160508298650818651)
XLA Ops:
  0.6 1.0 %pack_first.1 = (bf16[96,128]{1,0:T(8,128)(2,1)S(1)}, bf16[96,128]{1,0:T(8,128)(2,1)S(1)}, bf16[192,128]{1,0:T(8,128)(2,1)S(1)}, bf16[192,128]{1,0:T(8,128)(2,1)S(1)}) custom-call(f32[16,32,256]{2,1,0:T(8,128)} %atmos.3, f32[8,16,128]{2,1,0:T(8,128)} %ocean.5), custom_call_target="tpu_custom_call" | custom-call | tf_op jit(solution)/shard_map/pack_first/pallas_call | solution.py:534
  1.7 0.5 %collective-permute-start.1 = (bf16[96,128]{1,0:T(8,128)(2,1)S(1)}, bf16[96,128]{1,0:T(8,128)(2,1)S(1)}, u32[]{:S(2)}, u32[]{:S(2)}) collective-permute-start(bf16[96,128]{1,0:T(8,128)(2,1)S(1)} %get-tuple-element.22), channel_id=1, source_target_pairs={{0,8},{1,2},{2,1},{3,4},{4,3},{5,6},{6,5},{7,15},{8,0},{9,10},{10,... | collective-permute-start | bytes 73736 | tf_op jit(solution)/shard_map/ppermute | solution.py:565
  2.2 4.0 %collective-permute-start = (bf16[96,128]{1,0:T(8,128)(2,1)S(1)}, bf16[96,128]{1,0:T(8,128)(2,1)S(1)}, u32[]{:S(2)}, u32[]{:S(2)}) collective-permute-start(bf16[96,128]{1,0:T(8,128)(2,1)S(1)} %get-tuple-element.20.first), channel_id=1, source_target_pairs={{0,1},{1,0},{2,3},{3,2},{4,5},{5,4},{6,7},{7,6},{8,9},{9,8},{10,11... | collective-permute-start | bytes 73736 | tf_op jit(solution)/shard_map/ppermute | solution.py:564
  6.2 0.4 %collective-permute-start.2 = (bf16[192,128]{1,0:T(8,128)(2,1)S(1)}, bf16[192,128]{1,0:T(8,128)(2,1)S(1)}, u32[]{:S(2)}, u32[]{:S(2)}) collective-permute-start(bf16[192,128]{1,0:T(8,128)(2,1)S(1)} %get-tuple-element.23), channel_id=1, source_target_pairs={{0,24},{1,25},{2,26},{3,27},{4,28},{5,29},{6,30},{7,31},{8,16},{9,... | collective-permute-start | bytes 147464 | tf_op jit(solution)/shard_map/ppermute | solution.py:566
  6.6 0.0 copy-start
  6.6 0.0 copy-start.1
  6.6 0.0 copy-start.2
  6.6 0.0 copy-start.3
  6.6 0.0 copy-start.4
  6.6 1.3 %collective-permute-start.3 = (bf16[192,128]{1,0:T(8,128)(2,1)S(1)}, bf16[192,128]{1,0:T(8,128)(2,1)S(1)}, u32[]{:S(2)}, u32[]{:S(2)}) collective-permute-start(bf16[192,128]{1,0:T(8,128)(2,1)S(1)} %get-tuple-element.24), channel_id=1, source_target_pairs={{0,8},{1,9},{2,10},{3,11},{4,12},{5,13},{6,14},{7,15},{8,0},{9,1},... | collective-permute-start | bytes 147464 | tf_op jit(solution)/shard_map/ppermute | solution.py:567
  7.9 0.9 %plan.1 = (bf16[80,384]{1,0:T(8,128)(2,1)S(1)}, f32[72,128]{1,0:T(8,128)S(1)}, bf16[256,256]{1,0:T(8,128)(2,1)S(1)}, bf16[128,256]{1,0:T(8,128)(2,1)S(1)}, bf16[...) custom-call(bf16[96,128]{1,0:T(8,128)(2,1)S(1)} %get-tuple-element.20.first, s32[8]{0:T(128)} %tile_map.1, s32[16,32]{1,0:T(8,128)} %cloudy.1), custom_call_target="tpu_custom_call" | custom-call | flops 1073741824 | tf_op jit(solution)/shard_map/plan/pallas_call | solution.py:534
  8.8 0.0 copy-start.5
  8.9 0.0 collective-permute-done.1.tile_b
  8.9 0.0 collective-permute-done.tile_a
  8.9 0.4 %collective-permute-start.4 = (bf16[48,128]{1,0:T(8,128)(2,1)S(1)}, bf16[48,128]{1,0:T(8,128)(2,1)S(1)}, u32[]{:S(2)}, u32[]{:S(2)}) collective-permute-start(bf16[48,128]{1,0:T(8,128)(2,1)S(1)} %get-tuple-element.28), channel_id=1, source_target_pairs={{0,24},{1,25},{2,26},{3,27},{4,28},{5,29},{6,30},{7,31},{8,16},{9,... | collective-permute-start | bytes 36872 | tf_op jit(solution)/shard_map/ppermute | solution.py:594
  9.3 0.5 %collective-permute-start.5 = (bf16[48,128]{1,0:T(8,128)(2,1)S(1)}, bf16[48,128]{1,0:T(8,128)(2,1)S(1)}, u32[]{:S(2)}, u32[]{:S(2)}) collective-permute-start(bf16[48,128]{1,0:T(8,128)(2,1)S(1)} %get-tuple-element.29), channel_id=1, source_target_pairs={{0,8},{1,9},{2,10},{3,11},{4,12},{5,13},{6,14},{7,15},{8,0},{9,1},... | collective-permute-start | bytes 36872 | tf_op jit(solution)/shard_map/ppermute | solution.py:595
  9.8 0.4 %collective-permute-done.2.rows_b = bf16[192,128]{1,0:T(8,128)(2,1)S(1)} collective-permute-done((bf16[192,128]{1,0:T(8,128)(2,1)S(1)}, bf16[192,128]{1,0:T(8,128)(2,1)S(1)}, u32[]{:S(2)}, u32[]{:S(2)}) %collective-permute-start.2) | collective-permute-done | bytes 49184 | tf_op jit(solution)/shard_map/ppermute | solution.py:566
  10.2 0.0 collective-permute-done.3.rows_a
  10.2 0.0 copy-done
  10.2 0.0 copy-done.1
  10.2 0.0 copy-done.2
  10.2 0.0 copy-done.3
  10.2 0.0 copy-done.4
  10.2 0.0 copy-done.5
  10.3 1.9 %main.1 = (f32[16,32,256]{2,1,0:T(8,128)S(1)}, f32[4,8,128]{2,1,0:T(8,128)S(1)}, f32[8,256]{1,0:T(8,128)S(1)}) custom-call(f32[16,32,256]{2,1,0:T(8,128)S(1)} %copy-done, f32[512,128]{1,0:T(8,128)S(1)} %get-tuple-element.21.flags.all_flags, bf16[256,1024]{1,0:T(8,128)(2,1)S(1)} %copy-done.1, bf16[1024,256]{1,0:T(8,128)(2,1)S(1)} %copy-done.2, ...), custom_call_target="tpu_custom_call" | custom-call | flops 1073741824 | tf_op jit(solution)/shard_map/main/pallas_call | solution.py:534
  12.2 0.0 collective-permute-done.4.corner_b
  12.2 0.0 collective-permute-done.5.corner_a
  12.2 0.6 %finish.1 = (f32[16,32,256]{2,1,0:T(8,128)S(1)}, f32[32,4,128]{2,1,0:T(4,128)S(1)}) custom-call(f32[16,32,256]{2,1,0:T(8,128)S(1)} %get-tuple-element.25.old, f32[512,128]{1,0:T(8,128)S(1)} %get-tuple-element.21.flags.all_flags, bf16[256,1024]{1,0:T(8,128)(2,1)S(1)} %copy-done.1, bf16[1024,256]{1,0:T(8,128)(2,1)S(1)} %copy-done.2, ...), custom_call_target="tpu_custom_call", output_to_operand_aliasing={{0}: (0, {})} | custom-call | flops 33554432 | tf_op jit(solution)/shard_map/finish/pallas_call | solution.py:534
  12.8 11.4 %all_to_all.5.gathered = f32[32,4,128]{2,1,0:T(4,128)S(1)} all-to-all(f32[32,4,128]{2,1,0:T(4,128)S(1)} %get-tuple-element.31), channel_id=1, replica_groups=mesh['sec'=4,'tile'=8] {'sec','tile'}, dimensions={0} | all-to-all | bytes 131072 | tf_op jit(solution)/shard_map/all_to_all | solution.py:617
  24.2 1.5 %final.1 = (f32[16,32,256]{2,1,0:T(8,128)}, f32[8,16,128]{2,1,0:T(8,128)}, f32[16,32]{1,0:T(8,128)}) custom-call(f32[32,4,128]{2,1,0:T(4,128)S(1)} %all_to_all.5.gathered, bf16[80,384]{1,0:T(8,128)(2,1)S(1)} %get-tuple-element.32.blend, f32[72,128]{1,0:T(8,128)S(1)} %get-tuple-element.27.last.inside, bf16[256,256]{1,0:T(8,128)(2,1)S(1)} %get-tuple-element.33.spots, ...), custom_call_target="tpu_custom_call" | custom-call | tf_op jit(solution)/shard_map/final/pallas_call | solution.py:534
  (1 shorter events, 0.0 us)
Async XLA Ops:
  1.7 7.2 %collective-permute-start.1 = (bf16[96,128]{1,0:T(8,128)(2,1)S(1)}, bf16[96,128]{1,0:T(8,128)(2,1)S(1)}, u32[]{:S(2)}, u32[]{:S(2)}) collective-permute-start(bf16[96,128]{1,0:T(8,128)(2,1)S(1)} %get-tuple-element.22), channel_id=1, source_target_pairs={{0,8},{1,2},{2,1},{3,4},{4,3},{5,6},{6,5},{7,15},{8,0},{9,10},{10,... | collective-permute-start | bytes 73736 | tf_op jit(solution)/shard_map/ppermute | solution.py:565
  2.2 6.7 %collective-permute-start = (bf16[96,128]{1,0:T(8,128)(2,1)S(1)}, bf16[96,128]{1,0:T(8,128)(2,1)S(1)}, u32[]{:S(2)}, u32[]{:S(2)}) collective-permute-start(bf16[96,128]{1,0:T(8,128)(2,1)S(1)} %get-tuple-element.20.first), channel_id=1, source_target_pairs={{0,1},{1,0},{2,3},{3,2},{4,5},{5,4},{6,7},{7,6},{8,9},{9,8},{10,11... | collective-permute-start | bytes 73736 | tf_op jit(solution)/shard_map/ppermute | solution.py:564
  6.2 4.0 %collective-permute-start.2 = (bf16[192,128]{1,0:T(8,128)(2,1)S(1)}, bf16[192,128]{1,0:T(8,128)(2,1)S(1)}, u32[]{:S(2)}, u32[]{:S(2)}) collective-permute-start(bf16[192,128]{1,0:T(8,128)(2,1)S(1)} %get-tuple-element.23), channel_id=1, source_target_pairs={{0,24},{1,25},{2,26},{3,27},{4,28},{5,29},{6,30},{7,31},{8,16},{9,... | collective-permute-start | bytes 147464 | tf_op jit(solution)/shard_map/ppermute | solution.py:566
  6.6 3.6 %copy-start = (f32[16,32,256]{2,1,0:T(8,128)S(1)}, f32[16,32,256]{2,1,0:T(8,128)}, u32[]{:S(2)}) copy-start(f32[16,32,256]{2,1,0:T(8,128)} %atmos.3) | copy-start | bytes 1572868
  6.6 3.6 %copy-start.1 = (bf16[256,1024]{1,0:T(8,128)(2,1)S(1)}, bf16[256,1024]{1,0:T(8,128)(2,1)}, u32[]{:S(2)}) copy-start(bf16[256,1024]{1,0:T(8,128)(2,1)} %w_in.3) | copy-start | bytes 1572868
  6.6 3.6 %copy-start.2 = (bf16[1024,256]{1,0:T(8,128)(2,1)S(1)}, bf16[1024,256]{1,0:T(8,128)(2,1)}, u32[]{:S(2)}) copy-start(bf16[1024,256]{1,0:T(8,128)(2,1)} %w_out.3) | copy-start | bytes 1572868
  6.6 3.6 %copy-start.3 = (bf16[256,1024]{1,0:T(8,128)(2,1)S(1)}, bf16[256,1024]{1,0:T(8,128)(2,1)}, u32[]{:S(2)}) copy-start(bf16[256,1024]{1,0:T(8,128)(2,1)} %c_in.3) | copy-start | bytes 1572868
  6.6 3.6 %copy-start.4 = (bf16[1024,256]{1,0:T(8,128)(2,1)S(1)}, bf16[1024,256]{1,0:T(8,128)(2,1)}, u32[]{:S(2)}) copy-start(bf16[1024,256]{1,0:T(8,128)(2,1)} %c_out.3) | copy-start | bytes 1572868
  6.6 3.6 %collective-permute-start.3 = (bf16[192,128]{1,0:T(8,128)(2,1)S(1)}, bf16[192,128]{1,0:T(8,128)(2,1)S(1)}, u32[]{:S(2)}, u32[]{:S(2)}) collective-permute-start(bf16[192,128]{1,0:T(8,128)(2,1)S(1)} %get-tuple-element.24), channel_id=1, source_target_pairs={{0,8},{1,9},{2,10},{3,11},{4,12},{5,13},{6,14},{7,15},{8,0},{9,1},... | collective-permute-start | bytes 147464 | tf_op jit(solution)/shard_map/ppermute | solution.py:567
  8.8 1.4 %copy-start.5 = (f32[8,16,128]{2,1,0:T(8,128)S(1)}, f32[8,16,128]{2,1,0:T(8,128)}, u32[]{:S(2)}) copy-start(f32[8,16,128]{2,1,0:T(8,128)} %ocean.5) | copy-start | bytes 196612
  8.9 3.3 %collective-permute-start.4 = (bf16[48,128]{1,0:T(8,128)(2,1)S(1)}, bf16[48,128]{1,0:T(8,128)(2,1)S(1)}, u32[]{:S(2)}, u32[]{:S(2)}) collective-permute-start(bf16[48,128]{1,0:T(8,128)(2,1)S(1)} %get-tuple-element.28), channel_id=1, source_target_pairs={{0,24},{1,25},{2,26},{3,27},{4,28},{5,29},{6,30},{7,31},{8,16},{9,... | collective-permute-start | bytes 36872 | tf_op jit(solution)/shard_map/ppermute | solution.py:594
  9.3 3.0 %collective-permute-start.5 = (bf16[48,128]{1,0:T(8,128)(2,1)S(1)}, bf16[48,128]{1,0:T(8,128)(2,1)S(1)}, u32[]{:S(2)}, u32[]{:S(2)}) collective-permute-start(bf16[48,128]{1,0:T(8,128)(2,1)S(1)} %get-tuple-element.29), channel_id=1, source_target_pairs={{0,8},{1,9},{2,10},{3,11},{4,12},{5,13},{6,14},{7,15},{8,0},{9,1},... | collective-permute-start | bytes 36872 | tf_op jit(solution)/shard_map/ppermute | solution.py:595

commit v8 on v7

--- a/solution.py
+++ b/solution.py
@@ -170,20 +170,13 @@
     return jnp.concatenate([row[:own], jnp.where(ok, side, 0.0)], axis=0)
 
 
-def silu(v):
-    return v * (0.5 + 0.5 * jnp.tanh(0.5 * v))
-
-
-def physics(x, w_in, w_out, c_in, c_out, hid):
-    width = w_in.shape[1]
+def physics(x, layers, hid):
+    first, second = layers
     block = 256
-    for which, first in enumerate((w_in, c_in)):
-        for j in range(0, width, block):
-            h = jnp.dot(x, first[:, j : j + block], preferred_element_type=f32)
-            hid[which, :, j : j + block] = silu(h).astype(bf16)
-    clear = jnp.dot(hid[0], w_out[...], preferred_element_type=f32)
-    cloud = jnp.dot(hid[1], c_out[...], preferred_element_type=f32)
-    return clear, cloud
+    for j in range(0, first.shape[1], block):
+        u = jnp.dot(x, first[:, j : j + block], preferred_element_type=f32)
+        hid[:, j : j + block] = (u + u * jnp.tanh(u)).astype(bf16)
+    return lambda: jnp.dot(hid[...], second[...], preferred_element_type=f32)
 
 
 def upright(line):
@@ -298,12 +291,13 @@
         if len(ones) >= 3:
             two = kappa_air**ASTEPS * five(*ones[-3:])[:cols]
             field[r - 1] = two
-            xs[(r - 1) * cols : r * cols, :] = two.astype(bf16)
+            xs[(r - 1) * cols : r * cols, :] = (0.5 * two).astype(bf16)
     ends[...] = jnp.zeros(ends.shape, f32)
     for k, r in enumerate((0, rows - 1)):
         ends[2 * k : 2 * k + 1, :] = field[r, 0:1, :]
         ends[2 * k + 1 : 2 * k + 2, :] = field[r, cols - 1 : cols, :]
-    clear, cloud = physics(xs[...], w_in, w_out, c_in, c_out, hid)
+    clear = physics(xs[...], (w_in, w_out), hid.at[0])()
+    cloud = physics(xs[...], (c_in, c_out), hid.at[1])()
     means = [jnp.zeros((8, LANES), f32) for _ in range(2)]
     for r in range(rows):
         span = slice(r * cols, (r + 1) * cols)
@@ -342,8 +336,10 @@
     for k, cell in enumerate((north[7:8], north[0:1], south[7:8], south[0:1])):
         diagonal = jnp.where(sub == k, cell, diagonal)
     state = ends[...] + 2.0 * kappa_air**ASTEPS * diagonal
-    x = jnp.concatenate([state, jnp.zeros((8, feat), f32)], axis=0).astype(bf16)
-    clear, cloud = physics(x, w_in, w_out, c_in, c_out, hid)
+    x = (0.5 * jnp.concatenate([state, jnp.zeros((8, feat), f32)], axis=0)).astype(bf16)
+    clear = physics(x, (w_in, w_out), hid.at[0])
+    cloud = physics(x, (c_in, c_out), hid.at[1])
+    clear, cloud = clear(), cloud()
     places = ((0, 0), (0, cols - 1), (rows - 1, 0), (rows - 1, cols - 1))
     flag = jnp.zeros((8, LANES), f32)
     lane, sub_lane = tile_iotas()

time: 25.9 us -> 25.9 us (level)
  no operation moved by 1% of the time
where the time goes in v8:
time: 25.9 us; the launch traced here: 25.7 us
  blocking collectives  11.5 us (44%)
  starting transfers between devices  7.07 us (27%)
  Pallas kernels  5.84 us (23%)
  between operations  0.75 us (3%)
  waiting for transfers between devices  0.5 us (2%)
    all_to_all x1, blocking collectives, local(): gathered = lax.all_to_all(pay, AXES, 0, 0)  11.5 us
    pallas_call x6, Pallas kernels, call(): pl.pallas_call(body, out_shape=out_shape, in_specs=in_specs, out_specs=ou...  5.84 us
    ppermute x1, starting transfers between devices, local(): tile_a = lax.ppermute(send_a, AXES, tile_even)  4.03 us
    ppermute x1, starting transfers between devices, local(): rows_a = lax.ppermute(ends_a, AXES, sec_even)  1.3 us
  transfers between devices with their start and end apart: 6, of which 1 were waited for; matrix products, arithmetic and copies ran while one was open for 0% of the time, Pallas kernels for 11%

profile of v8, /device:TPU:0, one launch (start us, length us, event | category | flops | bytes accessed | tf_op | source)
XLA Modules:
  0.0 25.7 jit_solution(2737066881335951001)
XLA Ops:
  0.6 1.0 %pack_first.1 = (bf16[96,128]{1,0:T(8,128)(2,1)S(1)}, bf16[96,128]{1,0:T(8,128)(2,1)S(1)}, bf16[192,128]{1,0:T(8,128)(2,1)S(1)}, bf16[192,128]{1,0:T(8,128)(2,1)S(1)}) custom-call(f32[16,32,256]{2,1,0:T(8,128)} %atmos.3, f32[8,16,128]{2,1,0:T(8,128)} %ocean.5), custom_call_target="tpu_custom_call" | custom-call | tf_op jit(solution)/shard_map/pack_first/pallas_call | solution.py:530
  1.7 0.5 %collective-permute-start.1 = (bf16[96,128]{1,0:T(8,128)(2,1)S(1)}, bf16[96,128]{1,0:T(8,128)(2,1)S(1)}, u32[]{:S(2)}, u32[]{:S(2)}) collective-permute-start(bf16[96,128]{1,0:T(8,128)(2,1)S(1)} %get-tuple-element.22), channel_id=1, source_target_pairs={{0,8},{1,2},{2,1},{3,4},{4,3},{5,6},{6,5},{7,15},{8,0},{9,10},{10,... | collective-permute-start | bytes 73736 | tf_op jit(solution)/shard_map/ppermute | solution.py:561
  2.2 4.0 %collective-permute-start = (bf16[96,128]{1,0:T(8,128)(2,1)S(1)}, bf16[96,128]{1,0:T(8,128)(2,1)S(1)}, u32[]{:S(2)}, u32[]{:S(2)}) collective-permute-start(bf16[96,128]{1,0:T(8,128)(2,1)S(1)} %get-tuple-element.20.first), channel_id=1, source_target_pairs={{0,1},{1,0},{2,3},{3,2},{4,5},{5,4},{6,7},{7,6},{8,9},{9,8},{10,11... | collective-permute-start | bytes 73736 | tf_op jit(solution)/shard_map/ppermute | solution.py:560
  6.2 0.4 %collective-permute-start.2 = (bf16[192,128]{1,0:T(8,128)(2,1)S(1)}, bf16[192,128]{1,0:T(8,128)(2,1)S(1)}, u32[]{:S(2)}, u32[]{:S(2)}) collective-permute-start(bf16[192,128]{1,0:T(8,128)(2,1)S(1)} %get-tuple-element.23), channel_id=1, source_target_pairs={{0,24},{1,25},{2,26},{3,27},{4,28},{5,29},{6,30},{7,31},{8,16},{9,... | collective-permute-start | bytes 147464 | tf_op jit(solution)/shard_map/ppermute | solution.py:562
  6.6 0.0 copy-start
  6.6 0.0 copy-start.1
  6.6 0.0 copy-start.2
  6.6 0.0 copy-start.3
  6.6 0.0 copy-start.4
  6.6 1.3 %collective-permute-start.3 = (bf16[192,128]{1,0:T(8,128)(2,1)S(1)}, bf16[192,128]{1,0:T(8,128)(2,1)S(1)}, u32[]{:S(2)}, u32[]{:S(2)}) collective-permute-start(bf16[192,128]{1,0:T(8,128)(2,1)S(1)} %get-tuple-element.24), channel_id=1, source_target_pairs={{0,8},{1,9},{2,10},{3,11},{4,12},{5,13},{6,14},{7,15},{8,0},{9,1},... | collective-permute-start | bytes 147464 | tf_op jit(solution)/shard_map/ppermute | solution.py:563
  7.9 0.9 %plan.1 = (bf16[80,384]{1,0:T(8,128)(2,1)S(1)}, f32[72,128]{1,0:T(8,128)S(1)}, bf16[256,256]{1,0:T(8,128)(2,1)S(1)}, bf16[128,256]{1,0:T(8,128)(2,1)S(1)}, bf16[...) custom-call(bf16[96,128]{1,0:T(8,128)(2,1)S(1)} %get-tuple-element.20.first, s32[8]{0:T(128)} %tile_map.1, s32[16,32]{1,0:T(8,128)} %cloudy.1), custom_call_target="tpu_custom_call" | custom-call | flops 1073741824 | tf_op jit(solution)/shard_map/plan/pallas_call | solution.py:530
  8.8 0.0 copy-start.5
  8.9 0.0 collective-permute-done.1.tile_b
  8.9 0.0 collective-permute-done.tile_a
  8.9 0.4 %collective-permute-start.4 = (bf16[48,128]{1,0:T(8,128)(2,1)S(1)}, bf16[48,128]{1,0:T(8,128)(2,1)S(1)}, u32[]{:S(2)}, u32[]{:S(2)}) collective-permute-start(bf16[48,128]{1,0:T(8,128)(2,1)S(1)} %get-tuple-element.28), channel_id=1, source_target_pairs={{0,24},{1,25},{2,26},{3,27},{4,28},{5,29},{6,30},{7,31},{8,16},{9,... | collective-permute-start | bytes 36872 | tf_op jit(solution)/shard_map/ppermute | solution.py:590
  9.3 0.5 %collective-permute-start.5 = (bf16[48,128]{1,0:T(8,128)(2,1)S(1)}, bf16[48,128]{1,0:T(8,128)(2,1)S(1)}, u32[]{:S(2)}, u32[]{:S(2)}) collective-permute-start(bf16[48,128]{1,0:T(8,128)(2,1)S(1)} %get-tuple-element.29), channel_id=1, source_target_pairs={{0,8},{1,9},{2,10},{3,11},{4,12},{5,13},{6,14},{7,15},{8,0},{9,1},... | collective-permute-start | bytes 36872 | tf_op jit(solution)/shard_map/ppermute | solution.py:591
  9.8 0.4 %collective-permute-done.2.rows_b = bf16[192,128]{1,0:T(8,128)(2,1)S(1)} collective-permute-done((bf16[192,128]{1,0:T(8,128)(2,1)S(1)}, bf16[192,128]{1,0:T(8,128)(2,1)S(1)}, u32[]{:S(2)}, u32[]{:S(2)}) %collective-permute-start.2) | collective-permute-done | bytes 49184 | tf_op jit(solution)/shard_map/ppermute | solution.py:562
  10.2 0.0 collective-permute-done.3.rows_a
  10.2 0.0 copy-done
  10.2 0.0 copy-done.1
  10.2 0.0 copy-done.2
  10.2 0.0 copy-done.3
  10.2 0.0 copy-done.4
  10.2 0.0 copy-done.5
  10.3 1.8 %main.1 = (f32[16,32,256]{2,1,0:T(8,128)S(1)}, f32[4,8,128]{2,1,0:T(8,128)S(1)}, f32[8,256]{1,0:T(8,128)S(1)}) custom-call(f32[16,32,256]{2,1,0:T(8,128)S(1)} %copy-done, f32[512,128]{1,0:T(8,128)S(1)} %get-tuple-element.21.flags.all_flags, bf16[256,1024]{1,0:T(8,128)(2,1)S(1)} %copy-done.1, bf16[1024,256]{1,0:T(8,128)(2,1)S(1)} %copy-done.2, ...), custom_call_target="tpu_custom_call" | custom-call | flops 1073741824 | tf_op jit(solution)/shard_map/main/pallas_call | solution.py:530
  12.1 0.0 collective-permute-done.4.corner_b
  12.1 0.0 collective-permute-done.5.corner_a
  12.1 0.6 %finish.1 = (f32[16,32,256]{2,1,0:T(8,128)S(1)}, f32[32,4,128]{2,1,0:T(4,128)S(1)}) custom-call(f32[16,32,256]{2,1,0:T(8,128)S(1)} %get-tuple-element.25.old, f32[512,128]{1,0:T(8,128)S(1)} %get-tuple-element.21.flags.all_flags, bf16[256,1024]{1,0:T(8,128)(2,1)S(1)} %copy-done.1, bf16[1024,256]{1,0:T(8,128)(2,1)S(1)} %copy-done.2, ...), custom_call_target="tpu_custom_call", output_to_operand_aliasing={{0}: (0, {})} | custom-call | flops 33554432 | tf_op jit(solution)/shard_map/finish/pallas_call | solution.py:530
  12.7 11.5 %all_to_all.5.gathered = f32[32,4,128]{2,1,0:T(4,128)S(1)} all-to-all(f32[32,4,128]{2,1,0:T(4,128)S(1)} %get-tuple-element.31), channel_id=1, replica_groups=mesh['sec'=4,'tile'=8] {'sec','tile'}, dimensions={0} | all-to-all | bytes 131072 | tf_op jit(solution)/shard_map/all_to_all | solution.py:613
  24.2 1.5 %final.1 = (f32[16,32,256]{2,1,0:T(8,128)}, f32[8,16,128]{2,1,0:T(8,128)}, f32[16,32]{1,0:T(8,128)}) custom-call(f32[32,4,128]{2,1,0:T(4,128)S(1)} %all_to_all.5.gathered, bf16[80,384]{1,0:T(8,128)(2,1)S(1)} %get-tuple-element.32.blend, f32[72,128]{1,0:T(8,128)S(1)} %get-tuple-element.27.last.inside, bf16[256,256]{1,0:T(8,128)(2,1)S(1)} %get-tuple-element.33.spots, ...), custom_call_target="tpu_custom_call" | custom-call | tf_op jit(solution)/shard_map/final/pallas_call | solution.py:530
  (1 shorter events, 0.0 us)
Async XLA Ops:
  1.7 7.2 %collective-permute-start.1 = (bf16[96,128]{1,0:T(8,128)(2,1)S(1)}, bf16[96,128]{1,0:T(8,128)(2,1)S(1)}, u32[]{:S(2)}, u32[]{:S(2)}) collective-permute-start(bf16[96,128]{1,0:T(8,128)(2,1)S(1)} %get-tuple-element.22), channel_id=1, source_target_pairs={{0,8},{1,2},{2,1},{3,4},{4,3},{5,6},{6,5},{7,15},{8,0},{9,10},{10,... | collective-permute-start | bytes 73736 | tf_op jit(solution)/shard_map/ppermute | solution.py:561
  2.2 6.7 %collective-permute-start = (bf16[96,128]{1,0:T(8,128)(2,1)S(1)}, bf16[96,128]{1,0:T(8,128)(2,1)S(1)}, u32[]{:S(2)}, u32[]{:S(2)}) collective-permute-start(bf16[96,128]{1,0:T(8,128)(2,1)S(1)} %get-tuple-element.20.first), channel_id=1, source_target_pairs={{0,1},{1,0},{2,3},{3,2},{4,5},{5,4},{6,7},{7,6},{8,9},{9,8},{10,11... | collective-permute-start | bytes 73736 | tf_op jit(solution)/shard_map/ppermute | solution.py:560
  6.2 4.0 %collective-permute-start.2 = (bf16[192,128]{1,0:T(8,128)(2,1)S(1)}, bf16[192,128]{1,0:T(8,128)(2,1)S(1)}, u32[]{:S(2)}, u32[]{:S(2)}) collective-permute-start(bf16[192,128]{1,0:T(8,128)(2,1)S(1)} %get-tuple-element.23), channel_id=1, source_target_pairs={{0,24},{1,25},{2,26},{3,27},{4,28},{5,29},{6,30},{7,31},{8,16},{9,... | collective-permute-start | bytes 147464 | tf_op jit(solution)/shard_map/ppermute | solution.py:562
  6.6 3.6 %copy-start = (f32[16,32,256]{2,1,0:T(8,128)S(1)}, f32[16,32,256]{2,1,0:T(8,128)}, u32[]{:S(2)}) copy-start(f32[16,32,256]{2,1,0:T(8,128)} %atmos.3) | copy-start | bytes 1572868
  6.6 3.6 %copy-start.1 = (bf16[256,1024]{1,0:T(8,128)(2,1)S(1)}, bf16[256,1024]{1,0:T(8,128)(2,1)}, u32[]{:S(2)}) copy-start(bf16[256,1024]{1,0:T(8,128)(2,1)} %w_in.3) | copy-start | bytes 1572868
  6.6 3.6 %copy-start.2 = (bf16[1024,256]{1,0:T(8,128)(2,1)S(1)}, bf16[1024,256]{1,0:T(8,128)(2,1)}, u32[]{:S(2)}) copy-start(bf16[1024,256]{1,0:T(8,128)(2,1)} %w_out.3) | copy-start | bytes 1572868
  6.6 3.6 %copy-start.3 = (bf16[256,1024]{1,0:T(8,128)(2,1)S(1)}, bf16[256,1024]{1,0:T(8,128)(2,1)}, u32[]{:S(2)}) copy-start(bf16[256,1024]{1,0:T(8,128)(2,1)} %c_in.3) | copy-start | bytes 1572868
  6.6 3.6 %copy-start.4 = (bf16[1024,256]{1,0:T(8,128)(2,1)S(1)}, bf16[1024,256]{1,0:T(8,128)(2,1)}, u32[]{:S(2)}) copy-start(bf16[1024,256]{1,0:T(8,128)(2,1)} %c_out.3) | copy-start | bytes 1572868
  6.6 3.6 %collective-permute-start.3 = (bf16[192,128]{1,0:T(8,128)(2,1)S(1)}, bf16[192,128]{1,0:T(8,128)(2,1)S(1)}, u32[]{:S(2)}, u32[]{:S(2)}) collective-permute-start(bf16[192,128]{1,0:T(8,128)(2,1)S(1)} %get-tuple-element.24), channel_id=1, source_target_pairs={{0,8},{1,9},{2,10},{3,11},{4,12},{5,13},{6,14},{7,15},{8,0},{9,1},... | collective-permute-start | bytes 147464 | tf_op jit(solution)/shard_map/ppermute | solution.py:563
  8.8 1.4 %copy-start.5 = (f32[8,16,128]{2,1,0:T(8,128)S(1)}, f32[8,16,128]{2,1,0:T(8,128)}, u32[]{:S(2)}) copy-start(f32[8,16,128]{2,1,0:T(8,128)} %ocean.5) | copy-start | bytes 196612
  8.9 3.2 %collective-permute-start.4 = (bf16[48,128]{1,0:T(8,128)(2,1)S(1)}, bf16[48,128]{1,0:T(8,128)(2,1)S(1)}, u32[]{:S(2)}, u32[]{:S(2)}) collective-permute-start(bf16[48,128]{1,0:T(8,128)(2,1)S(1)} %get-tuple-element.28), channel_id=1, source_target_pairs={{0,24},{1,25},{2,26},{3,27},{4,28},{5,29},{6,30},{7,31},{8,16},{9,... | collective-permute-start | bytes 36872 | tf_op jit(solution)/shard_map/ppermute | solution.py:590
  9.3 2.8 %collective-permute-start.5 = (bf16[48,128]{1,0:T(8,128)(2,1)S(1)}, bf16[48,128]{1,0:T(8,128)(2,1)S(1)}, u32[]{:S(2)}, u32[]{:S(2)}) collective-permute-start(bf16[48,128]{1,0:T(8,128)(2,1)S(1)} %get-tuple-element.29), channel_id=1, source_target_pairs={{0,8},{1,9},{2,10},{3,11},{4,12},{5,13},{6,14},{7,15},{8,0},{9,1},... | collective-permute-start | bytes 36872 | tf_op jit(solution)/shard_map/ppermute | solution.py:591

commit v9 on v7

--- a/solution.py
+++ b/solution.py
@@ -133,12 +133,16 @@
 def pack_corners(tiles, rows, feat, sea_rows, tile_a, tile_b, last, out_a, out_b):
     sides = Sides(tiles, rows, feat, tile_a, tile_b)
 
-    def corners(corner, sea_first):
-        sea = [sides.sea(sea_first + r) for r in range(OSTEPS)]
-        return jnp.concatenate(halves_of(sides.air(corner)) + sea, axis=0).astype(bf16)
+    sub = sublane((8, LANES))
+
+    def corners(corner, near, inward):
+        second, third = sides.sea(near + inward), sides.sea(near + 2 * inward)
+        shared = jnp.where(sub == 2, turn(third, 2), jnp.where(sub == 5, turn(third, -2), second))
+        parts = halves_of(sides.air(corner)) + [sides.sea(near), shared]
+        return jnp.concatenate(parts, axis=0).astype(bf16)
 
     even = lax.axis_index("sec") % 2 == 0
-    north, south = corners(0, 0), corners(rows - 1, sea_rows - OSTEPS)
+    north, south = corners(0, 0, 1), corners(rows - 1, sea_rows - 1, -1)
     out_a[...] = jnp.where(even, south, north)
     out_b[...] = jnp.where(even, north, south)
 
@@ -240,7 +244,7 @@
         return kind, at_s * tiles, at_t, ok
 
     present[...] = device(present.shape)[3].astype(f32)
-    shape = (blend.shape[0], blend.shape[1] // 3)
+    shape = (blend.shape[0], blend.shape[1] // 2)
     kind, base, at_t, ok = device(shape)
     above = jnp.zeros(shape, jnp.int32)
     for k in range(tiles):
@@ -249,18 +253,18 @@
     which, column = column // count, column % count
     here = jnp.where(column == base + at_t, 1.0, 0.0)
     there = jnp.where(column == base + above, 1.0, 0.0)
-    top = jnp.where(kind == 1, 0.2, jnp.where(kind == 3, 1.0, 1.4))
+    top = jnp.where((kind == 1) | (kind == 3), 1.0, 7.0)
     parts = (
-        jnp.where((kind == 0) | (kind == 2), -0.4, 0.0) * there,
-        jnp.where(kind == 1, -0.4, 0.0) * there,
+        jnp.where((kind == 0) | (kind == 2), -2.0, 0.0) * there,
+        jnp.where(kind == 1, -2.0, 0.0) * there,
         top * here,
-        jnp.where(kind == 1, 1.0, 0.0) * here,
+        jnp.where(kind == 1, 5.0, 0.0) * here,
     )
     total = jnp.zeros(shape, f32)
     for q, part in enumerate(parts):
         total = jnp.where(which == q, part, total)
-    high, low = parts_of(jnp.where(ok & (kind < 4), total, 0.0), 2)
-    blend[...] = jnp.concatenate([high, high, low], axis=1)
+    total = jnp.where(ok & (kind < 4), total, 0.0)
+    blend[...] = jnp.concatenate([total, total], axis=1).astype(bf16)
     flags_copy.wait()
     values = cloudy_here[...].astype(f32)
     for r in range(rows):
@@ -381,8 +385,11 @@
             end, k = (0, r + OSTEPS) if r < 0 else (1, r - sea_rows)
             at = ASTEPS * halves * cols + k * sea_cols
             core = cores[end][at : at + sea_cols]
-            at = 8 * (halves + k)
-            side = corners[end][at : at + 8]
+            near, shared = (corners[end][8 * (halves + q) : 8 * (halves + q) + 8] for q in range(2))
+            low = sublane(near.shape) < 4
+            third = jnp.where(low, turn(shared, -2), turn(shared, 2))
+            distance = -r if r < 0 else r - sea_rows + 1
+            side = (near, shared, third, jnp.zeros(near.shape, f32))[distance - 1]
         state.append(jnp.concatenate([core, side], axis=0))
     for depth in reversed(range(OSTEPS)):
         state = [five(*state[k : k + 3]) for k in range(len(state) - 2)]
@@ -432,12 +439,8 @@
         )
 
     everything = jnp.concatenate([gathered[:, q, :] for q in range(4)], axis=0)
-    high, low = parts_of(everything, 2)
-    blocks = jnp.dot(
-        blend[...],
-        jnp.concatenate([high, low, high], axis=0),
-        preferred_element_type=f32,
-    )
+    everything = jnp.concatenate(parts_of(everything, 2), axis=0)
+    blocks = jnp.dot(blend[...], everything, preferred_element_type=f32)
     keep = inside[...]
     blocks = {
         (k // 3, k % 3): (blocks[8 * k : 8 * k + 8], keep[8 * k : 8 * k + 8] > 0.0)
@@ -496,7 +499,7 @@
     plus = [(0, 1), (1, 0), (1, 1), (1, 2), (2, 1)]
     for wanted in [list(blocks)] * (OSTEPS - 2) + [plus, [(1, 1)]]:
         blocks = step(blocks, wanted)
-    mine = kappa_sea**OSTEPS * blocks[1, 1][0]
+    mine = kappa_sea ** (OSTEPS + 1) * blocks[1, 1][0]
     own = upright_at([mine[0:1], mine[1:2]], 0, sea_feat // 2)
     own = against(cells[...], own)
     lane_s = lax.broadcasted_iota(jnp.int32, (sea_cols, sea_feat), 1)
@@ -568,7 +571,7 @@
     *planned, flags = call(
         functools.partial(plan, secs, tiles), "plan",
         (
-            shape((80, 12 * count), bf16),
+            shape((80, 8 * count), bf16),
             shape((72, LANES), f32),
             shape((rows // 2 * cols, 2 * LANES), bf16),
             shape((LANES, 2 * LANES), bf16),
@@ -585,7 +588,7 @@
         flops=1 << 30,
         args=(send_a, hbm(tile_map), hbm(cloudy)),
     )
-    out = shape((8 * (halves + OSTEPS), LANES), bf16)
+    out = shape((8 * (halves + 2), LANES), bf16)
     send_a, send_b = call(
         functools.partial(pack_corners, tiles, rows, feat, sea_rows), "pack_corners", (out, out),
         [VMEM] * 2 + [pl.BlockSpec(memory_space=pl.ANY)], (VMEM, VMEM),

time: 25.9 us -> 25.9 us (level)
  no operation moved by 1% of the time
where the time goes in v9:
time: 25.9 us; the launch traced here: 25.7 us
  blocking collectives  11.4 us (44%)
  starting transfers between devices  7.07 us (27%)
  Pallas kernels  6 us (23%)
  between operations  0.76 us (3%)
  waiting for transfers between devices  0.44 us (2%)
    all_to_all x1, blocking collectives, local(): gathered = lax.all_to_all(pay, AXES, 0, 0)  11.4 us
    pallas_call x6, Pallas kernels, call(): pl.pallas_call(body, out_shape=out_shape, in_specs=in_specs, out_specs=ou...  6 us
    ppermute x1, starting transfers between devices, local(): tile_a = lax.ppermute(send_a, AXES, tile_even)  4.03 us
    ppermute x1, starting transfers between devices, local(): rows_a = lax.ppermute(ends_a, AXES, sec_even)  1.3 us
  transfers between devices with their start and end apart: 6, of which 1 were waited for; matrix products, arithmetic and copies ran while one was open for 0% of the time, Pallas kernels for 11%

profile of v9, /device:TPU:0, one launch (start us, length us, event | category | flops | bytes accessed | tf_op | source)
XLA Modules:
  0.0 25.7 jit_solution(4708800189497586151)
XLA Ops:
  0.6 1.0 %pack_first.1 = (bf16[96,128]{1,0:T(8,128)(2,1)S(1)}, bf16[96,128]{1,0:T(8,128)(2,1)S(1)}, bf16[192,128]{1,0:T(8,128)(2,1)S(1)}, bf16[192,128]{1,0:T(8,128)(2,1)S(1)}) custom-call(f32[16,32,256]{2,1,0:T(8,128)} %atmos.3, f32[8,16,128]{2,1,0:T(8,128)} %ocean.5), custom_call_target="tpu_custom_call" | custom-call | tf_op jit(solution)/shard_map/pack_first/pallas_call | solution.py:537
  1.7 0.5 %collective-permute-start.1 = (bf16[96,128]{1,0:T(8,128)(2,1)S(1)}, bf16[96,128]{1,0:T(8,128)(2,1)S(1)}, u32[]{:S(2)}, u32[]{:S(2)}) collective-permute-start(bf16[96,128]{1,0:T(8,128)(2,1)S(1)} %get-tuple-element.22), channel_id=1, source_target_pairs={{0,8},{1,2},{2,1},{3,4},{4,3},{5,6},{6,5},{7,15},{8,0},{9,10},{10,... | collective-permute-start | bytes 73736 | tf_op jit(solution)/shard_map/ppermute | solution.py:568
  2.2 4.0 %collective-permute-start = (bf16[96,128]{1,0:T(8,128)(2,1)S(1)}, bf16[96,128]{1,0:T(8,128)(2,1)S(1)}, u32[]{:S(2)}, u32[]{:S(2)}) collective-permute-start(bf16[96,128]{1,0:T(8,128)(2,1)S(1)} %get-tuple-element.20.first), channel_id=1, source_target_pairs={{0,1},{1,0},{2,3},{3,2},{4,5},{5,4},{6,7},{7,6},{8,9},{9,8},{10,11... | collective-permute-start | bytes 73736 | tf_op jit(solution)/shard_map/ppermute | solution.py:567
  6.2 0.4 %collective-permute-start.2 = (bf16[192,128]{1,0:T(8,128)(2,1)S(1)}, bf16[192,128]{1,0:T(8,128)(2,1)S(1)}, u32[]{:S(2)}, u32[]{:S(2)}) collective-permute-start(bf16[192,128]{1,0:T(8,128)(2,1)S(1)} %get-tuple-element.23), channel_id=1, source_target_pairs={{0,24},{1,25},{2,26},{3,27},{4,28},{5,29},{6,30},{7,31},{8,16},{9,... | collective-permute-start | bytes 147464 | tf_op jit(solution)/shard_map/ppermute | solution.py:569
  6.6 0.0 copy-start
  6.6 0.0 copy-start.1
  6.6 0.0 copy-start.2
  6.6 0.0 copy-start.3
  6.6 0.0 copy-start.4
  6.6 1.3 %collective-permute-start.3 = (bf16[192,128]{1,0:T(8,128)(2,1)S(1)}, bf16[192,128]{1,0:T(8,128)(2,1)S(1)}, u32[]{:S(2)}, u32[]{:S(2)}) collective-permute-start(bf16[192,128]{1,0:T(8,128)(2,1)S(1)} %get-tuple-element.24), channel_id=1, source_target_pairs={{0,8},{1,9},{2,10},{3,11},{4,12},{5,13},{6,14},{7,15},{8,0},{9,1},... | collective-permute-start | bytes 147464 | tf_op jit(solution)/shard_map/ppermute | solution.py:570
  7.9 1.0 %plan.1 = (bf16[80,256]{1,0:T(8,128)(2,1)S(1)}, f32[72,128]{1,0:T(8,128)S(1)}, bf16[256,256]{1,0:T(8,128)(2,1)S(1)}, bf16[128,256]{1,0:T(8,128)(2,1)S(1)}, bf16[...) custom-call(bf16[96,128]{1,0:T(8,128)(2,1)S(1)} %get-tuple-element.20.first, s32[8]{0:T(128)} %tile_map.1, s32[16,32]{1,0:T(8,128)} %cloudy.1), custom_call_target="tpu_custom_call" | custom-call | flops 1073741824 | tf_op jit(solution)/shard_map/plan/pallas_call | solution.py:537
  8.9 0.0 copy-start.5
  8.9 0.0 collective-permute-done.1.tile_b
  8.9 0.0 collective-permute-done.tile_a
  8.9 0.4 %collective-permute-start.4 = (bf16[32,128]{1,0:T(8,128)(2,1)S(1)}, bf16[32,128]{1,0:T(8,128)(2,1)S(1)}, u32[]{:S(2)}, u32[]{:S(2)}) collective-permute-start(bf16[32,128]{1,0:T(8,128)(2,1)S(1)} %get-tuple-element.28), channel_id=1, source_target_pairs={{0,24},{1,25},{2,26},{3,27},{4,28},{5,29},{6,30},{7,31},{8,16},{9,... | collective-permute-start | bytes 24584 | tf_op jit(solution)/shard_map/ppermute | solution.py:597
  9.3 0.5 %collective-permute-start.5 = (bf16[32,128]{1,0:T(8,128)(2,1)S(1)}, bf16[32,128]{1,0:T(8,128)(2,1)S(1)}, u32[]{:S(2)}, u32[]{:S(2)}) collective-permute-start(bf16[32,128]{1,0:T(8,128)(2,1)S(1)} %get-tuple-element.29), channel_id=1, source_target_pairs={{0,8},{1,9},{2,10},{3,11},{4,12},{5,13},{6,14},{7,15},{8,0},{9,1},... | collective-permute-start | bytes 24584 | tf_op jit(solution)/shard_map/ppermute | solution.py:598
  9.8 0.4 %collective-permute-done.2.rows_b = bf16[192,128]{1,0:T(8,128)(2,1)S(1)} collective-permute-done((bf16[192,128]{1,0:T(8,128)(2,1)S(1)}, bf16[192,128]{1,0:T(8,128)(2,1)S(1)}, u32[]{:S(2)}, u32[]{:S(2)}) %collective-permute-start.2) | collective-permute-done | bytes 49184 | tf_op jit(solution)/shard_map/ppermute | solution.py:569
  10.2 0.0 collective-permute-done.3.rows_a
  10.2 0.0 copy-done
  10.2 0.0 copy-done.1
  10.2 0.0 copy-done.2
  10.2 0.0 copy-done.3
  10.2 0.0 copy-done.4
  10.2 0.0 copy-done.5
  10.3 1.9 %main.1 = (f32[16,32,256]{2,1,0:T(8,128)S(1)}, f32[4,8,128]{2,1,0:T(8,128)S(1)}, f32[8,256]{1,0:T(8,128)S(1)}) custom-call(f32[16,32,256]{2,1,0:T(8,128)S(1)} %copy-done, f32[512,128]{1,0:T(8,128)S(1)} %get-tuple-element.21.flags.all_flags, bf16[256,1024]{1,0:T(8,128)(2,1)S(1)} %copy-done.1, bf16[1024,256]{1,0:T(8,128)(2,1)S(1)} %copy-done.2, ...), custom_call_target="tpu_custom_call" | custom-call | flops 1073741824 | tf_op jit(solution)/shard_map/main/pallas_call | solution.py:537
  12.2 0.0 collective-permute-done.4.corner_b
  12.2 0.0 collective-permute-done.5.corner_a
  12.2 0.6 %finish.1 = (f32[16,32,256]{2,1,0:T(8,128)S(1)}, f32[32,4,128]{2,1,0:T(4,128)S(1)}) custom-call(f32[16,32,256]{2,1,0:T(8,128)S(1)} %get-tuple-element.25.old, f32[512,128]{1,0:T(8,128)S(1)} %get-tuple-element.21.flags.all_flags, bf16[256,1024]{1,0:T(8,128)(2,1)S(1)} %copy-done.1, bf16[1024,256]{1,0:T(8,128)(2,1)S(1)} %copy-done.2, ...), custom_call_target="tpu_custom_call", output_to_operand_aliasing={{0}: (0, {})} | custom-call | flops 33554432 | tf_op jit(solution)/shard_map/finish/pallas_call | solution.py:537
  12.8 11.4 %all_to_all.5.gathered = f32[32,4,128]{2,1,0:T(4,128)S(1)} all-to-all(f32[32,4,128]{2,1,0:T(4,128)S(1)} %get-tuple-element.31), channel_id=1, replica_groups=mesh['sec'=4,'tile'=8] {'sec','tile'}, dimensions={0} | all-to-all | bytes 131072 | tf_op jit(solution)/shard_map/all_to_all | solution.py:620
  24.2 1.5 %final.1 = (f32[16,32,256]{2,1,0:T(8,128)}, f32[8,16,128]{2,1,0:T(8,128)}, f32[16,32]{1,0:T(8,128)}) custom-call(f32[32,4,128]{2,1,0:T(4,128)S(1)} %all_to_all.5.gathered, bf16[80,256]{1,0:T(8,128)(2,1)S(1)} %get-tuple-element.32.blend, f32[72,128]{1,0:T(8,128)S(1)} %get-tuple-element.27.last.inside, bf16[256,256]{1,0:T(8,128)(2,1)S(1)} %get-tuple-element.33.spots, ...), custom_call_target="tpu_custom_call" | custom-call | tf_op jit(solution)/shard_map/final/pallas_call | solution.py:537
  (1 shorter events, 0.0 us)
Async XLA Ops:
  1.7 7.2 %collective-permute-start.1 = (bf16[96,128]{1,0:T(8,128)(2,1)S(1)}, bf16[96,128]{1,0:T(8,128)(2,1)S(1)}, u32[]{:S(2)}, u32[]{:S(2)}) collective-permute-start(bf16[96,128]{1,0:T(8,128)(2,1)S(1)} %get-tuple-element.22), channel_id=1, source_target_pairs={{0,8},{1,2},{2,1},{3,4},{4,3},{5,6},{6,5},{7,15},{8,0},{9,10},{10,... | collective-permute-start | bytes 73736 | tf_op jit(solution)/shard_map/ppermute | solution.py:568
  2.2 6.7 %collective-permute-start = (bf16[96,128]{1,0:T(8,128)(2,1)S(1)}, bf16[96,128]{1,0:T(8,128)(2,1)S(1)}, u32[]{:S(2)}, u32[]{:S(2)}) collective-permute-start(bf16[96,128]{1,0:T(8,128)(2,1)S(1)} %get-tuple-element.20.first), channel_id=1, source_target_pairs={{0,1},{1,0},{2,3},{3,2},{4,5},{5,4},{6,7},{7,6},{8,9},{9,8},{10,11... | collective-permute-start | bytes 73736 | tf_op jit(solution)/shard_map/ppermute | solution.py:567
  6.2 4.0 %collective-permute-start.2 = (bf16[192,128]{1,0:T(8,128)(2,1)S(1)}, bf16[192,128]{1,0:T(8,128)(2,1)S(1)}, u32[]{:S(2)}, u32[]{:S(2)}) collective-permute-start(bf16[192,128]{1,0:T(8,128)(2,1)S(1)} %get-tuple-element.23), channel_id=1, source_target_pairs={{0,24},{1,25},{2,26},{3,27},{4,28},{5,29},{6,30},{7,31},{8,16},{9,... | collective-permute-start | bytes 147464 | tf_op jit(solution)/shard_map/ppermute | solution.py:569
  6.6 3.6 %copy-start = (f32[16,32,256]{2,1,0:T(8,128)S(1)}, f32[16,32,256]{2,1,0:T(8,128)}, u32[]{:S(2)}) copy-start(f32[16,32,256]{2,1,0:T(8,128)} %atmos.3) | copy-start | bytes 1572868
  6.6 3.6 %copy-start.1 = (bf16[256,1024]{1,0:T(8,128)(2,1)S(1)}, bf16[256,1024]{1,0:T(8,128)(2,1)}, u32[]{:S(2)}) copy-start(bf16[256,1024]{1,0:T(8,128)(2,1)} %w_in.3) | copy-start | bytes 1572868
  6.6 3.6 %copy-start.2 = (bf16[1024,256]{1,0:T(8,128)(2,1)S(1)}, bf16[1024,256]{1,0:T(8,128)(2,1)}, u32[]{:S(2)}) copy-start(bf16[1024,256]{1,0:T(8,128)(2,1)} %w_out.3) | copy-start | bytes 1572868
  6.6 3.6 %copy-start.3 = (bf16[256,1024]{1,0:T(8,128)(2,1)S(1)}, bf16[256,1024]{1,0:T(8,128)(2,1)}, u32[]{:S(2)}) copy-start(bf16[256,1024]{1,0:T(8,128)(2,1)} %c_in.3) | copy-start | bytes 1572868
  6.6 3.6 %copy-start.4 = (bf16[1024,256]{1,0:T(8,128)(2,1)S(1)}, bf16[1024,256]{1,0:T(8,128)(2,1)}, u32[]{:S(2)}) copy-start(bf16[1024,256]{1,0:T(8,128)(2,1)} %c_out.3) | copy-start | bytes 1572868
  6.6 3.6 %collective-permute-start.3 = (bf16[192,128]{1,0:T(8,128)(2,1)S(1)}, bf16[192,128]{1,0:T(8,128)(2,1)S(1)}, u32[]{:S(2)}, u32[]{:S(2)}) collective-permute-start(bf16[192,128]{1,0:T(8,128)(2,1)S(1)} %get-tuple-element.24), channel_id=1, source_target_pairs={{0,8},{1,9},{2,10},{3,11},{4,12},{5,13},{6,14},{7,15},{8,0},{9,1},... | collective-permute-start | bytes 147464 | tf_op jit(solution)/shard_map/ppermute | solution.py:570
  8.9 1.4 %copy-start.5 = (f32[8,16,128]{2,1,0:T(8,128)S(1)}, f32[8,16,128]{2,1,0:T(8,128)}, u32[]{:S(2)}) copy-start(f32[8,16,128]{2,1,0:T(8,128)} %ocean.5) | copy-start | bytes 196612
  8.9 3.3 %collective-permute-start.4 = (bf16[32,128]{1,0:T(8,128)(2,1)S(1)}, bf16[32,128]{1,0:T(8,128)(2,1)S(1)}, u32[]{:S(2)}, u32[]{:S(2)}) collective-permute-start(bf16[32,128]{1,0:T(8,128)(2,1)S(1)} %get-tuple-element.28), channel_id=1, source_target_pairs={{0,24},{1,25},{2,26},{3,27},{4,28},{5,29},{6,30},{7,31},{8,16},{9,... | collective-permute-start | bytes 24584 | tf_op jit(solution)/shard_map/ppermute | solution.py:597
  9.3 2.9 %collective-permute-start.5 = (bf16[32,128]{1,0:T(8,128)(2,1)S(1)}, bf16[32,128]{1,0:T(8,128)(2,1)S(1)}, u32[]{:S(2)}, u32[]{:S(2)}) collective-permute-start(bf16[32,128]{1,0:T(8,128)(2,1)S(1)} %get-tuple-element.29), channel_id=1, source_target_pairs={{0,8},{1,9},{2,10},{3,11},{4,12},{5,13},{6,14},{7,15},{8,0},{9,1},... | collective-permute-start | bytes 24584 | tf_op jit(solution)/shard_map/ppermute | solution.py:598

commit v10 on v9

--- a/solution.py
+++ b/solution.py
@@ -63,17 +63,17 @@
     rows, cols, feat = atmos.shape
     sea_rows, sea_cols, _ = ocean.shape
     copies = (
-        pltpu.make_async_copy(atmos.at[0:ASTEPS], ends.at[0], sems.at[3]),
-        pltpu.make_async_copy(atmos.at[rows - ASTEPS : rows], ends.at[1], sems.at[4]),
         pltpu.make_async_copy(atmos.at[:, 0:ASTEPS], west.at[:, 0:ASTEPS], sems.at[0]),
         pltpu.make_async_copy(
             atmos.at[:, cols - ASTEPS : cols], east.at[:, 8 - ASTEPS : 8], sems.at[1]
         ),
         pltpu.make_async_copy(ocean, sea, sems.at[2]),
+        pltpu.make_async_copy(atmos.at[0:ASTEPS], ends.at[0], sems.at[3]),
+        pltpu.make_async_copy(atmos.at[rows - ASTEPS : rows], ends.at[1], sems.at[4]),
     )
     for copy in copies:
         copy.start()
-    for copy in copies:
+    for copy in copies[:3]:
         copy.wait()
     to_west, to_east = [], []
     sub = sublane((8, feat))
@@ -95,6 +95,8 @@
     even = lax.axis_index("tile") % 2 == 0
     out_a[...] = jnp.where(even, to_east, to_west)
     out_b[...] = jnp.where(even, to_west, to_east)
+    for copy in copies[3:]:
+        copy.wait()
     south = 1 - lax.axis_index("sec") % 2
     for out, end in ((rows_a, south), (rows_b, 1 - south)):
         parts = []
@@ -174,20 +176,13 @@
     return jnp.concatenate([row[:own], jnp.where(ok, side, 0.0)], axis=0)
 
 
-def silu(v):
-    return v * (0.5 + 0.5 * jnp.tanh(0.5 * v))
-
-
-def physics(x, w_in, w_out, c_in, c_out, hid):
-    width = w_in.shape[1]
+def physics(x, layers, hid):
+    first, second = layers
     block = 256
-    for which, first in enumerate((w_in, c_in)):
-        for j in range(0, width, block):
-            h = jnp.dot(x, first[:, j : j + block], preferred_element_type=f32)
-            hid[which, :, j : j + block] = silu(h).astype(bf16)
-    clear = jnp.dot(hid[0], w_out[...], preferred_element_type=f32)
-    cloud = jnp.dot(hid[1], c_out[...], preferred_element_type=f32)
-    return clear, cloud
+    for j in range(0, first.shape[1], block):
+        u = jnp.dot(x, first[:, j : j + block], preferred_element_type=f32)
+        hid[:, j : j + block] = (u + u * jnp.tanh(u)).astype(bf16)
+    return lambda: jnp.dot(hid[...], second[...], preferred_element_type=f32)
 
 
 def upright(line):
@@ -213,12 +208,10 @@
 
 def plan(
     secs, tiles, first, tile_map, cloudy, blend, present, spots, cells, spread, flags,
-    place, cloudy_here, sems,
+    place, sems,
 ):
     map_copy = pltpu.make_async_copy(tile_map, place, sems.at[0])
     map_copy.start()
-    flags_copy = pltpu.make_async_copy(cloudy, cloudy_here, sems.at[1])
-    flags_copy.start()
     rows, cols = cloudy.shape
     half_cols = cols // 2
     cell = sublane(spots.shape)
@@ -265,8 +258,7 @@
         total = jnp.where(which == q, part, total)
     total = jnp.where(ok & (kind < 4), total, 0.0)
     blend[...] = jnp.concatenate([total, total], axis=1).astype(bf16)
-    flags_copy.wait()
-    values = cloudy_here[...].astype(f32)
+    values = cloudy[...].astype(f32)
     for r in range(rows):
         flag = upright(values[r : r + 1, :])
         flags[r * cols : (r + 1) * cols, :] = jnp.broadcast_to(flag, (cols, LANES))
@@ -302,12 +294,13 @@
         if len(ones) >= 3:
             two = kappa_air**ASTEPS * five(*ones[-3:])[:cols]
             field[r - 1] = two
-            xs[(r - 1) * cols : r * cols, :] = two.astype(bf16)
+            xs[(r - 1) * cols : r * cols, :] = (0.5 * two).astype(bf16)
     ends[...] = jnp.zeros(ends.shape, f32)
     for k, r in enumerate((0, rows - 1)):
         ends[2 * k : 2 * k + 1, :] = field[r, 0:1, :]
         ends[2 * k + 1 : 2 * k + 2, :] = field[r, cols - 1 : cols, :]
-    clear, cloud = physics(xs[...], w_in, w_out, c_in, c_out, hid)
+    clear = physics(xs[...], (w_in, w_out), hid.at[0])()
+    cloud = physics(xs[...], (c_in, c_out), hid.at[1])()
     means = [jnp.zeros((8, LANES), f32) for _ in range(2)]
     for r in range(rows):
         span = slice(r * cols, (r + 1) * cols)
@@ -346,8 +339,10 @@
     for k, cell in enumerate((north[7:8], north[0:1], south[7:8], south[0:1])):
         diagonal = jnp.where(sub == k, cell, diagonal)
     state = ends[...] + 2.0 * kappa_air**ASTEPS * diagonal
-    x = jnp.concatenate([state, jnp.zeros((8, feat), f32)], axis=0).astype(bf16)
-    clear, cloud = physics(x, w_in, w_out, c_in, c_out, hid)
+    x = (0.5 * jnp.concatenate([state, jnp.zeros((8, feat), f32)], axis=0)).astype(bf16)
+    clear = physics(x, (w_in, w_out), hid.at[0])
+    cloud = physics(x, (c_in, c_out), hid.at[1])
+    clear, cloud = clear(), cloud()
     places = ((0, 0), (0, cols - 1), (rows - 1, 0), (rows - 1, cols - 1))
     flag = jnp.zeros((8, LANES), f32)
     lane, sub_lane = tile_iotas()
@@ -493,7 +488,7 @@
             west = side((i, j), first_c, 1, 1 - sea_cols)((i, j - 1))
             east = side((i, j), last_c, -1, sea_cols - 1)((i, j + 1))
             v = v + (up + down) + (west + east)
-            new[i, j] = jnp.where(ok, v, 0.0), ok
+            new[i, j] = (v if (i, j) == (1, 1) else jnp.where(ok, v, 0.0)), ok
         return new
 
     plus = [(0, 1), (1, 0), (1, 1), (1, 2), (2, 1)]
@@ -578,15 +573,14 @@
             shape((2 * LANES, cols), bf16),
             shape((rows * cols, LANES), f32),
         ),
-        [pl.BlockSpec(memory_space=pl.ANY), HBM, HBM],
+        [pl.BlockSpec(memory_space=pl.ANY), HBM, VMEM],
         (VMEM,) * 6,
         [
             pltpu.SMEM(tile_map.shape, jnp.int32),
-            pltpu.VMEM(cloudy.shape, jnp.int32),
-            pltpu.SemaphoreType.DMA((2,)),
+            pltpu.SemaphoreType.DMA((1,)),
         ],
         flops=1 << 30,
-        args=(send_a, hbm(tile_map), hbm(cloudy)),
+        args=(send_a, hbm(tile_map), cloudy),
     )
     out = shape((8 * (halves + 2), LANES), bf16)
     send_a, send_b = call(

time: 25.9 us -> 25.9 us (level)
  Pallas kernels: 6 us -> 5.73 us
    pallas_call x6, Pallas kernels: 6 us -> 5.73 us  [call(): pl.pallas_call(body, out_shape=out_shape, in_specs=in_specs, out_specs=ou...]
  transfers between devices with their start and end apart: 6 -> 6, of which waited for: 1 -> 1; matrix products, arithmetic and copies ran while one was open for 0% -> 0% of each run, Pallas kernels for 11% -> 10%
where the time goes in v10:
time: 25.9 us; the launch traced here: 25.7 us
  blocking collectives  11.5 us (44%)
  starting transfers between devices  7.09 us (27%)
  Pallas kernels  5.73 us (22%)
  between operations  0.77 us (3%)
  waiting for transfers between devices  0.51 us (2%)
    all_to_all x1, blocking collectives, local(): gathered = lax.all_to_all(pay, AXES, 0, 0)  11.5 us
    pallas_call x6, Pallas kernels, call(): pl.pallas_call(body, out_shape=out_shape, in_specs=in_specs, out_specs=ou...  5.73 us
    ppermute x1, starting transfers between devices, local(): tile_a = lax.ppermute(send_a, AXES, tile_even)  4.03 us
    ppermute x1, starting transfers between devices, local(): rows_a = lax.ppermute(ends_a, AXES, sec_even)  1.3 us
  transfers between devices with their start and end apart: 6, of which 1 were waited for; matrix products, arithmetic and copies ran while one was open for 0% of the time, Pallas kernels for 10%

profile of v10, /device:TPU:0, one launch (start us, length us, event | category | flops | bytes accessed | tf_op | source)
XLA Modules:
  0.0 25.7 jit_solution(8617388156712754621)
XLA Ops:
  0.6 0.0 copy-start.6
  0.6 1.0 %pack_first.1 = (bf16[96,128]{1,0:T(8,128)(2,1)S(1)}, bf16[96,128]{1,0:T(8,128)(2,1)S(1)}, bf16[192,128]{1,0:T(8,128)(2,1)S(1)}, bf16[192,128]{1,0:T(8,128)(2,1)S(1)}) custom-call(f32[16,32,256]{2,1,0:T(8,128)} %atmos.3, f32[8,16,128]{2,1,0:T(8,128)} %ocean.5), custom_call_target="tpu_custom_call" | custom-call | tf_op jit(solution)/shard_map/pack_first/pallas_call | solution.py:532
  1.7 0.5 %collective-permute-start.1 = (bf16[96,128]{1,0:T(8,128)(2,1)S(1)}, bf16[96,128]{1,0:T(8,128)(2,1)S(1)}, u32[]{:S(2)}, u32[]{:S(2)}) collective-permute-start(bf16[96,128]{1,0:T(8,128)(2,1)S(1)} %get-tuple-element.22), channel_id=1, source_target_pairs={{0,8},{1,2},{2,1},{3,4},{4,3},{5,6},{6,5},{7,15},{8,0},{9,10},{10,... | collective-permute-start | bytes 73736 | tf_op jit(solution)/shard_map/ppermute | solution.py:563
  2.2 4.0 %collective-permute-start = (bf16[96,128]{1,0:T(8,128)(2,1)S(1)}, bf16[96,128]{1,0:T(8,128)(2,1)S(1)}, u32[]{:S(2)}, u32[]{:S(2)}) collective-permute-start(bf16[96,128]{1,0:T(8,128)(2,1)S(1)} %get-tuple-element.20.first), channel_id=1, source_target_pairs={{0,1},{1,0},{2,3},{3,2},{4,5},{5,4},{6,7},{7,6},{8,9},{9,8},{10,11... | collective-permute-start | bytes 73736 | tf_op jit(solution)/shard_map/ppermute | solution.py:562
  6.2 0.4 %collective-permute-start.2 = (bf16[192,128]{1,0:T(8,128)(2,1)S(1)}, bf16[192,128]{1,0:T(8,128)(2,1)S(1)}, u32[]{:S(2)}, u32[]{:S(2)}) collective-permute-start(bf16[192,128]{1,0:T(8,128)(2,1)S(1)} %get-tuple-element.23), channel_id=1, source_target_pairs={{0,24},{1,25},{2,26},{3,27},{4,28},{5,29},{6,30},{7,31},{8,16},{9,... | collective-permute-start | bytes 147464 | tf_op jit(solution)/shard_map/ppermute | solution.py:564
  6.6 0.0 copy-start
  6.6 0.0 copy-start.1
  6.6 0.0 copy-start.2
  6.6 0.0 copy-start.3
  6.6 0.0 copy-start.4
  6.6 1.3 %collective-permute-start.3 = (bf16[192,128]{1,0:T(8,128)(2,1)S(1)}, bf16[192,128]{1,0:T(8,128)(2,1)S(1)}, u32[]{:S(2)}, u32[]{:S(2)}) collective-permute-start(bf16[192,128]{1,0:T(8,128)(2,1)S(1)} %get-tuple-element.24), channel_id=1, source_target_pairs={{0,8},{1,9},{2,10},{3,11},{4,12},{5,13},{6,14},{7,15},{8,0},{9,1},... | collective-permute-start | bytes 147464 | tf_op jit(solution)/shard_map/ppermute | solution.py:565
  7.9 0.0 copy-done.6
  7.9 0.9 %plan.1 = (bf16[80,256]{1,0:T(8,128)(2,1)S(1)}, f32[72,128]{1,0:T(8,128)S(1)}, bf16[256,256]{1,0:T(8,128)(2,1)S(1)}, bf16[128,256]{1,0:T(8,128)(2,1)S(1)}, bf16[...) custom-call(bf16[96,128]{1,0:T(8,128)(2,1)S(1)} %get-tuple-element.20.first, s32[8]{0:T(128)} %tile_map.1, ...), custom_call_target="tpu_custom_call" | custom-call | flops 1073741824 | tf_op jit(solution)/shard_map/plan/pallas_call | solution.py:532
  8.8 0.0 copy-start.5
  8.8 0.0 collective-permute-done.1.tile_b
  8.8 0.0 collective-permute-done.tile_a
  8.8 0.4 %collective-permute-start.4 = (bf16[32,128]{1,0:T(8,128)(2,1)S(1)}, bf16[32,128]{1,0:T(8,128)(2,1)S(1)}, u32[]{:S(2)}, u32[]{:S(2)}) collective-permute-start(bf16[32,128]{1,0:T(8,128)(2,1)S(1)} %get-tuple-element.28), channel_id=1, source_target_pairs={{0,24},{1,25},{2,26},{3,27},{4,28},{5,29},{6,30},{7,31},{8,16},{9,... | collective-permute-start | bytes 24584 | tf_op jit(solution)/shard_map/ppermute | solution.py:591
  9.2 0.5 %collective-permute-start.5 = (bf16[32,128]{1,0:T(8,128)(2,1)S(1)}, bf16[32,128]{1,0:T(8,128)(2,1)S(1)}, u32[]{:S(2)}, u32[]{:S(2)}) collective-permute-start(bf16[32,128]{1,0:T(8,128)(2,1)S(1)} %get-tuple-element.29), channel_id=1, source_target_pairs={{0,8},{1,9},{2,10},{3,11},{4,12},{5,13},{6,14},{7,15},{8,0},{9,1},... | collective-permute-start | bytes 24584 | tf_op jit(solution)/shard_map/ppermute | solution.py:592
  9.7 0.5 %collective-permute-done.2.rows_b = bf16[192,128]{1,0:T(8,128)(2,1)S(1)} collective-permute-done((bf16[192,128]{1,0:T(8,128)(2,1)S(1)}, bf16[192,128]{1,0:T(8,128)(2,1)S(1)}, u32[]{:S(2)}, u32[]{:S(2)}) %collective-permute-start.2) | collective-permute-done | bytes 49184 | tf_op jit(solution)/shard_map/ppermute | solution.py:564
  10.2 0.0 collective-permute-done.3.rows_a
  10.2 0.0 copy-done
  10.2 0.0 copy-done.1
  10.2 0.0 copy-done.2
  10.2 0.0 copy-done.3
  10.2 0.0 copy-done.4
  10.2 0.0 copy-done.5
  10.3 1.8 %main.1 = (f32[16,32,256]{2,1,0:T(8,128)S(1)}, f32[4,8,128]{2,1,0:T(8,128)S(1)}, f32[8,256]{1,0:T(8,128)S(1)}) custom-call(f32[16,32,256]{2,1,0:T(8,128)S(1)} %copy-done, f32[512,128]{1,0:T(8,128)S(1)} %get-tuple-element.21.flags.all_flags, bf16[256,1024]{1,0:T(8,128)(2,1)S(1)} %copy-done.1, bf16[1024,256]{1,0:T(8,128)(2,1)S(1)} %copy-done.2, ...), custom_call_target="tpu_custom_call" | custom-call | flops 1073741824 | tf_op jit(solution)/shard_map/main/pallas_call | solution.py:532
  12.0 0.0 collective-permute-done.4.corner_b
  12.1 0.0 collective-permute-done.5.corner_a
  12.1 0.6 %finish.1 = (f32[16,32,256]{2,1,0:T(8,128)S(1)}, f32[32,4,128]{2,1,0:T(4,128)S(1)}) custom-call(f32[16,32,256]{2,1,0:T(8,128)S(1)} %get-tuple-element.25.old, f32[512,128]{1,0:T(8,128)S(1)} %get-tuple-element.21.flags.all_flags, bf16[256,1024]{1,0:T(8,128)(2,1)S(1)} %copy-done.1, bf16[1024,256]{1,0:T(8,128)(2,1)S(1)} %copy-done.2, ...), custom_call_target="tpu_custom_call", output_to_operand_aliasing={{0}: (0, {})} | custom-call | flops 33554432 | tf_op jit(solution)/shard_map/finish/pallas_call | solution.py:532
  12.6 11.5 %all_to_all.5.gathered = f32[32,4,128]{2,1,0:T(4,128)S(1)} all-to-all(f32[32,4,128]{2,1,0:T(4,128)S(1)} %get-tuple-element.31), channel_id=1, replica_groups=mesh['sec'=4,'tile'=8] {'sec','tile'}, dimensions={0} | all-to-all | bytes 131072 | tf_op jit(solution)/shard_map/all_to_all | solution.py:614
  24.2 1.5 %final.1 = (f32[16,32,256]{2,1,0:T(8,128)}, f32[8,16,128]{2,1,0:T(8,128)}, f32[16,32]{1,0:T(8,128)}) custom-call(f32[32,4,128]{2,1,0:T(4,128)S(1)} %all_to_all.5.gathered, bf16[80,256]{1,0:T(8,128)(2,1)S(1)} %get-tuple-element.32.blend, f32[72,128]{1,0:T(8,128)S(1)} %get-tuple-element.27.last.inside, bf16[256,256]{1,0:T(8,128)(2,1)S(1)} %get-tuple-element.33.spots, ...), custom_call_target="tpu_custom_call" | custom-call | tf_op jit(solution)/shard_map/final/pallas_call | solution.py:532
  (1 shorter events, 0.0 us)
Async XLA Ops:
  0.6 7.3 %copy-start.6 = (s32[16,32]{1,0:T(8,128)S(1)}, s32[16,32]{1,0:T(8,128)}, u32[]{:S(2)}) copy-start(s32[16,32]{1,0:T(8,128)} %cloudy.1) | copy-start | bytes 6148
  1.7 7.1 %collective-permute-start.1 = (bf16[96,128]{1,0:T(8,128)(2,1)S(1)}, bf16[96,128]{1,0:T(8,128)(2,1)S(1)}, u32[]{:S(2)}, u32[]{:S(2)}) collective-permute-start(bf16[96,128]{1,0:T(8,128)(2,1)S(1)} %get-tuple-element.22), channel_id=1, source_target_pairs={{0,8},{1,2},{2,1},{3,4},{4,3},{5,6},{6,5},{7,15},{8,0},{9,10},{10,... | collective-permute-start | bytes 73736 | tf_op jit(solution)/shard_map/ppermute | solution.py:563
  2.2 6.6 %collective-permute-start = (bf16[96,128]{1,0:T(8,128)(2,1)S(1)}, bf16[96,128]{1,0:T(8,128)(2,1)S(1)}, u32[]{:S(2)}, u32[]{:S(2)}) collective-permute-start(bf16[96,128]{1,0:T(8,128)(2,1)S(1)} %get-tuple-element.20.first), channel_id=1, source_target_pairs={{0,1},{1,0},{2,3},{3,2},{4,5},{5,4},{6,7},{7,6},{8,9},{9,8},{10,11... | collective-permute-start | bytes 73736 | tf_op jit(solution)/shard_map/ppermute | solution.py:562
  6.2 4.0 %collective-permute-start.2 = (bf16[192,128]{1,0:T(8,128)(2,1)S(1)}, bf16[192,128]{1,0:T(8,128)(2,1)S(1)}, u32[]{:S(2)}, u32[]{:S(2)}) collective-permute-start(bf16[192,128]{1,0:T(8,128)(2,1)S(1)} %get-tuple-element.23), channel_id=1, source_target_pairs={{0,24},{1,25},{2,26},{3,27},{4,28},{5,29},{6,30},{7,31},{8,16},{9,... | collective-permute-start | bytes 147464 | tf_op jit(solution)/shard_map/ppermute | solution.py:564
  6.6 3.6 %copy-start = (f32[16,32,256]{2,1,0:T(8,128)S(1)}, f32[16,32,256]{2,1,0:T(8,128)}, u32[]{:S(2)}) copy-start(f32[16,32,256]{2,1,0:T(8,128)} %atmos.3) | copy-start | bytes 1572868
  6.6 3.6 %copy-start.1 = (bf16[256,1024]{1,0:T(8,128)(2,1)S(1)}, bf16[256,1024]{1,0:T(8,128)(2,1)}, u32[]{:S(2)}) copy-start(bf16[256,1024]{1,0:T(8,128)(2,1)} %w_in.3) | copy-start | bytes 1572868
  6.6 3.6 %copy-start.2 = (bf16[1024,256]{1,0:T(8,128)(2,1)S(1)}, bf16[1024,256]{1,0:T(8,128)(2,1)}, u32[]{:S(2)}) copy-start(bf16[1024,256]{1,0:T(8,128)(2,1)} %w_out.3) | copy-start | bytes 1572868
  6.6 3.6 %copy-start.3 = (bf16[256,1024]{1,0:T(8,128)(2,1)S(1)}, bf16[256,1024]{1,0:T(8,128)(2,1)}, u32[]{:S(2)}) copy-start(bf16[256,1024]{1,0:T(8,128)(2,1)} %c_in.3) | copy-start | bytes 1572868
  6.6 3.6 %copy-start.4 = (bf16[1024,256]{1,0:T(8,128)(2,1)S(1)}, bf16[1024,256]{1,0:T(8,128)(2,1)}, u32[]{:S(2)}) copy-start(bf16[1024,256]{1,0:T(8,128)(2,1)} %c_out.3) | copy-start | bytes 1572868
  6.6 3.6 %collective-permute-start.3 = (bf16[192,128]{1,0:T(8,128)(2,1)S(1)}, bf16[192,128]{1,0:T(8,128)(2,1)S(1)}, u32[]{:S(2)}, u32[]{:S(2)}) collective-permute-start(bf16[192,128]{1,0:T(8,128)(2,1)S(1)} %get-tuple-element.24), channel_id=1, source_target_pairs={{0,8},{1,9},{2,10},{3,11},{4,12},{5,13},{6,14},{7,15},{8,0},{9,1},... | collective-permute-start | bytes 147464 | tf_op jit(solution)/shard_map/ppermute | solution.py:565
  8.8 1.5 %copy-start.5 = (f32[8,16,128]{2,1,0:T(8,128)S(1)}, f32[8,16,128]{2,1,0:T(8,128)}, u32[]{:S(2)}) copy-start(f32[8,16,128]{2,1,0:T(8,128)} %ocean.5) | copy-start | bytes 196612
  8.8 3.2 %collective-permute-start.4 = (bf16[32,128]{1,0:T(8,128)(2,1)S(1)}, bf16[32,128]{1,0:T(8,128)(2,1)S(1)}, u32[]{:S(2)}, u32[]{:S(2)}) collective-permute-start(bf16[32,128]{1,0:T(8,128)(2,1)S(1)} %get-tuple-element.28), channel_id=1, source_target_pairs={{0,24},{1,25},{2,26},{3,27},{4,28},{5,29},{6,30},{7,31},{8,16},{9,... | collective-permute-start | bytes 24584 | tf_op jit(solution)/shard_map/ppermute | solution.py:591
  9.2 2.9 %collective-permute-start.5 = (bf16[32,128]{1,0:T(8,128)(2,1)S(1)}, bf16[32,128]{1,0:T(8,128)(2,1)S(1)}, u32[]{:S(2)}, u32[]{:S(2)}) collective-permute-start(bf16[32,128]{1,0:T(8,128)(2,1)S(1)} %get-tuple-element.29), channel_id=1, source_target_pairs={{0,8},{1,9},{2,10},{3,11},{4,12},{5,13},{6,14},{7,15},{8,0},{9,1},... | collective-permute-start | bytes 24584 | tf_op jit(solution)/shard_map/ppermute | solution.py:592

commit v11 on v10

--- a/solution.py
+++ b/solution.py
@@ -178,7 +178,7 @@
 
 def physics(x, layers, hid):
     first, second = layers
-    block = 256
+    block = 512
     for j in range(0, first.shape[1], block):
         u = jnp.dot(x, first[:, j : j + block], preferred_element_type=f32)
         hid[:, j : j + block] = (u + u * jnp.tanh(u)).astype(bf16)

time: 25.9 us -> 25.9 us (level)
  no operation moved by 1% of the time
where the time goes in v11:
time: 25.9 us; the launch traced here: 25.7 us
  blocking collectives  11.5 us (44%)
  starting transfers between devices  7.09 us (27%)
  Pallas kernels  5.73 us (22%)
  between operations  0.77 us (3%)
  waiting for transfers between devices  0.51 us (2%)
    all_to_all x1, blocking collectives, local(): gathered = lax.all_to_all(pay, AXES, 0, 0)  11.5 us
    pallas_call x6, Pallas kernels, call(): pl.pallas_call(body, out_shape=out_shape, in_specs=in_specs, out_specs=ou...  5.73 us
    ppermute x1, starting transfers between devices, local(): tile_a = lax.ppermute(send_a, AXES, tile_even)  4.03 us
    ppermute x1, starting transfers between devices, local(): rows_a = lax.ppermute(ends_a, AXES, sec_even)  1.3 us
  transfers between devices with their start and end apart: 6, of which 1 were waited for; matrix products, arithmetic and copies ran while one was open for 0% of the time, Pallas kernels for 10%

profile of v11, /device:TPU:0, one launch (start us, length us, event | category | flops | bytes accessed | tf_op | source)
XLA Modules:
  0.0 25.7 jit_solution(8617388156712754621)
XLA Ops:
  0.6 0.0 copy-start.6
  0.6 1.0 %pack_first.1 = (bf16[96,128]{1,0:T(8,128)(2,1)S(1)}, bf16[96,128]{1,0:T(8,128)(2,1)S(1)}, bf16[192,128]{1,0:T(8,128)(2,1)S(1)}, bf16[192,128]{1,0:T(8,128)(2,1)S(1)}) custom-call(f32[16,32,256]{2,1,0:T(8,128)} %atmos.3, f32[8,16,128]{2,1,0:T(8,128)} %ocean.5), custom_call_target="tpu_custom_call" | custom-call | tf_op jit(solution)/shard_map/pack_first/pallas_call | solution.py:532
  1.7 0.5 %collective-permute-start.1 = (bf16[96,128]{1,0:T(8,128)(2,1)S(1)}, bf16[96,128]{1,0:T(8,128)(2,1)S(1)}, u32[]{:S(2)}, u32[]{:S(2)}) collective-permute-start(bf16[96,128]{1,0:T(8,128)(2,1)S(1)} %get-tuple-element.22), channel_id=1, source_target_pairs={{0,8},{1,2},{2,1},{3,4},{4,3},{5,6},{6,5},{7,15},{8,0},{9,10},{10,... | collective-permute-start | bytes 73736 | tf_op jit(solution)/shard_map/ppermute | solution.py:563
  2.2 4.0 %collective-permute-start = (bf16[96,128]{1,0:T(8,128)(2,1)S(1)}, bf16[96,128]{1,0:T(8,128)(2,1)S(1)}, u32[]{:S(2)}, u32[]{:S(2)}) collective-permute-start(bf16[96,128]{1,0:T(8,128)(2,1)S(1)} %get-tuple-element.20.first), channel_id=1, source_target_pairs={{0,1},{1,0},{2,3},{3,2},{4,5},{5,4},{6,7},{7,6},{8,9},{9,8},{10,11... | collective-permute-start | bytes 73736 | tf_op jit(solution)/shard_map/ppermute | solution.py:562
  6.2 0.4 %collective-permute-start.2 = (bf16[192,128]{1,0:T(8,128)(2,1)S(1)}, bf16[192,128]{1,0:T(8,128)(2,1)S(1)}, u32[]{:S(2)}, u32[]{:S(2)}) collective-permute-start(bf16[192,128]{1,0:T(8,128)(2,1)S(1)} %get-tuple-element.23), channel_id=1, source_target_pairs={{0,24},{1,25},{2,26},{3,27},{4,28},{5,29},{6,30},{7,31},{8,16},{9,... | collective-permute-start | bytes 147464 | tf_op jit(solution)/shard_map/ppermute | solution.py:564
  6.6 0.0 copy-start
  6.6 0.0 copy-start.1
  6.6 0.0 copy-start.2
  6.6 0.0 copy-start.3
  6.6 0.0 copy-start.4
  6.6 1.3 %collective-permute-start.3 = (bf16[192,128]{1,0:T(8,128)(2,1)S(1)}, bf16[192,128]{1,0:T(8,128)(2,1)S(1)}, u32[]{:S(2)}, u32[]{:S(2)}) collective-permute-start(bf16[192,128]{1,0:T(8,128)(2,1)S(1)} %get-tuple-element.24), channel_id=1, source_target_pairs={{0,8},{1,9},{2,10},{3,11},{4,12},{5,13},{6,14},{7,15},{8,0},{9,1},... | collective-permute-start | bytes 147464 | tf_op jit(solution)/shard_map/ppermute | solution.py:565
  7.9 0.0 copy-done.6
  7.9 0.9 %plan.1 = (bf16[80,256]{1,0:T(8,128)(2,1)S(1)}, f32[72,128]{1,0:T(8,128)S(1)}, bf16[256,256]{1,0:T(8,128)(2,1)S(1)}, bf16[128,256]{1,0:T(8,128)(2,1)S(1)}, bf16[...) custom-call(bf16[96,128]{1,0:T(8,128)(2,1)S(1)} %get-tuple-element.20.first, s32[8]{0:T(128)} %tile_map.1, ...), custom_call_target="tpu_custom_call" | custom-call | flops 1073741824 | tf_op jit(solution)/shard_map/plan/pallas_call | solution.py:532
  8.8 0.0 copy-start.5
  8.8 0.0 collective-permute-done.1.tile_b
  8.8 0.0 collective-permute-done.tile_a
  8.8 0.4 %collective-permute-start.4 = (bf16[32,128]{1,0:T(8,128)(2,1)S(1)}, bf16[32,128]{1,0:T(8,128)(2,1)S(1)}, u32[]{:S(2)}, u32[]{:S(2)}) collective-permute-start(bf16[32,128]{1,0:T(8,128)(2,1)S(1)} %get-tuple-element.28), channel_id=1, source_target_pairs={{0,24},{1,25},{2,26},{3,27},{4,28},{5,29},{6,30},{7,31},{8,16},{9,... | collective-permute-start | bytes 24584 | tf_op jit(solution)/shard_map/ppermute | solution.py:591
  9.2 0.5 %collective-permute-start.5 = (bf16[32,128]{1,0:T(8,128)(2,1)S(1)}, bf16[32,128]{1,0:T(8,128)(2,1)S(1)}, u32[]{:S(2)}, u32[]{:S(2)}) collective-permute-start(bf16[32,128]{1,0:T(8,128)(2,1)S(1)} %get-tuple-element.29), channel_id=1, source_target_pairs={{0,8},{1,9},{2,10},{3,11},{4,12},{5,13},{6,14},{7,15},{8,0},{9,1},... | collective-permute-start | bytes 24584 | tf_op jit(solution)/shard_map/ppermute | solution.py:592
  9.7 0.5 %collective-permute-done.2.rows_b = bf16[192,128]{1,0:T(8,128)(2,1)S(1)} collective-permute-done((bf16[192,128]{1,0:T(8,128)(2,1)S(1)}, bf16[192,128]{1,0:T(8,128)(2,1)S(1)}, u32[]{:S(2)}, u32[]{:S(2)}) %collective-permute-start.2) | collective-permute-done | bytes 49184 | tf_op jit(solution)/shard_map/ppermute | solution.py:564
  10.2 0.0 collective-permute-done.3.rows_a
  10.2 0.0 copy-done
  10.2 0.0 copy-done.1
  10.2 0.0 copy-done.2
  10.2 0.0 copy-done.3
  10.2 0.0 copy-done.4
  10.2 0.0 copy-done.5
  10.3 1.8 %main.1 = (f32[16,32,256]{2,1,0:T(8,128)S(1)}, f32[4,8,128]{2,1,0:T(8,128)S(1)}, f32[8,256]{1,0:T(8,128)S(1)}) custom-call(f32[16,32,256]{2,1,0:T(8,128)S(1)} %copy-done, f32[512,128]{1,0:T(8,128)S(1)} %get-tuple-element.21.flags.all_flags, bf16[256,1024]{1,0:T(8,128)(2,1)S(1)} %copy-done.1, bf16[1024,256]{1,0:T(8,128)(2,1)S(1)} %copy-done.2, ...), custom_call_target="tpu_custom_call" | custom-call | flops 1073741824 | tf_op jit(solution)/shard_map/main/pallas_call | solution.py:532
  12.0 0.0 collective-permute-done.4.corner_b
  12.1 0.0 collective-permute-done.5.corner_a
  12.1 0.6 %finish.1 = (f32[16,32,256]{2,1,0:T(8,128)S(1)}, f32[32,4,128]{2,1,0:T(4,128)S(1)}) custom-call(f32[16,32,256]{2,1,0:T(8,128)S(1)} %get-tuple-element.25.old, f32[512,128]{1,0:T(8,128)S(1)} %get-tuple-element.21.flags.all_flags, bf16[256,1024]{1,0:T(8,128)(2,1)S(1)} %copy-done.1, bf16[1024,256]{1,0:T(8,128)(2,1)S(1)} %copy-done.2, ...), custom_call_target="tpu_custom_call", output_to_operand_aliasing={{0}: (0, {})} | custom-call | flops 33554432 | tf_op jit(solution)/shard_map/finish/pallas_call | solution.py:532
  12.6 11.5 %all_to_all.5.gathered = f32[32,4,128]{2,1,0:T(4,128)S(1)} all-to-all(f32[32,4,128]{2,1,0:T(4,128)S(1)} %get-tuple-element.31), channel_id=1, replica_groups=mesh['sec'=4,'tile'=8] {'sec','tile'}, dimensions={0} | all-to-all | bytes 131072 | tf_op jit(solution)/shard_map/all_to_all | solution.py:614
  24.2 1.5 %final.1 = (f32[16,32,256]{2,1,0:T(8,128)}, f32[8,16,128]{2,1,0:T(8,128)}, f32[16,32]{1,0:T(8,128)}) custom-call(f32[32,4,128]{2,1,0:T(4,128)S(1)} %all_to_all.5.gathered, bf16[80,256]{1,0:T(8,128)(2,1)S(1)} %get-tuple-element.32.blend, f32[72,128]{1,0:T(8,128)S(1)} %get-tuple-element.27.last.inside, bf16[256,256]{1,0:T(8,128)(2,1)S(1)} %get-tuple-element.33.spots, ...), custom_call_target="tpu_custom_call" | custom-call | tf_op jit(solution)/shard_map/final/pallas_call | solution.py:532
  (1 shorter events, 0.0 us)
Async XLA Ops:
  0.6 7.3 %copy-start.6 = (s32[16,32]{1,0:T(8,128)S(1)}, s32[16,32]{1,0:T(8,128)}, u32[]{:S(2)}) copy-start(s32[16,32]{1,0:T(8,128)} %cloudy.1) | copy-start | bytes 6148
  1.7 7.1 %collective-permute-start.1 = (bf16[96,128]{1,0:T(8,128)(2,1)S(1)}, bf16[96,128]{1,0:T(8,128)(2,1)S(1)}, u32[]{:S(2)}, u32[]{:S(2)}) collective-permute-start(bf16[96,128]{1,0:T(8,128)(2,1)S(1)} %get-tuple-element.22), channel_id=1, source_target_pairs={{0,8},{1,2},{2,1},{3,4},{4,3},{5,6},{6,5},{7,15},{8,0},{9,10},{10,... | collective-permute-start | bytes 73736 | tf_op jit(solution)/shard_map/ppermute | solution.py:563
  2.2 6.6 %collective-permute-start = (bf16[96,128]{1,0:T(8,128)(2,1)S(1)}, bf16[96,128]{1,0:T(8,128)(2,1)S(1)}, u32[]{:S(2)}, u32[]{:S(2)}) collective-permute-start(bf16[96,128]{1,0:T(8,128)(2,1)S(1)} %get-tuple-element.20.first), channel_id=1, source_target_pairs={{0,1},{1,0},{2,3},{3,2},{4,5},{5,4},{6,7},{7,6},{8,9},{9,8},{10,11... | collective-permute-start | bytes 73736 | tf_op jit(solution)/shard_map/ppermute | solution.py:562
  6.2 4.0 %collective-permute-start.2 = (bf16[192,128]{1,0:T(8,128)(2,1)S(1)}, bf16[192,128]{1,0:T(8,128)(2,1)S(1)}, u32[]{:S(2)}, u32[]{:S(2)}) collective-permute-start(bf16[192,128]{1,0:T(8,128)(2,1)S(1)} %get-tuple-element.23), channel_id=1, source_target_pairs={{0,24},{1,25},{2,26},{3,27},{4,28},{5,29},{6,30},{7,31},{8,16},{9,... | collective-permute-start | bytes 147464 | tf_op jit(solution)/shard_map/ppermute | solution.py:564
  6.6 3.6 %copy-start = (f32[16,32,256]{2,1,0:T(8,128)S(1)}, f32[16,32,256]{2,1,0:T(8,128)}, u32[]{:S(2)}) copy-start(f32[16,32,256]{2,1,0:T(8,128)} %atmos.3) | copy-start | bytes 1572868
  6.6 3.6 %copy-start.1 = (bf16[256,1024]{1,0:T(8,128)(2,1)S(1)}, bf16[256,1024]{1,0:T(8,128)(2,1)}, u32[]{:S(2)}) copy-start(bf16[256,1024]{1,0:T(8,128)(2,1)} %w_in.3) | copy-start | bytes 1572868
  6.6 3.6 %copy-start.2 = (bf16[1024,256]{1,0:T(8,128)(2,1)S(1)}, bf16[1024,256]{1,0:T(8,128)(2,1)}, u32[]{:S(2)}) copy-start(bf16[1024,256]{1,0:T(8,128)(2,1)} %w_out.3) | copy-start | bytes 1572868
  6.6 3.6 %copy-start.3 = (bf16[256,1024]{1,0:T(8,128)(2,1)S(1)}, bf16[256,1024]{1,0:T(8,128)(2,1)}, u32[]{:S(2)}) copy-start(bf16[256,1024]{1,0:T(8,128)(2,1)} %c_in.3) | copy-start | bytes 1572868
  6.6 3.6 %copy-start.4 = (bf16[1024,256]{1,0:T(8,128)(2,1)S(1)}, bf16[1024,256]{1,0:T(8,128)(2,1)}, u32[]{:S(2)}) copy-start(bf16[1024,256]{1,0:T(8,128)(2,1)} %c_out.3) | copy-start | bytes 1572868
  6.6 3.6 %collective-permute-start.3 = (bf16[192,128]{1,0:T(8,128)(2,1)S(1)}, bf16[192,128]{1,0:T(8,128)(2,1)S(1)}, u32[]{:S(2)}, u32[]{:S(2)}) collective-permute-start(bf16[192,128]{1,0:T(8,128)(2,1)S(1)} %get-tuple-element.24), channel_id=1, source_target_pairs={{0,8},{1,9},{2,10},{3,11},{4,12},{5,13},{6,14},{7,15},{8,0},{9,1},... | collective-permute-start | bytes 147464 | tf_op jit(solution)/shard_map/ppermute | solution.py:565
  8.8 1.5 %copy-start.5 = (f32[8,16,128]{2,1,0:T(8,128)S(1)}, f32[8,16,128]{2,1,0:T(8,128)}, u32[]{:S(2)}) copy-start(f32[8,16,128]{2,1,0:T(8,128)} %ocean.5) | copy-start | bytes 196612
  8.8 3.2 %collective-permute-start.4 = (bf16[32,128]{1,0:T(8,128)(2,1)S(1)}, bf16[32,128]{1,0:T(8,128)(2,1)S(1)}, u32[]{:S(2)}, u32[]{:S(2)}) collective-permute-start(bf16[32,128]{1,0:T(8,128)(2,1)S(1)} %get-tuple-element.28), channel_id=1, source_target_pairs={{0,24},{1,25},{2,26},{3,27},{4,28},{5,29},{6,30},{7,31},{8,16},{9,... | collective-permute-start | bytes 24584 | tf_op jit(solution)/shard_map/ppermute | solution.py:591
  9.2 2.9 %collective-permute-start.5 = (bf16[32,128]{1,0:T(8,128)(2,1)S(1)}, bf16[32,128]{1,0:T(8,128)(2,1)S(1)}, u32[]{:S(2)}, u32[]{:S(2)}) collective-permute-start(bf16[32,128]{1,0:T(8,128)(2,1)S(1)} %get-tuple-element.29), channel_id=1, source_target_pairs={{0,8},{1,9},{2,10},{3,11},{4,12},{5,13},{6,14},{7,15},{8,0},{9,1},... | collective-permute-start | bytes 24584 | tf_op jit(solution)/shard_map/ppermute | solution.py:592
